TPU v7x, 128 devices: a whole 4x4x4 slice. The times are simulated.
128 devices in a mesh: seq: 16 (over y_hi, z, core), res: 8 (over x, y_lo).
Axes of the slice: x: 4, y: 4 (y_hi: 2, y_lo: 2; y = y_hi * 2 + y_lo), z: 4, core: 2. Of those that a mesh axis runs over, the one named last changes fastest.
Arguments:
- alignment_features: bfloat16 [64, 1024, 256], P('seq', 'res'), may hold values from -6 to 40
- alignment_standardize_gain: float32 [256], replicated, may hold values from 0.75 to 1.25
- stacked_qkvg_matrix: bfloat16 [256, 1024], replicated, may hold values from -1.65 to 1.65
- sigmoid_shift_vector: float32 [256], replicated, may hold values from -4 to 4
- final_linear_matrix: bfloat16 [256, 256], replicated, may hold values from -0.375 to 0.375
- pairwise_features: bfloat16 [1024, 1024, 128], P('seq', 'res'), may hold values from -6 to 6
- pairwise_standardize_gain: float32 [128], replicated, may hold values from 0.5 to 1.5
- pairterm_linear_matrix: bfloat16 [128, 8], replicated, may hold values from -0.5 to 0.5
- upstream_derivative: bfloat16 [64, 1024, 256], P('seq', 'res'), may hold values from -6 to 6
Outputs:
- alignment_increment: bfloat16 [64, 1024, 256], P('seq', 'res')
- derivative_of_alignment: bfloat16 [64, 1024, 256], P('seq', 'res')
- derivative_of_pairwise: bfloat16 [1024, 1024, 128], P('seq', 'res')
- derivative_of_stacked_matrix: float32 [256, 1024], replicated
- derivative_of_final_matrix: float32 [256, 256], replicated
- derivative_of_pairterm_matrix: float32 [128, 8], replicated
All inputs are finite; a program needn't handle non-finite values.
Results may differ from a plain program's by a relative error of at most 0.022.
Values may be sent and summed in bfloat16 or wider, within the bound.
No kernel may reach another device: no remote copies, remote signals or barrier semaphores. Data moves between devices by JAX's collectives and lax.ppermute only.
A program may use at most 128 MiB of HBM per device.

v0:
```python
import jax
import jax.numpy as jnp
from jax import lax
from jax.sharding import PartitionSpec as P

NORM_EPSILON = 1e-05


def standardize_apply(content_vectors, norm_gain):
    content_vectors = content_vectors.astype(jnp.float32)
    average = jnp.mean(content_vectors, axis=-1, keepdims=True)
    centered = content_vectors - average
    inv_std = lax.rsqrt(jnp.mean(centered * centered, axis=-1, keepdims=True) + NORM_EPSILON)
    norm_hat = centered * inv_std
    return (norm_hat, inv_std, (norm_hat * norm_gain).astype(jnp.bfloat16))


def standardize_derivative(norm_hat, inv_std, norm_gain, grad_out):
    d_hat = grad_out * norm_gain
    mean_d = jnp.mean(d_hat, axis=-1, keepdims=True)
    mean_dx = jnp.mean(d_hat * norm_hat, axis=-1, keepdims=True)
    return inv_std * (d_hat - mean_d - norm_hat * mean_dx)


def score_block(q_one, k_one, bias_part):
    scores = jnp.einsum("ihd,jhd->hij", q_one, k_one, preferred_element_type=jnp.float32)
    return scores + bias_part.astype(jnp.float32)


def local(
    alignment_features,
    alignment_standardize_gain,
    stacked_qkvg_matrix,
    sigmoid_shift_vector,
    final_linear_matrix,
    pairwise_features,
    pairwise_standardize_gain,
    pairterm_linear_matrix,
    upstream_derivative,
):
    shard_alignments, shard_aminos, feature_width = alignment_features.shape
    head_count = pairterm_linear_matrix.shape[1]
    inner_width = final_linear_matrix.shape[0]
    head_dim = inner_width // head_count
    head_scale = head_dim ** (-0.5)
    alignment_centered_unitless, alignment_reciprocal_spread, alignment_after_standardize = (
        standardize_apply(alignment_features, alignment_standardize_gain)
    )
    linear_mapped_lines = jnp.einsum(
        "esc,cw->esw",
        alignment_after_standardize,
        stacked_qkvg_matrix,
        preferred_element_type=jnp.float32,
    )
    queries = (linear_mapped_lines[..., :inner_width] * head_scale).astype(jnp.bfloat16)
    key_vals = linear_mapped_lines[..., inner_width : 3 * inner_width].astype(jnp.bfloat16)
    gate_vals = jax.nn.sigmoid(linear_mapped_lines[..., 3 * inner_width :] + sigmoid_shift_vector)
    pair_hat, pair_inv, pair_normed = standardize_apply(
        pairwise_features, pairwise_standardize_gain
    )
    bias_tile = jnp.einsum(
        "jic,ch->hji", pair_normed, pairterm_linear_matrix, preferred_element_type=jnp.float32
    ).astype(jnp.bfloat16)
    bias_keys = lax.all_gather(bias_tile, "seq", axis=1, tiled=True)
    bias_t = jnp.swapaxes(bias_keys, 1, 2)
    all_kv = lax.all_gather(key_vals, "res", axis=1, tiled=True)
    total_res = all_kv.shape[1]
    q_heads = queries.reshape(shard_alignments, shard_aminos, head_count, head_dim)
    kv_heads = all_kv.reshape(shard_alignments, total_res, 2, head_count, head_dim)

    def forward_one(inputs):
        q_one, kv_one = inputs
        scores = score_block(q_one, kv_one[:, 0], bias_t)
        row_max = jnp.max(scores, axis=-1, keepdims=True)
        exp_scores = jnp.exp(scores - row_max)
        row_sum = jnp.sum(exp_scores, axis=-1, keepdims=True)
        prob_low = (exp_scores / row_sum).astype(jnp.bfloat16)
        attended = jnp.einsum(
            "hij,jhd->ihd", prob_low, kv_one[:, 1], preferred_element_type=jnp.float32
        )
        return (attended, row_max, row_sum)

    attended, row_maxes, row_sums = lax.map(forward_one, (q_heads, kv_heads))
    attended = attended.reshape(shard_alignments, shard_aminos, inner_width)
    gated_out = (gate_vals * attended).astype(jnp.bfloat16)
    alignment_increment = jnp.einsum(
        "srk,kc->src", gated_out, final_linear_matrix, preferred_element_type=jnp.float32
    ).astype(jnp.bfloat16)
    d_w_out_part = jnp.einsum(
        "srk,src->kc", gated_out, upstream_derivative, preferred_element_type=jnp.float32
    )
    d_gated = jnp.einsum(
        "src,kc->srk", upstream_derivative, final_linear_matrix, preferred_element_type=jnp.float32
    )
    d_att = (d_gated * gate_vals).astype(jnp.bfloat16)
    d_gate_pre = d_gated * attended * gate_vals * (1.0 - gate_vals)
    datt_heads = d_att.reshape(shard_alignments, shard_aminos, head_count, head_dim)

    def probs_and_grads(q_one, kv_one, datt_one, row_max, row_sum, bias_part):
        scores = score_block(q_one, kv_one[:, 0], bias_part)
        prob_full = jnp.exp(scores - row_max) / row_sum
        d_probs = jnp.einsum(
            "ihd,jhd->hij", datt_one, kv_one[:, 1], preferred_element_type=jnp.float32
        )
        return (prob_full, d_probs)

    def key_terms_of(prob_full, d_scores, q_one, datt_one):
        d_key = jnp.einsum("hij,ihd->jhd", d_scores, q_one, preferred_element_type=jnp.float32)
        d_value = jnp.einsum(
            "hij,ihd->jhd",
            prob_full.astype(jnp.bfloat16),
            datt_one,
            preferred_element_type=jnp.float32,
        )
        key_rows = d_key.shape[0]
        return jnp.concatenate(
            (d_key.reshape(key_rows, inner_width), d_value.reshape(key_rows, inner_width)), axis=-1
        )

    def query_core(inputs):
        q_one, kv_one, datt_one, row_max, row_sum = inputs
        prob_full, d_probs = probs_and_grads(q_one, kv_one, datt_one, row_max, row_sum, bias_t)
        row_dot = jnp.sum(prob_full * d_probs, axis=-1, keepdims=True)
        d_scores = (prob_full * (d_probs - row_dot)).astype(jnp.bfloat16)
        d_query = (
            jnp.einsum("hij,jhd->ihd", d_scores, kv_one[:, 0], preferred_element_type=jnp.float32)
            * head_scale
        )
        return (prob_full, row_dot, d_scores, d_query)

    scan_inputs = (q_heads, kv_heads, datt_heads, row_maxes, row_sums)
    zero_bias = jnp.zeros((head_count, total_res, shard_aminos), jnp.float32)

    def query_whole(running, inputs):
        prob_full, row_dot, d_scores, d_query = query_core(inputs)
        key_terms = key_terms_of(prob_full, d_scores, inputs[0], inputs[2])
        running = running + jnp.swapaxes(d_scores, 1, 2).astype(jnp.float32)
        return (running, (d_query, key_terms))

    d_bias, (d_queries, key_terms) = lax.scan(query_whole, zero_bias, scan_inputs)
    key_grads = lax.psum_scatter(
        key_terms.astype(jnp.bfloat16), "res", scatter_dimension=1, tiled=True
    ).astype(jnp.float32)
    d_queries = d_queries.reshape(shard_alignments, shard_aminos, inner_width)
    derivative_of_mapped = jnp.concatenate((d_queries, key_grads, d_gate_pre), axis=-1).astype(
        jnp.bfloat16
    )
    d_w_qkvg_part = jnp.einsum(
        "kde,kdh->eh",
        alignment_after_standardize,
        derivative_of_mapped,
        preferred_element_type=jnp.float32,
    )
    derivative_of_standardized_alignment = jnp.einsum(
        "njr,kr->njk", derivative_of_mapped, stacked_qkvg_matrix, preferred_element_type=jnp.float32
    )
    derivative_of_alignment = standardize_derivative(
        alignment_centered_unitless,
        alignment_reciprocal_spread,
        alignment_standardize_gain,
        derivative_of_standardized_alignment,
    ).astype(jnp.bfloat16)
    bias_grad = lax.psum_scatter(
        d_bias.astype(jnp.bfloat16), "seq", scatter_dimension=1, tiled=True
    ).astype(jnp.float32)
    d_pair_normed = jnp.einsum(
        "hji,ch->jic",
        bias_grad,
        pairterm_linear_matrix.astype(jnp.float32),
        precision=lax.Precision.HIGHEST,
    )
    derivative_of_pairwise = standardize_derivative(
        pair_hat, pair_inv, pairwise_standardize_gain, d_pair_normed
    ).astype(jnp.bfloat16)
    d_w_bias_part = jnp.einsum(
        "jic,hji->ch", pair_normed.astype(jnp.float32), bias_grad, precision=lax.Precision.HIGHEST
    )
    derivative_of_stacked_matrix, derivative_of_final_matrix, derivative_of_pairterm_matrix = (
        lax.psum((d_w_qkvg_part, d_w_out_part, d_w_bias_part), ("seq", "res"))
    )
    return (
        alignment_increment,
        derivative_of_alignment,
        derivative_of_pairwise,
        derivative_of_stacked_matrix,
        derivative_of_final_matrix,
        derivative_of_pairterm_matrix,
    )


def solution(mesh):
    return jax.shard_map(
        local,
        mesh=mesh,
        in_specs=(
            P("seq", "res", None),
            P(),
            P(),
            P(),
            P(),
            P("seq", "res", None),
            P(),
            P(),
            P("seq", "res", None),
        ),
        out_specs=(
            P("seq", "res", None),
            P("seq", "res", None),
            P("seq", "res", None),
            P(),
            P(),
            P(),
        ),
        check_vma=False,
    )
```

profile of v0, /device:TPU:1, one launch (start us, length us, event | category | flops | bytes accessed | tf_op | source)
XLA Modules:
  0.0 624.2 jit_solution(17188192520851521474)
XLA Ops:
  7.2 3.3 copy.52
  16.5 48.2 %all-gather.5.cloned.1.call-done = bf16[8,1024,128]{2,0,1:T(8,128)(2,1)} async-done(((bf16[8,64,128]{2,0,1:T(8,128)(2,1)}), bf16[8,1024,128]{2,0,1:T(8,128)(2,1)}) %all-gather.5.cloned.1.call-update) | async-done | bytes 2097168 | tf_op jit(solution)/shard_map/all_gather | solution.py:64
  64.7 4.1 copy.54
  68.8 85.6 %all-gather.3.cloned.1.call-done = bf16[4,1024,512]{2,1,0:T(8,128)(2,1)} async-done(((bf16[4,128,512]{2,1,0:T(8,128)(2,1)}), bf16[4,1024,512]{2,1,0:T(8,128)(2,1)}) %all-gather.3.cloned.1.call-update) | async-done | bytes 4194320 | tf_op jit(solution)/shard_map/all_gather | solution.py:66
  154.4 6.3 %copy.50 = bf16[4,1024,512]{1,2,0:T(8,128)(2,1)} copy(bf16[4,1024,512]{2,1,0:T(8,128)(2,1)} %all-gather.3.cloned.1.call-done) | data formatting | bytes 8388608 | tf_op jit(solution)/shard_map/all_gather | solution.py:66
  160.7 26.2 %while.31 = (s32[]{:T(128)}, f32[4,128,8,32]{1,3,2,0:T(8,128)}, f32[4,8,128,1]{2,1,3,0:T(8,128)S(1)}, f32[4,8,128,1]{2,1,3,0:T(8,128)S(1)}, bf16[4,1024,2,8,32]{...) while((s32[]{:T(128)}, f32[4,128,8,32]{1,3,2,0:T(8,128)}, ...), condition=%wide.region_7.8_spmd.clone, body=%wide.region_4.7_spmd.sunk.clone | while | flops 142604288 | bytes 18059864 | solution.py:83
  192.5 94.0 %while.32 = (s32[]{:T(128)}, f32[8,1024,128]{1,2,0:T(8,128)}, bf16[4,128,8,32]{1,3,2,0:T(8,128)(2,1)}, bf16[4,1024,512]{2,1,0:T(8,128)(2,1)}, bf16[4,128,8,32]{1...) while((s32[]{:T(128)}, f32[8,1024,128]{1,2,0:T(8,128)}, ...), condition=%wide.region_10.11_spmd.clone.clone, body=%wide.region_8.10_spmd.clone.sunk.clone | while | flops 351304704 | bytes 91129048 | solution.py:140
  194.6 5.2 multiply_reduce_fusion.4
  199.9 6.3 %bitcast_add_fusion.3 = (f32[8,1024,128]{1,2,0:T(8,128)}, bf16[8,128,1024]{2,1,0:T(8,128)(2,1)S(1)}) fusion(f32[8,1024,128]{1,2,0:T(8,128)} %get-tuple-element.471, pred[]{:T(512)S(6)} %compare.4, f32[8,128,1024]{2,1,0:T(8,128)} %get-tuple-element.423, f32[8,128,1024]{2,1,0:T(8,128)} %copy-done.1, f32[8,128]{1,0:T(8,128)S(1)} %get-tuple-element.424), kind=kLoop, calls=%fused_computation.15.clone.1.clone | loop fusion | flops 6291456 | bytes 18878464 | tf_op jit(solution)/shard_map/while/body/eval_jaxpr/add | solution.py:137
  217.3 5.2 multiply_reduce_fusion.4
  222.5 7.5 %bitcast_add_fusion.3 = (f32[8,1024,128]{1,2,0:T(8,128)}, bf16[8,128,1024]{2,1,0:T(8,128)(2,1)S(1)}) fusion(f32[8,1024,128]{1,2,0:T(8,128)} %get-tuple-element.471, pred[]{:T(512)S(6)} %compare.4, f32[8,128,1024]{2,1,0:T(8,128)} %get-tuple-element.423, f32[8,128,1024]{2,1,0:T(8,128)} %copy-done.1, f32[8,128]{1,0:T(8,128)S(1)} %get-tuple-element.424), kind=kLoop, calls=%fused_computation.15.clone.1.clone | loop fusion | flops 6291456 | bytes 18878464 | tf_op jit(solution)/shard_map/while/body/eval_jaxpr/add | solution.py:137
  241.1 5.2 multiply_reduce_fusion.4
  246.3 7.5 %bitcast_add_fusion.3 = (f32[8,1024,128]{1,2,0:T(8,128)}, bf16[8,128,1024]{2,1,0:T(8,128)(2,1)S(1)}) fusion(f32[8,1024,128]{1,2,0:T(8,128)} %get-tuple-element.471, pred[]{:T(512)S(6)} %compare.4, f32[8,128,1024]{2,1,0:T(8,128)} %get-tuple-element.423, f32[8,128,1024]{2,1,0:T(8,128)} %copy-done.1, f32[8,128]{1,0:T(8,128)S(1)} %get-tuple-element.424), kind=kLoop, calls=%fused_computation.15.clone.1.clone | loop fusion | flops 6291456 | bytes 18878464 | tf_op jit(solution)/shard_map/while/body/eval_jaxpr/add | solution.py:137
  260.2 2.5 fusion.114
  264.9 5.2 multiply_reduce_fusion.4
  270.1 7.5 %bitcast_add_fusion.3 = (f32[8,1024,128]{1,2,0:T(8,128)}, bf16[8,128,1024]{2,1,0:T(8,128)(2,1)S(1)}) fusion(f32[8,1024,128]{1,2,0:T(8,128)} %get-tuple-element.471, pred[]{:T(512)S(6)} %compare.4, f32[8,128,1024]{2,1,0:T(8,128)} %get-tuple-element.423, f32[8,128,1024]{2,1,0:T(8,128)} %copy-done.1, f32[8,128]{1,0:T(8,128)S(1)} %get-tuple-element.424), kind=kLoop, calls=%fused_computation.15.clone.1.clone | loop fusion | flops 6291456 | bytes 18878464 | tf_op jit(solution)/shard_map/while/body/eval_jaxpr/add | solution.py:137
  286.5 4.9 copy.61
  297.0 66.4 %reduce-scatter.5.cloned.1.call-done = bf16[8,64,128]{2,0,1:T(8,128)(2,1)} async-done(((bf16[8,1024,128]{2,0,1:T(8,128)(2,1)}), bf16[8,64,128]{2,0,1:T(8,128)(2,1)}) %reduce-scatter.5.cloned.1.call-update) | async-done | bytes 131088 | tf_op jit(solution)/shard_map/reduce_scatter | solution.py:163
  365.7 2.8 fusion.34
  368.5 4.1 copy.65
  373.4 80.1 %psum.23 = f32[128,8]{0,1:T(8,128)} all-reduce(f32[128,8]{0,1:T(8,128)S(1)} %convolution_bitcast_fusion.2), channel_id=1, replica_groups=mesh['seq'=16,'res'=8] {'seq','res'}, use_global_device_ids=true, to_apply=%region_19.20 | all-reduce | flops 1024 | bytes 8192 | tf_op jit(solution)/shard_map/psum | solution.py:179
  453.5 4.5 reduce-scatter.3.cloned.1.call-done
  458.1 2.8 convolution_bitcast_fusion
  462.5 151.2 %all-reduce.3.cloned.1.call-done = (f32[256,1024]{1,0:T(8,128)}, f32[256,256]{1,0:T(8,128)}) async-done(((f32[256,1024]{1,0:T(8,128)}, f32[256,256]{1,0:T(8,128)}), (f32[256,1024]{1,0:T(8,128)}, f32[256,256]{1,0:T(8,128)})) %all-reduce.3.cloned.1.call-update) | async-done | bytes 1310736 | tf_op jit(solution)/shard_map/psum | solution.py:179
  (152 shorter events, 93.4 us)
Async XLA Ops:
  7.2 6.7 %copy-start = (bf16[256,1024]{1,0:T(8,128)(2,1)S(1)}, bf16[256,1024]{1,0:T(8,128)(2,1)}, u32[]{:S(2)}) copy-start(bf16[256,1024]{1,0:T(8,128)(2,1)} %param.15) | copy-start | bytes 1572868
  7.2 4.7 copy-start.12
  7.2 57.5 %all-gather.5.cloned.1.call-start = ((), (), s32[]{:S(2)}) async-start(), calls=%async_computation.3 | async-start | bytes 2228224 | tf_op jit(solution)/shard_map/all_gather | solution.py:64
  13.3 141.1 %all-gather.3.cloned.1.call-start = ((), (), s32[]{:S(2)}) async-start(), calls=%async_computation.2 | async-start | bytes 4718592 | tf_op jit(solution)/shard_map/all_gather | solution.py:66
  15.2 348.2 %reduce-scatter.5.cloned.1.call-start = ((), (), s32[]{:S(2)}) async-start(), calls=%async_computation.5 | async-start | bytes 2228224 | tf_op jit(solution)/shard_map/reduce_scatter | solution.py:163
  160.7 28.3 %copy-start.10 = (bf16[256,256]{1,0:T(8,128)(2,1)S(1)}, bf16[256,256]{1,0:T(8,128)(2,1)}, u32[]{:S(2)}) copy-start(bf16[256,256]{1,0:T(8,128)(2,1)} %param.17) | copy-start | bytes 393220
  160.7 28.3 %copy-start.16 = (f32[256]{0:T(256)S(1)}, f32[256]{0:T(256)}, u32[]{:S(2)}) copy-start(f32[256]{0:T(256)} %param.16) | copy-start | bytes 3076
  193.8 6.0 copy-start.3
  194.6 5.2 copy-start.1
  199.9 6.7 %copy-start.2 = (f32[8,128,1024]{2,1,0:T(8,128)S(1)}, f32[8,128,1024]{2,1,0:T(8,128)}, u32[]{:S(2)}) copy-start(f32[8,128,1024]{2,1,0:T(8,128)} %get-tuple-element.423) | copy-start | bytes 12582916 | tf_op jit(solution)/shard_map/while
  216.5 6.0 copy-start.3
  217.3 5.3 copy-start.1
  222.5 7.9 %copy-start.2 = (f32[8,128,1024]{2,1,0:T(8,128)S(1)}, f32[8,128,1024]{2,1,0:T(8,128)}, u32[]{:S(2)}) copy-start(f32[8,128,1024]{2,1,0:T(8,128)} %get-tuple-element.423) | copy-start | bytes 12582916 | tf_op jit(solution)/shard_map/while
  240.3 6.0 copy-start.3
  241.0 5.3 copy-start.1
  246.3 7.9 %copy-start.2 = (f32[8,128,1024]{2,1,0:T(8,128)S(1)}, f32[8,128,1024]{2,1,0:T(8,128)}, u32[]{:S(2)}) copy-start(f32[8,128,1024]{2,1,0:T(8,128)} %get-tuple-element.423) | copy-start | bytes 12582916 | tf_op jit(solution)/shard_map/while
  264.1 6.0 copy-start.3
  264.8 5.3 copy-start.1
  270.1 7.9 %copy-start.2 = (f32[8,128,1024]{2,1,0:T(8,128)S(1)}, f32[8,128,1024]{2,1,0:T(8,128)}, u32[]{:S(2)}) copy-start(f32[8,128,1024]{2,1,0:T(8,128)} %get-tuple-element.423) | copy-start | bytes 12582916 | tf_op jit(solution)/shard_map/while
  291.4 72.0 %copy-start.5 = (bf16[64,128,128]{1,2,0:T(8,128)(2,1)S(1)}, bf16[64,128,128]{1,2,0:T(8,128)(2,1)}, u32[]{:S(2)}) copy-start(bf16[64,128,128]{1,2,0:T(8,128)(2,1)} %copy-done.4) | copy-start | bytes 6291460
  291.5 166.6 %reduce-scatter.3.cloned.1.call-start = ((), (), s32[]{:S(2)}) async-start(), calls=%async_computation.4 | async-start | bytes 4718592 | tf_op jit(solution)/shard_map/reduce_scatter | solution.py:141
  292.0 321.7 %all-reduce.3.cloned.1.call-start = ((), (), s32[]{:S(2)}) async-start(), calls=%async_computation.6 | async-start | bytes 2621440 | tf_op jit(solution)/shard_map/psum | solution.py:179
  368.5 89.5 %copy-start.9 = (bf16[4,128,256]{2,1,0:T(8,128)(2,1)S(1)}, bf16[4,128,256]{2,1,0:T(8,128)(2,1)}, u32[]{:S(2)}) copy-start(bf16[4,128,256]{2,1,0:T(8,128)(2,1)} %copy.60) | copy-start | bytes 786436
  373.4 87.5 %copy-start.17 = (bf16[4,128,256]{2,1,0:T(8,128)(2,1)S(1)}, bf16[4,128,256]{2,1,0:T(8,128)(2,1)}, u32[]{:S(2)}) copy-start(bf16[4,128,256]{2,1,0:T(8,128)(2,1)} %get-tuple-element.258) | copy-start | bytes 786436
  (8 other events, 22.8 us)
Sparse Core Ops, SparseCore 0:
  13.5 51.2 all-gather.4
  66.4 87.9 all-gather.2
  291.6 71.7 reduce-scatter.4
  365.8 92.2 reduce-scatter.2
  464.2 149.4 all-reduce.2
where the time goes:
time: 626 us; the launch traced here: 624 us
  waiting for transfers between devices  356 us (57%)
  blocking collectives  80.1 us (13%)
  matrix products  67.8 us (11%)
  local copies, waits for them, and re-layouts  60.9 us (10%)
  other arithmetic  43.8 us (7%)
  between operations  14 us (2%)
    psum x1, waiting for transfers between devices, local(): lax.psum((d_w_qkvg_part, d_w_out_part, d_w_bias_part), ('seq', 'res'))  151 us
    all_gather x1, waiting for transfers between devices, local(): all_kv = lax.all_gather(key_vals, 'res', axis=1, tiled=True)  85.6 us
    psum x1, blocking collectives, local(): lax.psum((d_w_qkvg_part, d_w_out_part, d_w_bias_part), ('seq', 'res'))  80.1 us
    reduce_scatter x1, waiting for transfers between devices, local(): lax.psum_scatter(d_bias.astype(jnp.bfloat16), 'seq', scatter_dimension=1,...  66.4 us
    all_gather x1, waiting for transfers between devices, local(): bias_keys = lax.all_gather(bias_tile, 'seq', axis=1, tiled=True)  48.2 us
    dot_general x8, matrix products, score_block(): jnp.einsum('ihd,jhd->hij', q_one, k_one, preferred_element_type=jnp.float32)  30.6 us
    add x4, other arithmetic, query_whole(): running = running + jnp.swapaxes(d_scores, 1, 2).astype(jnp.float32)  28.7 us
    dynamic_update_slice x8, local copies, waits for them, and re-layouts, local(): lax.scan(query_whole, zero_bias, scan_inputs)  18.4 us
  transfers between devices with their start and end apart: 5, of which 5 were waited for; matrix products, arithmetic and copies ran while one was open for 4% of the time, Pallas kernels for 0%

commit v1 on v0

v1 whole, which is shorter than its diff:
```python
import functools

import jax
import jax.numpy as jnp
from jax import lax
from jax.experimental import pallas as pl
from jax.experimental.pallas import tpu as pltpu
from jax.sharding import PartitionSpec as P

EPS = 1e-05
F32 = jnp.float32
BF16 = jnp.bfloat16
HEADS = 8
DH = 32
SCALE = DH ** (-0.5)
VMEM = 48 * 1024 * 1024


def nn(a, b):
    return lax.dot_general(a, b, (((1,), (0,)), ((), ())), preferred_element_type=F32)


def nt(a, b):
    return lax.dot_general(a, b, (((1,), (1,)), ((), ())), preferred_element_type=F32)


def tn(a, b):
    return lax.dot_general(a, b, (((0,), (0,)), ((), ())), preferred_element_type=F32)


def normalize(x):
    x = x.astype(F32)
    centered = x - jnp.mean(x, axis=-1, keepdims=True)
    inv = lax.rsqrt(jnp.mean(centered * centered, axis=-1, keepdims=True) + EPS)
    return centered * inv, inv


def normalize_grad(hat, inv, gain, grad):
    g = grad * gain
    mean_g = jnp.mean(g, axis=-1, keepdims=True)
    mean_gx = jnp.mean(g * hat, axis=-1, keepdims=True)
    return inv * (g - mean_g - hat * mean_gx)


def params(n=1):
    return pltpu.CompilerParams(
        dimension_semantics=("arbitrary",) * n, vmem_limit_bytes=VMEM
    )


def project_kernel(x_ref, gain_ref, w_ref, shift_ref, wo_ref, up_ref, pack_ref, gate_ref, dg_ref):
    hat, _ = normalize(x_ref[0])
    normed = (hat * gain_ref[...]).astype(BF16)
    proj = nn(normed, w_ref[...])
    q = (proj[:, :256] * SCALE).astype(BF16)
    k = proj[:, 256:512].astype(BF16)
    v = proj[:, 512:768].astype(BF16)
    gate = jax.nn.sigmoid(proj[:, 768:] + shift_ref[...])
    d_gated = nt(up_ref[0], wo_ref[...])
    da = (d_gated * gate).astype(BF16)
    gate_ref[0] = gate
    dg_ref[0] = d_gated
    for h in range(HEADS):
        c = slice(h * DH, (h + 1) * DH)
        pack_ref[h, 0] = jnp.concatenate([q[:, c], k[:, c], v[:, c], da[:, c]], axis=1)


def project(x, gain, w, shift, wo, up):
    s, n, c = x.shape
    whole = lambda *shape: pl.BlockSpec(shape, lambda i: (0,) * len(shape))
    row = pl.BlockSpec((1, n, c), lambda i: (i, 0, 0))
    return pl.pallas_call(
        project_kernel,
        grid=(s,),
        in_specs=[row, whole(1, c), whole(c, 4 * c), whole(1, c), whole(c, c), row],
        out_specs=[pl.BlockSpec((HEADS, 1, n, 128), lambda i: (0, i, 0, 0)), row, row],
        out_shape=[
            jax.ShapeDtypeStruct((HEADS, s, n, 128), BF16),
            jax.ShapeDtypeStruct((s, n, c), F32),
            jax.ShapeDtypeStruct((s, n, c), F32),
        ],
        compiler_params=params(),
        name="project",
    )(x, gain, w, shift, wo, up)


def bias_kernel(x_ref, gain_ref, wt_ref, out_ref, tmp):
    wt = wt_ref[...]
    for j in range(x_ref.shape[0]):
        hat, _ = normalize(x_ref[j])
        normed = (hat * gain_ref[...]).astype(BF16)
        tmp[:, j, :] = nt(wt, normed)
    out_ref[...] = tmp[...].astype(BF16)


def pair_bias(pair, gain, wt):
    j, i, c = pair.shape
    step = 16
    return pl.pallas_call(
        bias_kernel,
        grid=(j // step,),
        in_specs=[
            pl.BlockSpec((step, i, c), lambda g: (g, 0, 0)),
            pl.BlockSpec((1, c), lambda g: (0, 0)),
            pl.BlockSpec((HEADS, c), lambda g: (0, 0)),
        ],
        out_specs=pl.BlockSpec((HEADS, step, i), lambda g: (0, g, 0)),
        out_shape=jax.ShapeDtypeStruct((HEADS, j, i), BF16),
        scratch_shapes=[pltpu.VMEM((HEADS, step, i), F32)],
        compiler_params=params(),
        name="pair_bias",
    )(pair, gain, wt)


def attention_kernel(x_ref, b_ref, o_ref, db_ref, xt, acc, scores, exps, dsc, rq, ra, delta):
    step = pl.program_id(0)
    n_seq = x_ref.shape[1]
    iw = 256
    zeros = lambda rows: jnp.zeros((rows, iw), BF16)

    @pl.when(step == 0)
    def _():
        for s in range(n_seq):
            for r in range(8):
                xt[s, :, r * 128 : (r + 1) * 128] = x_ref[r, s].T
        acc[...] = jnp.zeros_like(acc)

    cols = pl.ds(pl.multiple_of(step * iw, iw), iw)
    ones = jnp.ones((16, 1024), BF16)
    for s in range(n_seq):
        rhs_q = jnp.concatenate([zeros(32), xt[s, 0:32, cols], zeros(64)], axis=0)
        rq[s] = rhs_q
        top = jnp.full((8, iw), -jnp.inf, F32)
        for c in range(8):
            lo = b_ref[2 * c : 2 * c + 2, 0].reshape(128, 128)
            hi = b_ref[2 * c : 2 * c + 2, 1].reshape(128, 128)
            sc = nn(x_ref[c, s], rhs_q) + jnp.concatenate([lo, hi], axis=1).astype(F32)
            scores[c] = sc
            top = jnp.maximum(top, jnp.max(sc.reshape(16, 8, iw), axis=0))
        top = jnp.max(top, axis=0, keepdims=True)
        for c in range(8):
            exps[s, c] = jnp.exp(scores[c] - top).astype(BF16)
        left = jnp.concatenate([xt[s, 64:96, :], ones], axis=0)
        ot = nn(left, exps[s].reshape(1024, iw))
        inv = 1.0 / ot[32:33]
        ot = ot[0:32] * inv
        da = (xt[s, 96:128, cols].astype(F32) * inv).astype(BF16)
        delta[s] = jnp.sum(da.astype(F32) * ot, axis=0, keepdims=True)
        ra[s] = jnp.concatenate([zeros(64), da, zeros(32)], axis=0)
        for t in range(2):
            part = jnp.concatenate(
                [ot[:, t * 128 : (t + 1) * 128], jnp.zeros((96, 128), F32)], axis=0
            )
            acc[s, step * 2 + t] += part.T
    for c in range(8):
        total = jnp.zeros((128, iw), F32)
        for s in range(n_seq):
            e = exps[s, c]
            ds = e.astype(F32) * (nn(x_ref[c, s], ra[s]) - delta[s])
            total = total + ds
            ds = ds.astype(BF16)
            dsc[s, c] = ds
            acc[s, c] += nt(ds, rq[s]) + nt(e, ra[s])
        low = total.astype(BF16)
        db_ref[2 * c : 2 * c + 2, 0] = low[:, :128].reshape(2, 64, 128)
        db_ref[2 * c : 2 * c + 2, 1] = low[:, 128:].reshape(2, 64, 128)
    for s in range(n_seq):
        dq = nn(xt[s, 32:64, :], dsc[s].reshape(1024, iw)) * SCALE
        for t in range(2):
            part = jnp.concatenate(
                [jnp.zeros((96, 128), F32), dq[:, t * 128 : (t + 1) * 128]], axis=0
            )
            acc[s, step * 2 + t] += part.T

    @pl.when(step == pl.num_programs(0) - 1)
    def _():
        for s in range(n_seq):
            for r in range(8):
                o_ref[r, s] = acc[s, r].astype(BF16)


def attention(x, bias):
    r, s, n, _ = x.shape
    seqs = bias.shape[0]
    return pl.pallas_call(
        attention_kernel,
        grid=(4,),
        in_specs=[
            pl.BlockSpec((r, s, n, 128), lambda g: (0, 0, 0, 0)),
            pl.BlockSpec((seqs, 2, 64, 128), lambda g: (0, g, 0, 0)),
        ],
        out_specs=[
            pl.BlockSpec((r, s, n, 128), lambda g: (0, 0, 0, 0)),
            pl.BlockSpec((seqs, 2, 64, 128), lambda g: (0, g, 0, 0)),
        ],
        out_shape=[
            jax.ShapeDtypeStruct((r, s, n, 128), BF16),
            jax.ShapeDtypeStruct((seqs, r, 64, 128), BF16),
        ],
        scratch_shapes=[
            pltpu.VMEM((s, 128, 1024), BF16),
            pltpu.VMEM((s, 8, 128, 128), F32),
            pltpu.VMEM((8, 128, 256), F32),
            pltpu.VMEM((s, 8, 128, 256), BF16),
            pltpu.VMEM((s, 8, 128, 256), BF16),
            pltpu.VMEM((s, 128, 256), BF16),
            pltpu.VMEM((s, 128, 256), BF16),
            pltpu.VMEM((s, 1, 256), F32),
        ],
        compiler_params=params(),
        name="attention",
    )(x, bias)


def finish_kernel(
    x_ref, gain_ref, w_ref, wo_ref, up_ref, gate_ref, dg_ref, back_ref,
    inc_ref, dx_ref, dw_ref, acc,
):
    step = pl.program_id(0)
    hat, inv = normalize(x_ref[0])
    gain = gain_ref[...]
    normed = (hat * gain).astype(BF16)
    gate = gate_ref[0]
    d_gated = dg_ref[0]
    up = up_ref[0]
    back = [back_ref[h, 0] for h in range(HEADS)]
    pick = lambda a: jnp.concatenate([b[:, a * DH : (a + 1) * DH] for b in back], axis=1)
    attended = pick(0).astype(F32)
    gated = (gate * attended).astype(BF16)
    inc_ref[0] = nn(gated, wo_ref[...]).astype(BF16)
    d_pre = (d_gated * attended * gate * (1.0 - gate)).astype(BF16)
    d_proj = jnp.concatenate([pick(3), pick(1), pick(2), d_pre], axis=1)
    grad = nt(d_proj, w_ref[...])
    dx_ref[0] = normalize_grad(hat, inv, gain, grad).astype(BF16)

    @pl.when(step == 0)
    def _():
        acc[...] = jnp.zeros_like(acc)

    acc[:, :1024] += tn(normed, d_proj)
    acc[:, 1024:] += tn(gated, up)

    @pl.when(step == pl.num_programs(0) - 1)
    def _():
        for b in range(10):
            dw_ref[b] = acc[:, b * 128 : (b + 1) * 128].astype(BF16)


def finish(x, gain, w, wo, up, gate, dg, back):
    s, n, c = x.shape
    whole = lambda *shape: pl.BlockSpec(shape, lambda i: (0,) * len(shape))
    row = pl.BlockSpec((1, n, c), lambda i: (i, 0, 0))
    return pl.pallas_call(
        finish_kernel,
        grid=(s,),
        in_specs=[
            row, whole(1, c), whole(c, 4 * c), whole(c, c), row, row, row,
            pl.BlockSpec((HEADS, 1, n, 128), lambda i: (0, i, 0, 0)),
        ],
        out_specs=[row, row, whole(10, 256, 128)],
        out_shape=[
            jax.ShapeDtypeStruct((s, n, c), BF16),
            jax.ShapeDtypeStruct((s, n, c), BF16),
            jax.ShapeDtypeStruct((10, 256, 128), BF16),
        ],
        scratch_shapes=[pltpu.VMEM((c, 5 * c), F32)],
        compiler_params=params(),
        name="finish",
    )(x, gain, w, wo, up, gate, dg, back)


def pair_grad_kernel(x_ref, gain_ref, wt_ref, db_ref, dx_ref, dw_ref, tmp):
    step = pl.program_id(0)
    gain = gain_ref[...]
    wt = wt_ref[...]
    tmp[...] = db_ref[...].astype(F32)

    @pl.when(step == 0)
    def _():
        dw_ref[...] = jnp.zeros_like(dw_ref)

    total = jnp.zeros((HEADS, 128), F32)
    for j in range(x_ref.shape[0]):
        hat, inv = normalize(x_ref[j])
        normed = (hat * gain).astype(BF16)
        db = tmp[:, j, :].astype(BF16)
        dx_ref[j] = normalize_grad(hat, inv, gain, tn(db, wt)).astype(BF16)
        total = total + nn(db, normed)
    dw_ref[...] += total


def pair_grad(pair, gain, wt, db):
    j, i, c = pair.shape
    step = 16
    return pl.pallas_call(
        pair_grad_kernel,
        grid=(j // step,),
        in_specs=[
            pl.BlockSpec((step, i, c), lambda g: (g, 0, 0)),
            pl.BlockSpec((1, c), lambda g: (0, 0)),
            pl.BlockSpec((HEADS, c), lambda g: (0, 0)),
            pl.BlockSpec((HEADS, step, i), lambda g: (0, g, 0)),
        ],
        out_specs=[
            pl.BlockSpec((step, i, c), lambda g: (g, 0, 0)),
            pl.BlockSpec((HEADS, c), lambda g: (0, 0)),
        ],
        out_shape=[
            jax.ShapeDtypeStruct((j, i, c), BF16),
            jax.ShapeDtypeStruct((HEADS, c), F32),
        ],
        scratch_shapes=[pltpu.VMEM((HEADS, step, i), F32)],
        compiler_params=params(),
        name="pair_grad",
    )(pair, gain, wt, db)


def swap(x, axis, groups=None):
    return lax.all_to_all(
        x, axis, split_axis=0, concat_axis=0, tiled=True, axis_index_groups=groups
    )


CORES = [[2 * m + c for m in range(8)] for c in range(2)]
OTHER = [(i, i ^ 1) for i in range(16)]


def gather_bias(x):
    core = lax.axis_index("seq") & 1
    mine = swap(jnp.broadcast_to(x[None], (8,) + x.shape), "seq", CORES)
    other = lax.ppermute(mine, "seq", OTHER)
    first = jnp.where(core == 0, mine, other)
    second = jnp.where(core == 0, other, mine)
    return jnp.stack([first, second], axis=1).reshape((16,) + x.shape)


def scatter_bias(x):
    core = lax.axis_index("seq") & 1
    x = x.reshape((8, 2) + x.shape[1:])
    send = lax.dynamic_index_in_dim(x, 1 - core, 1, keepdims=False)
    keep = lax.dynamic_index_in_dim(x, core, 1, keepdims=False)
    got = lax.ppermute(send, "seq", OTHER)
    both = (keep.astype(F32) + got.astype(F32)).astype(BF16)
    return jnp.sum(swap(both, "seq", CORES).astype(F32), axis=0).astype(BF16)


def local(x, gain, w, shift, wo, pair, pair_gain, wb, up):
    gain = gain.reshape(1, -1)
    shift = shift.reshape(1, -1)
    pair_gain = pair_gain.reshape(1, -1)
    wt = wb.T
    packed, gate, dg = project(x, gain, w, shift, wo, up)
    bias = pair_bias(pair, pair_gain, wt)
    bias = gather_bias(swap(bias, "res"))
    back, d_bias = attention(swap(packed, "res"), bias)
    d_bias = swap(scatter_bias(d_bias), "res")
    back = swap(back, "res")
    inc, dx, dw = finish(x, gain, w, wo, up, gate, dg, back)
    d_pair, dwb = pair_grad(pair, pair_gain, wt, d_bias)
    rows = jnp.concatenate(
        [dw.reshape(2560, 128), dwb.astype(BF16), jnp.zeros((120, 128), BF16)], axis=0
    ).reshape(128, 21, 128)
    part = jnp.sum(swap(rows, ("seq", "res")).astype(F32), axis=0).astype(BF16)
    rows = swap(jnp.broadcast_to(part[None], (128, 21, 128)), ("seq", "res"))
    rows = rows.reshape(2688, 128).astype(F32)
    dw = jnp.swapaxes(rows[:2560].reshape(10, 256, 128), 0, 1).reshape(256, 1280)
    return inc, dx, d_pair, dw[:, :1024], dw[:, 1024:], rows[2560:2568].T


def solution(mesh):
    tok = P("seq", "res", None)
    return jax.shard_map(
        local,
        mesh=mesh,
        in_specs=(tok, P(), P(), P(), P(), tok, P(), P(), tok),
        out_specs=(tok, tok, tok, P(), P(), P()),
        check_vma=False,
    )
```

time: 626 us -> 216 us (0.35)
  waiting for transfers between devices: 356 us -> 28.5 us
  matrix products: 67.8 us -> 0 us
  Pallas kernels: 0 us -> 50.7 us
  local copies, waits for them, and re-layouts: 60.9 us -> 14.3 us
  other arithmetic: 43.8 us -> 7.32 us
  blocking collectives: 80.1 us -> 97.2 us
  starting transfers between devices: 0.6 us -> 16.3 us
  between operations: 14 us -> 0.88 us
    psum x1 -> x0, waiting for transfers between devices: 151 us -> none  [local(): lax.psum((d_w_qkvg_part, d_w_out_part, d_w_bias_part), ('seq', 'res'))]
    all_gather x2 -> x0, waiting for transfers between devices: 134 us -> none  [the longest x1 85.6 us: local(): all_kv = lax.all_gather(key_vals, 'res', axis=1, tiled=True)]
    all_to_all x0 -> x5, blocking collectives: none -> 97.2 us  [swap(): lax.all_to_all(x, axis, split_axis=0, concat_axis=0, tiled=True, axis_ind...]
    psum x1 -> x0, blocking collectives: 80.1 us -> none  [local(): lax.psum((d_w_qkvg_part, d_w_out_part, d_w_bias_part), ('seq', 'res'))]
    reduce_scatter x2 -> x0, waiting for transfers between devices: 70.9 us -> none  [the longest x1 66.4 us: local(): lax.psum_scatter(d_bias.astype(jnp.bfloat16), 'seq', scatter_dimension=1,...]
    dot_general x37 -> x0, matrix products: 67.8 us -> none  [the longest x8 30.6 us: score_block(): jnp.einsum('ihd,jhd->hij', q_one, k_one, preferred_element_type=jnp.float32)]
    pallas_call x0 -> x5, Pallas kernels: none -> 50.7 us  [the longest x1 24.5 us: attention(): pl.pallas_call(attention_kernel, grid=(4,), in_specs=[pl.BlockSpec((r, s,...]
    add x4 -> x0, other arithmetic: 28.7 us -> none  [query_whole(): running = running + jnp.swapaxes(d_scores, 1, 2).astype(jnp.float32)]
  transfers between devices with their start and end apart: 5 -> 5, of which waited for: 5 -> 3; matrix products, arithmetic and copies ran while one was open for 4% -> 3% of each run, Pallas kernels for 0% -> 4%
where the time goes in v1:
time: 216 us; the launch traced here: 215 us
  blocking collectives  97.2 us (45%)
  Pallas kernels  50.7 us (23%)
  waiting for transfers between devices  28.5 us (13%)
  starting transfers between devices  16.3 us (8%)
  local copies, waits for them, and re-layouts  14.3 us (7%)
  other arithmetic  7.32 us (3%)
    all_to_all x5, blocking collectives, swap(): lax.all_to_all(x, axis, split_axis=0, concat_axis=0, tiled=True, axis_ind...  97.2 us
    all_to_all x3, waiting for transfers between devices, swap(): lax.all_to_all(x, axis, split_axis=0, concat_axis=0, tiled=True, axis_ind...  26.1 us
    pallas_call x1, Pallas kernels, attention(): pl.pallas_call(attention_kernel, grid=(4,), in_specs=[pl.BlockSpec((r, s,...  24.5 us
    pallas_call x1, Pallas kernels, pair_grad(): pl.pallas_call(pair_grad_kernel, grid=(j // step,), in_specs=[pl.BlockSpe...  14.4 us
    unnamed x44, local copies, waits for them, and re-layouts  11.6 us
    all_to_all x3, starting transfers between devices, swap(): lax.all_to_all(x, axis, split_axis=0, concat_axis=0, tiled=True, axis_ind...  11.4 us
    pallas_call x1, Pallas kernels, finish(): pl.pallas_call(finish_kernel, grid=(s,), in_specs=[row, whole(1, c), whol...  4.88 us
  transfers between devices with their start and end apart: 5, of which 3 were waited for; matrix products, arithmetic and copies ran while one was open for 3% of the time, Pallas kernels for 4%

profile of v1, /device:TPU:1, one launch (start us, length us, event | category | flops | bytes accessed | tf_op | source)
XLA Modules:
  0.0 215.1 jit_solution(10263487743999256485)
XLA Ops:
  0.6 1.6 copy-done
  3.6 3.7 %pair_bias.1 = bf16[8,64,128]{2,1,0:T(8,128)(2,1)S(1)} custom-call(bf16[64,128,128]{2,1,0:T(8,128)(2,1)S(1)} %copy-done, f32[1,128]{1,0:T(1,128)S(1)} %bitcast.31, bf16[8,128]{1,0:T(8,128)(2,1)S(1)} %bitcast.27), custom_call_target="tpu_custom_call" | custom-call | tf_op jit(solution)/shard_map/pair_bias/pallas_call | solution.py:99
  7.3 11.0 %all_to_all.40 = bf16[8,64,128]{2,1,0:T(8,128)(2,1)S(1)} all-to-all(bf16[8,64,128]{2,1,0:T(8,128)(2,1)S(1)} %pair_bias.1), channel_id=1, replica_groups=mesh['seq'=16,'res'=8] {'res'}, dimensions={0} | all-to-all | bytes 262144 | tf_op jit(solution)/shard_map/all_to_all | solution.py:319
  18.6 21.3 %all_to_all.41 = bf16[8,8,64,128]{3,2,1,0:T(8,128)(2,1)S(1)} all-to-all(bf16[8,8,64,128]{3,2,1,0:T(8,128)(2,1)S(1)} %broadcast_in_dim.6), channel_id=1, replica_groups={{0,16,32,48,64,80,96,112},{8,24,40,56,72,88,104,120},{1,17,33,49,65,81,..., dimensions={0} | all-to-all | bytes 2097152 | tf_op jit(solution)/shard_map/all_to_all | solution.py:319
  40.0 4.0 %collective-permute-start = (bf16[8,8,64,128]{3,2,1,0:T(8,128)(2,1)S(1)}, bf16[8,8,64,128]{3,2,1,0:T(8,128)(2,1)}, u32[]{:S(2)}, u32[]{:S(2)}) collective-permute-start(bf16[8,8,64,128]{3,2,1,0:T(8,128)(2,1)S(1)} %all_to_all.41), channel_id=1, source_target_pairs={{0,8},{8,0},{16,24},{24,16},{32,40},{40,32},{48,56},{56,48},{64,72... | collective-permute-start | bytes 3145736 | tf_op jit(solution)/shard_map/ppermute | solution.py:331
  43.9 3.2 %project.1 = (bf16[8,4,128,128]{3,2,1,0:T(8,128)(2,1)}, f32[4,128,256]{2,1,0:T(8,128)S(1)}, f32[4,128,256]{2,1,0:T(8,128)S(1)}) custom-call(bf16[4,128,256]{2,1,0:T(8,128)(2,1)S(1)} %copy-done.4, f32[1,256]{1,0:T(1,128)S(1)} %bitcast.29, bf16[256,1024]{1,0:T(8,128)(2,1)S(1)} %copy-done.2, f32[1,256]{1,0:T(1,128)S(1)} %bitcast.33, ...), custom_call_target="tpu_custom_call" | custom-call | tf_op jit(solution)/shard_map/project/pallas_call | solution.py:72
  48.7 3.6 %all-to-all-start = ((bf16[8,4,128,128]{3,2,1,0:T(8,128)(2,1)}), bf16[8,4,128,128]{3,2,1,0:T(8,128)(2,1)S(1)}, u32[]{:S(2)}, u32[]{:S(2)}) async-start(bf16[8,4,128,128]{3,2,1,0:T(8,128)(2,1)} %get-tuple-element.18), calls=%async_computation | async-start | bytes 2097152 | tf_op jit(solution)/shard_map/all_to_all | solution.py:319
  52.3 1.4 select_bitcast_fusion.1
  53.7 1.5 pad_maximum_fusion
  55.2 14.4 %all-to-all-done.x_ref = bf16[8,4,128,128]{3,2,1,0:T(8,128)(2,1)S(1)} async-done(((bf16[8,4,128,128]{3,2,1,0:T(8,128)(2,1)}), bf16[8,4,128,128]{3,2,1,0:T(8,128)(2,1)S(1)}, u32[]{:S(2)}, u32[]{:S(2)}) %all-to-all-start) | async-done | bytes 1048608 | tf_op jit(solution)/shard_map/all_to_all | solution.py:319
  69.6 24.5 %attention.1 = (bf16[8,4,128,128]{3,2,1,0:T(8,128)(2,1)}, bf16[16,8,64,128]{3,2,1,0:T(8,128)(2,1)S(1)}) custom-call(bf16[8,4,128,128]{3,2,1,0:T(8,128)(2,1)S(1)} %all-to-all-done.x_ref, bf16[16,8,64,128]{3,2,1,0:T(8,128)(2,1)} %bitcast.34), custom_call_target="tpu_custom_call" | custom-call | tf_op jit(solution)/shard_map/attention/pallas_call | solution.py:185
  95.0 2.4 %collective-permute-done.1 = bf16[8,8,64,128]{3,2,1,0:T(8,128)(2,1)} collective-permute-done((bf16[8,8,64,128]{3,2,1,0:T(8,128)(2,1)S(1)}, bf16[8,8,64,128]{3,2,1,0:T(8,128)(2,1)}, u32[]{:S(2)}, u32[]{:S(2)}) %collective-permute-start.1) | collective-permute-done | bytes 1048608 | tf_op jit(solution)/shard_map/ppermute | solution.py:342
  97.4 1.6 fusion
  99.0 19.1 %all_to_all.42 = bf16[8,8,64,128]{3,2,1,0:T(8,128)(2,1)} all-to-all(bf16[8,8,64,128]{3,2,1,0:T(8,128)(2,1)S(1)} %fusion), channel_id=1, replica_groups={{0,16,32,48,64,80,96,112},{8,24,40,56,72,88,104,120},{1,17,33,49,65,81,..., dimensions={0} | all-to-all | bytes 2097152 | tf_op jit(solution)/shard_map/all_to_all | solution.py:319
  118.1 3.7 %all-to-all-start.3 = ((bf16[8,4,128,128]{3,2,1,0:T(8,128)(2,1)}), bf16[8,4,128,128]{3,2,1,0:T(8,128)(2,1)S(1)}, u32[]{:S(2)}, u32[]{:S(2)}) async-start(bf16[8,4,128,128]{3,2,1,0:T(8,128)(2,1)} %get-tuple-element.19), calls=%async_computation.3 | async-start | bytes 2097152 | tf_op jit(solution)/shard_map/all_to_all | solution.py:319
  121.8 2.2 %reduce_sum.24 = bf16[8,64,128]{2,1,0:T(8,128)(2,1)} reduce(bf16[8,8,64,128]{3,2,1,0:T(8,128)(2,1)} %all_to_all.42, bf16[]{:T(256)} %constant.23.clone.1), dimensions={0}, to_apply=%region_0.1 | reduce | flops 458752 | bytes 1179650 | tf_op jit(solution)/shard_map/reduce_sum | solution.py:344
  124.0 11.7 %all-to-all-done.3.back_ref = bf16[8,4,128,128]{3,2,1,0:T(8,128)(2,1)S(1)} async-done(((bf16[8,4,128,128]{3,2,1,0:T(8,128)(2,1)}), bf16[8,4,128,128]{3,2,1,0:T(8,128)(2,1)S(1)}, u32[]{:S(2)}, u32[]{:S(2)}) %all-to-all-start.3) | async-done | bytes 1048608 | tf_op jit(solution)/shard_map/all_to_all | solution.py:319
  135.8 4.2 %all-to-all-start.5 = ((bf16[8,64,128]{2,1,0:T(8,128)(2,1)}), bf16[8,64,128]{2,1,0:T(8,128)(2,1)}, u32[]{:S(2)}, u32[]{:S(2)}) async-start(bf16[8,64,128]{2,1,0:T(8,128)(2,1)} %reduce_sum.24), calls=%async_computation.5 | async-start | bytes 262144 | tf_op jit(solution)/shard_map/all_to_all | solution.py:319
  140.7 1.0 copy-done.3
  144.7 4.9 %finish.1 = (bf16[4,128,256]{2,1,0:T(8,128)(2,1)}, bf16[4,128,256]{2,1,0:T(8,128)(2,1)}, bf16[10,256,128]{2,1,0:T(8,128)(2,1)S(1)}) custom-call(bf16[4,128,256]{2,1,0:T(8,128)(2,1)S(1)} %copy-done.4, f32[1,256]{1,0:T(1,128)S(1)} %bitcast.30, bf16[256,1024]{1,0:T(8,128)(2,1)S(1)} %copy-done.3, bf16[256,256]{1,0:T(8,128)(2,1)S(1)} %copy-done.9, ...), custom_call_target="tpu_custom_call" | custom-call | tf_op jit(solution)/shard_map/finish/pallas_call | solution.py:253
  150.5 14.4 %pair_grad.1 = (bf16[64,128,128]{2,1,0:T(8,128)(2,1)}, f32[8,128]{1,0:T(8,128)S(1)}) custom-call(bf16[64,128,128]{2,1,0:T(8,128)(2,1)S(1)} %copy-done.1, f32[1,128]{1,0:T(1,128)S(1)} %bitcast.32, bf16[8,128]{1,0:T(8,128)(2,1)S(1)} %bitcast.28, bf16[8,64,128]{2,1,0:T(8,128)(2,1)} %all-to-all-done.5.db_ref), custom_call_target="tpu_custom_call" | custom-call | tf_op jit(solution)/shard_map/pair_grad/pallas_call | solution.py:295
  165.6 25.3 %all_to_all.43 = bf16[128,21,128]{2,1,0:T(8,128)(2,1)S(1)} all-to-all(bf16[128,21,128]{2,1,0:T(8,128)(2,1)S(1)} %reshape.52), channel_id=1, replica_groups=mesh['seq'=16,'res'=8] {'seq','res'}, dimensions={0} | all-to-all | bytes 1376256 | tf_op jit(solution)/shard_map/all_to_all | solution.py:319
  191.2 20.4 %all_to_all.44 = bf16[128,21,128]{2,1,0:T(8,128)(2,1)S(1)} all-to-all(bf16[128,21,128]{2,1,0:T(8,128)(2,1)S(1)} %broadcast_in_dim.8), channel_id=1, replica_groups=mesh['seq'=16,'res'=8] {'seq','res'}, dimensions={0} | all-to-all | bytes 1376256 | tf_op jit(solution)/shard_map/all_to_all | solution.py:319
  213.0 1.3 copy.19
  (59 shorter events, 11.8 us)
Async XLA Ops:
  0.6 1.6 copy-start
  7.3 36.6 %copy-start.2 = (bf16[256,1024]{1,0:T(8,128)(2,1)S(1)}, bf16[256,1024]{1,0:T(8,128)(2,1)}, u32[]{:S(2)}) copy-start(bf16[256,1024]{1,0:T(8,128)(2,1)} %w_ref.3) | copy-start | bytes 1572868
  7.3 36.6 %copy-start.4 = (bf16[4,128,256]{2,1,0:T(8,128)(2,1)S(1)}, bf16[4,128,256]{2,1,0:T(8,128)(2,1)}, u32[]{:S(2)}) copy-start(bf16[4,128,256]{2,1,0:T(8,128)(2,1)} %x_ref.6) | copy-start | bytes 786436
  7.3 36.6 %copy-start.5 = (bf16[4,128,256]{2,1,0:T(8,128)(2,1)S(1)}, bf16[4,128,256]{2,1,0:T(8,128)(2,1)}, u32[]{:S(2)}) copy-start(bf16[4,128,256]{2,1,0:T(8,128)(2,1)} %up_ref.3) | copy-start | bytes 786436
  7.3 36.6 %copy-start.9 = (bf16[256,256]{1,0:T(8,128)(2,1)S(1)}, bf16[256,256]{1,0:T(8,128)(2,1)}, u32[]{:S(2)}) copy-start(bf16[256,256]{1,0:T(8,128)(2,1)} %wo_ref.3) | copy-start | bytes 393220
  7.3 36.6 %copy-start.16 = (f32[256]{0:T(256)S(1)}, f32[256]{0:T(256)}, u32[]{:S(2)}) copy-start(f32[256]{0:T(256)} %param.10) | copy-start | bytes 3076
  7.3 36.6 %copy-start.19 = (f32[256]{0:T(256)S(1)}, f32[256]{0:T(256)}, u32[]{:S(2)}) copy-start(f32[256]{0:T(256)} %param.12) | copy-start | bytes 3076
  40.0 12.4 %collective-permute-start = (bf16[8,8,64,128]{3,2,1,0:T(8,128)(2,1)S(1)}, bf16[8,8,64,128]{3,2,1,0:T(8,128)(2,1)}, u32[]{:S(2)}, u32[]{:S(2)}) collective-permute-start(bf16[8,8,64,128]{3,2,1,0:T(8,128)(2,1)S(1)} %all_to_all.41), channel_id=1, source_target_pairs={{0,8},{8,0},{16,24},{24,16},{32,40},{40,32},{48,56},{56,48},{64,72... | collective-permute-start | bytes 3145736 | tf_op jit(solution)/shard_map/ppermute | solution.py:331
  47.2 0.8 copy-start.10
  48.0 0.8 copy-start.12
  48.7 20.8 %all-to-all-start = ((bf16[8,4,128,128]{3,2,1,0:T(8,128)(2,1)}), bf16[8,4,128,128]{3,2,1,0:T(8,128)(2,1)S(1)}, u32[]{:S(2)}, u32[]{:S(2)}) async-start(bf16[8,4,128,128]{3,2,1,0:T(8,128)(2,1)} %get-tuple-element.18), calls=%async_computation | async-start | bytes 2097152 | tf_op jit(solution)/shard_map/all_to_all | solution.py:319
  94.1 3.3 %collective-permute-start.1 = (bf16[8,8,64,128]{3,2,1,0:T(8,128)(2,1)S(1)}, bf16[8,8,64,128]{3,2,1,0:T(8,128)(2,1)}, u32[]{:S(2)}, u32[]{:S(2)}) collective-permute-start(bf16[8,8,64,128]{3,2,1,0:T(8,128)(2,1)S(1)} %dynamic-slice_bitcast_fusion), channel_id=1, source_target_pairs={{0,8},{8,0},{16,24},{24,16},{32,40},{40,32},{48,56},{56,48},{64,72... | collective-permute-start | bytes 3145736 | tf_op jit(solution)/shard_map/ppermute | solution.py:342
  118.1 32.4 %copy-start.15 = (bf16[128,8]{0,1:T(8,128)(2,1)S(1)}, bf16[128,8]{0,1:T(8,128)(2,1)}, u32[]{:S(2)}) copy-start(bf16[128,8]{0,1:T(8,128)(2,1)} %param.16) | copy-start | bytes 6148
  118.1 32.4 %copy-start.18 = (f32[128]{0:T(128)S(1)}, f32[128]{0:T(128)}, u32[]{:S(2)}) copy-start(f32[128]{0:T(128)} %param.15) | copy-start | bytes 1540
  118.1 17.7 %all-to-all-start.3 = ((bf16[8,4,128,128]{3,2,1,0:T(8,128)(2,1)}), bf16[8,4,128,128]{3,2,1,0:T(8,128)(2,1)S(1)}, u32[]{:S(2)}, u32[]{:S(2)}) async-start(bf16[8,4,128,128]{3,2,1,0:T(8,128)(2,1)} %get-tuple-element.19), calls=%async_computation.3 | async-start | bytes 2097152 | tf_op jit(solution)/shard_map/all_to_all | solution.py:319
  121.8 28.7 %copy-start.1 = (bf16[64,128,128]{2,1,0:T(8,128)(2,1)S(1)}, bf16[64,128,128]{2,1,0:T(8,128)(2,1)}, u32[]{:S(2)}) copy-start(bf16[64,128,128]{2,1,0:T(8,128)(2,1)} %x_ref.7) | copy-start | bytes 6291460
  135.8 14.7 %all-to-all-start.5 = ((bf16[8,64,128]{2,1,0:T(8,128)(2,1)}), bf16[8,64,128]{2,1,0:T(8,128)(2,1)}, u32[]{:S(2)}, u32[]{:S(2)}) async-start(bf16[8,64,128]{2,1,0:T(8,128)(2,1)} %reduce_sum.24), calls=%async_computation.5 | async-start | bytes 262144 | tf_op jit(solution)/shard_map/all_to_all | solution.py:319
  140.7 1.0 copy-start.3
  141.7 0.9 copy-start.6
  142.6 1.0 copy-start.11
  143.7 1.0 copy-start.13
  149.6 0.8 copy-start.7
  150.4 14.5 %copy-start.20 = (bf16[2688]{0:T(1024)(128)(2,1)S(1)}, bf16[2688]{0:T(1024)(128)(2,1)}, u32[]{:S(2)}) copy-start(bf16[2688]{0:T(1024)(128)(2,1)} %pad.2.clone) | copy-start | bytes 16132
  150.5 14.5 %copy-start.8 = (bf16[10,256,128]{2,1,0:T(8,128)(2,1)S(1)}, bf16[10,256,128]{2,1,0:T(8,128)(2,1)}, u32[]{:S(2)}) copy-start(bf16[10,256,128]{2,1,0:T(8,128)(2,1)} %copy-done.7) | copy-start | bytes 1966084
  (2 other events, 1.3 us)

commit v2 on v1

--- a/solution.py
+++ b/solution.py
@@ -40,6 +40,10 @@
     mean_g = jnp.mean(g, axis=-1, keepdims=True)
     mean_gx = jnp.mean(g * hat, axis=-1, keepdims=True)
     return inv * (g - mean_g - hat * mean_gx)
+
+
+def cost(us):
+    return pl.CostEstimate(flops=int(us * 1e9), bytes_accessed=int(us * 3e6), transcendentals=0)
 
 
 def params(n=1):
@@ -80,6 +84,7 @@
             jax.ShapeDtypeStruct((s, n, c), F32),
         ],
         compiler_params=params(),
+        cost_estimate=cost(3),
         name="project",
     )(x, gain, w, shift, wo, up)
 
@@ -108,33 +113,44 @@
         out_shape=jax.ShapeDtypeStruct((HEADS, j, i), BF16),
         scratch_shapes=[pltpu.VMEM((HEADS, step, i), F32)],
         compiler_params=params(),
+        cost_estimate=cost(4),
         name="pair_bias",
     )(pair, gain, wt)
 
 
-def attention_kernel(x_ref, b_ref, o_ref, db_ref, xt, acc, scores, exps, dsc, rq, ra, delta):
+def attention_kernel(
+    place_ref, x_ref, own_ref, other_ref, begin_ref, o_ref, down_ref, dother_ref,
+    xr, xt, acc, scores, exps, dsc, rq, ra, delta, *, first, last,
+):
     step = pl.program_id(0)
     n_seq = x_ref.shape[1]
     iw = 256
+    core = place_ref[8]
+    mine = pl.ds(pl.multiple_of(core * 64, 64), 64)
+    others = pl.ds(pl.multiple_of((1 - core) * 64, 64), 64)
     zeros = lambda rows: jnp.zeros((rows, iw), BF16)
 
     @pl.when(step == 0)
     def _():
         for s in range(n_seq):
-            for r in range(8):
-                xt[s, :, r * 128 : (r + 1) * 128] = x_ref[r, s].T
-        acc[...] = jnp.zeros_like(acc)
-
-    cols = pl.ds(pl.multiple_of(step * iw, iw), iw)
+            for c in range(8):
+                chip = place_ref[c]
+                xr[c, s, 0:64] = x_ref[chip, s, mine]
+                xr[c, s, 64:128] = x_ref[chip, s, others]
+                xt[s, :, c * 128 : (c + 1) * 128] = xr[c, s].T
+        acc[...] = jnp.zeros_like(acc) if begin_ref is None else begin_ref[...]
+
     ones = jnp.ones((16, 1024), BF16)
     for s in range(n_seq):
-        rhs_q = jnp.concatenate([zeros(32), xt[s, 0:32, cols], zeros(64)], axis=0)
+        block = 2 * step + first
+        xq = jnp.concatenate([x_ref[block, s].T, x_ref[block + 1, s].T], axis=1)
+        rhs_q = jnp.concatenate([zeros(32), xq[0:32], zeros(64)], axis=0)
         rq[s] = rhs_q
         top = jnp.full((8, iw), -jnp.inf, F32)
         for c in range(8):
-            lo = b_ref[2 * c : 2 * c + 2, 0].reshape(128, 128)
-            hi = b_ref[2 * c : 2 * c + 2, 1].reshape(128, 128)
-            sc = nn(x_ref[c, s], rhs_q) + jnp.concatenate([lo, hi], axis=1).astype(F32)
+            lo = jnp.concatenate([own_ref[c, 0], other_ref[c, 0]], axis=0)
+            hi = jnp.concatenate([own_ref[c, 1], other_ref[c, 1]], axis=0)
+            sc = nn(xr[c, s], rhs_q) + jnp.concatenate([lo, hi], axis=1).astype(F32)
             scores[c] = sc
             top = jnp.maximum(top, jnp.max(sc.reshape(16, 8, iw), axis=0))
         top = jnp.max(top, axis=0, keepdims=True)
@@ -144,72 +160,89 @@
         ot = nn(left, exps[s].reshape(1024, iw))
         inv = 1.0 / ot[32:33]
         ot = ot[0:32] * inv
-        da = (xt[s, 96:128, cols].astype(F32) * inv).astype(BF16)
+        da = (xq[96:128].astype(F32) * inv).astype(BF16)
         delta[s] = jnp.sum(da.astype(F32) * ot, axis=0, keepdims=True)
         ra[s] = jnp.concatenate([zeros(64), da, zeros(32)], axis=0)
         for t in range(2):
             part = jnp.concatenate(
                 [ot[:, t * 128 : (t + 1) * 128], jnp.zeros((96, 128), F32)], axis=0
             )
-            acc[s, step * 2 + t] += part.T
+            acc[s, block + t] += part.T
     for c in range(8):
         total = jnp.zeros((128, iw), F32)
+        chip = place_ref[c]
         for s in range(n_seq):
             e = exps[s, c]
-            ds = e.astype(F32) * (nn(x_ref[c, s], ra[s]) - delta[s])
+            ds = e.astype(F32) * (nn(xr[c, s], ra[s]) - delta[s])
             total = total + ds
             ds = ds.astype(BF16)
             dsc[s, c] = ds
-            acc[s, c] += nt(ds, rq[s]) + nt(e, ra[s])
+            more = nt(ds, rq[s]) + nt(e, ra[s])
+            acc[s, chip, mine] += more[:64]
+            acc[s, chip, others] += more[64:]
         low = total.astype(BF16)
-        db_ref[2 * c : 2 * c + 2, 0] = low[:, :128].reshape(2, 64, 128)
-        db_ref[2 * c : 2 * c + 2, 1] = low[:, 128:].reshape(2, 64, 128)
+        for t in range(2):
+            down_ref[c, t] = low[:64, t * 128 : (t + 1) * 128]
+            dother_ref[c, t] = low[64:, t * 128 : (t + 1) * 128]
     for s in range(n_seq):
+        block = 2 * step + first
         dq = nn(xt[s, 32:64, :], dsc[s].reshape(1024, iw)) * SCALE
         for t in range(2):
             part = jnp.concatenate(
                 [jnp.zeros((96, 128), F32), dq[:, t * 128 : (t + 1) * 128]], axis=0
             )
-            acc[s, step * 2 + t] += part.T
+            acc[s, block + t] += part.T
 
     @pl.when(step == pl.num_programs(0) - 1)
     def _():
-        for s in range(n_seq):
-            for r in range(8):
-                o_ref[r, s] = acc[s, r].astype(BF16)
-
-
-def attention(x, bias):
+        if last:
+            for s in range(n_seq):
+                for r in range(8):
+                    o_ref[r, s] = acc[s, r].astype(BF16)
+        else:
+            o_ref[...] = acc[...]
+
+
+def attention(place, x, own, other, begin, first, last):
     r, s, n, _ = x.shape
-    seqs = bias.shape[0]
+    blocks = own.shape[1]
+    half = pl.BlockSpec((8, 2, 64, 128), lambda g, p: (0, g, 0, 0))
+    fixed = lambda *shape: pl.BlockSpec(shape, lambda g, p: (0, 0, 0, 0))
+    body = functools.partial(attention_kernel, first=first, last=last)
+    out = (r, s, n, 128) if last else (s, r, n, 128)
+    if begin is None:
+        kernel = lambda p, x, a, b, *rest: body(p, x, a, b, None, *rest)
+        more, more_specs = (), []
+    else:
+        kernel, more, more_specs = body, (begin,), [fixed(s, r, n, 128)]
     return pl.pallas_call(
-        attention_kernel,
-        grid=(4,),
-        in_specs=[
-            pl.BlockSpec((r, s, n, 128), lambda g: (0, 0, 0, 0)),
-            pl.BlockSpec((seqs, 2, 64, 128), lambda g: (0, g, 0, 0)),
-        ],
-        out_specs=[
-            pl.BlockSpec((r, s, n, 128), lambda g: (0, 0, 0, 0)),
-            pl.BlockSpec((seqs, 2, 64, 128), lambda g: (0, g, 0, 0)),
-        ],
+        kernel,
+        grid_spec=pltpu.PrefetchScalarGridSpec(
+            num_scalar_prefetch=1,
+            grid=(blocks // 2,),
+            in_specs=[fixed(r, s, n, 128), half, half] + more_specs,
+            out_specs=[fixed(*out), half, half],
+            scratch_shapes=[
+                pltpu.VMEM((r, s, n, 128), BF16),
+                pltpu.VMEM((s, 128, 1024), BF16),
+                pltpu.VMEM((s, 8, 128, 128), F32),
+                pltpu.VMEM((8, 128, 256), F32),
+                pltpu.VMEM((s, 8, 128, 256), BF16),
+                pltpu.VMEM((s, 8, 128, 256), BF16),
+                pltpu.VMEM((s, 128, 256), BF16),
+                pltpu.VMEM((s, 128, 256), BF16),
+                pltpu.VMEM((s, 1, 256), F32),
+            ],
+        ),
         out_shape=[
-            jax.ShapeDtypeStruct((r, s, n, 128), BF16),
-            jax.ShapeDtypeStruct((seqs, r, 64, 128), BF16),
-        ],
-        scratch_shapes=[
-            pltpu.VMEM((s, 128, 1024), BF16),
-            pltpu.VMEM((s, 8, 128, 128), F32),
-            pltpu.VMEM((8, 128, 256), F32),
-            pltpu.VMEM((s, 8, 128, 256), BF16),
-            pltpu.VMEM((s, 8, 128, 256), BF16),
-            pltpu.VMEM((s, 128, 256), BF16),
-            pltpu.VMEM((s, 128, 256), BF16),
-            pltpu.VMEM((s, 1, 256), F32),
+            jax.ShapeDtypeStruct(out, BF16 if last else F32),
+            jax.ShapeDtypeStruct((8, blocks, 64, 128), BF16),
+            jax.ShapeDtypeStruct((8, blocks, 64, 128), BF16),
         ],
         compiler_params=params(),
+        cost_estimate=cost(25),
         name="attention",
-    )(x, bias)
+    )(place, x, own, other, *more)
 
 
 def finish_kernel(
@@ -265,27 +298,34 @@
         ],
         scratch_shapes=[pltpu.VMEM((c, 5 * c), F32)],
         compiler_params=params(),
+        cost_estimate=cost(5),
         name="finish",
     )(x, gain, w, wo, up, gate, dg, back)
 
 
-def pair_grad_kernel(x_ref, gain_ref, wt_ref, db_ref, dx_ref, dw_ref, tmp):
+def pair_grad_kernel(x_ref, gain_ref, wt_ref, db_ref, dx_ref, dw_ref, tmp, spread):
     step = pl.program_id(0)
     gain = gain_ref[...]
-    wt = wt_ref[...]
+    rows = x_ref.shape[0]
     tmp[...] = db_ref[...].astype(F32)
 
     @pl.when(step == 0)
     def _():
         dw_ref[...] = jnp.zeros_like(dw_ref)
-
+        place = lax.broadcasted_iota(jnp.int32, (HEADS, rows, 128), 1)
+        wide = jnp.broadcast_to(wt_ref[...].astype(F32)[:, None, :], (HEADS, rows, 128))
+        for j in range(rows):
+            block = jnp.where(place == j, wide, 0.0).reshape(HEADS * rows, 128)
+            spread[:, j * 128 : (j + 1) * 128] = block.astype(BF16)
+
+    turned = tmp[...].reshape(HEADS * rows, 128).T.astype(BF16)
     total = jnp.zeros((HEADS, 128), F32)
-    for j in range(x_ref.shape[0]):
+    for j in range(rows):
         hat, inv = normalize(x_ref[j])
         normed = (hat * gain).astype(BF16)
-        db = tmp[:, j, :].astype(BF16)
-        dx_ref[j] = normalize_grad(hat, inv, gain, tn(db, wt)).astype(BF16)
-        total = total + nn(db, normed)
+        grad = nn(turned, spread[:, j * 128 : (j + 1) * 128])
+        dx_ref[j] = normalize_grad(hat, inv, gain, grad).astype(BF16)
+        total = total + nn(tmp[:, j, :].astype(BF16), normed)
     dw_ref[...] += total
 
 
@@ -309,39 +349,140 @@
             jax.ShapeDtypeStruct((j, i, c), BF16),
             jax.ShapeDtypeStruct((HEADS, c), F32),
         ],
-        scratch_shapes=[pltpu.VMEM((HEADS, step, i), F32)],
+        scratch_shapes=[
+            pltpu.VMEM((HEADS, step, i), F32),
+            pltpu.VMEM((HEADS * step, step * 128), BF16),
+        ],
         compiler_params=params(),
+        cost_estimate=cost(5),
         name="pair_grad",
     )(pair, gain, wt, db)
 
 
-def swap(x, axis, groups=None):
+def swap(x, axis):
+    return lax.all_to_all(x, axis, split_axis=0, concat_axis=0, tiled=True)
+
+
+OTHER = [(i, i ^ 1) for i in range(16)]
+FAR = [(i, i ^ 8) for i in range(16)]
+
+
+def along(shift):
+    move = lambda i: (i & 9) | (((((i >> 1) & 3) + shift) % 4) << 1)
+    return [(i, move(i)) for i in range(16)]
+
+
+def send(x, pairs):
+    return lax.ppermute(x, "seq", pairs)
+
+
+def chip_order():
+    me = lax.axis_index("seq")
+    far, z, core = me >> 3, (me >> 1) & 3, me & 1
+    chips = [(far ^ d) * 4 + ((z - shift) & 3) for shift in range(4) for d in range(2)]
+    return jnp.stack(chips + [core]).astype(jnp.int32)
+
+
+def device(far, low, z, x, core):
+    return (far * 8 + z * 2 + core) * 8 + x * 2 + low
+
+
+LAYERS = [
+    [device(far, low, z, x, core) for z in range(4) for x in range(4)]
+    for far in range(2)
+    for low in range(2)
+    for core in range(2)
+]
+ALL = ("seq", "res")
+
+
+def layer_swap(x):
     return lax.all_to_all(
-        x, axis, split_axis=0, concat_axis=0, tiled=True, axis_index_groups=groups
+        x, ALL, split_axis=0, concat_axis=0, tiled=True, axis_index_groups=LAYERS
     )
 
 
-CORES = [[2 * m + c for m in range(8)] for c in range(2)]
-OTHER = [(i, i ^ 1) for i in range(16)]
-
-
-def gather_bias(x):
+def across(k):
+    pairs = []
+    for i in range(128):
+        seq, res = divmod(i, 8)
+        pairs.append((i, (seq ^ ((k >> 1) * 8)) * 8 + (res ^ (k & 1))))
+    return pairs
+
+
+def halve(rows):
     core = lax.axis_index("seq") & 1
-    mine = swap(jnp.broadcast_to(x[None], (8,) + x.shape), "seq", CORES)
-    other = lax.ppermute(mine, "seq", OTHER)
-    first = jnp.where(core == 0, mine, other)
-    second = jnp.where(core == 0, other, mine)
-    return jnp.stack([first, second], axis=1).reshape((16,) + x.shape)
-
-
-def scatter_bias(x):
-    core = lax.axis_index("seq") & 1
-    x = x.reshape((8, 2) + x.shape[1:])
-    send = lax.dynamic_index_in_dim(x, 1 - core, 1, keepdims=False)
-    keep = lax.dynamic_index_in_dim(x, core, 1, keepdims=False)
-    got = lax.ppermute(send, "seq", OTHER)
-    both = (keep.astype(F32) + got.astype(F32)).astype(BF16)
-    return jnp.sum(swap(both, "seq", CORES).astype(F32), axis=0).astype(BF16)
+    away = lax.dynamic_index_in_dim(rows, 1 - core, 0, keepdims=False)
+    keep = lax.dynamic_index_in_dim(rows, core, 0, keepdims=False)
+    return (keep.astype(F32) + send(away, OTHER).astype(F32)).astype(BF16)
+
+
+def sum_layers(part, extra):
+    part = jnp.sum(layer_swap(part).astype(F32), axis=0)
+    part = jnp.concatenate([part, jnp.pad(extra, ((0, 8), (0, 0)))])
+    low = part.astype(BF16)
+    for k in (1, 2, 3):
+        part = part + lax.ppermute(low, ALL, across(k)).astype(F32)
+    part = part.astype(BF16)
+    mine = layer_swap(jnp.broadcast_to(part[None], (16,) + part.shape))
+    return mine, send(mine, OTHER)
+
+
+def unpack_kernel(place_ref, mine_ref, other_ref, dw_ref, dwo_ref, dwb_ref):
+    dwb_ref[...] = sum(
+        ref[i, 80:96].astype(F32) for ref in (mine_ref, other_ref) for i in range(16)
+    )[0:8]
+
+    def write(low, high):
+        get = lambda ref, b: jnp.concatenate(
+            [ref[i, lo:hi].astype(F32) for i, lo, hi in block_rows(b)], axis=0
+        )
+        for b in range(10):
+            block = get(low, b) if b < 5 else get(high, b - 5)
+            if b < 8:
+                dw_ref[:, b * 128 : (b + 1) * 128] = block
+            else:
+                dwo_ref[:, (b - 8) * 128 : (b - 7) * 128] = block
+
+    @pl.when(place_ref[8] == 0)
+    def _():
+        write(mine_ref, other_ref)
+
+    @pl.when(place_ref[8] != 0)
+    def _():
+        write(other_ref, mine_ref)
+
+
+def block_rows(b):
+    pieces = []
+    row = b * 256
+    while row < (b + 1) * 256:
+        i, lo = divmod(row, 80)
+        hi = min(80, lo + (b + 1) * 256 - row)
+        pieces.append((i, lo, hi))
+        row += hi - lo
+    return pieces
+
+
+def unpack(place, mine, other):
+    fixed = lambda *shape: pl.BlockSpec(shape, lambda g, p: (0,) * len(shape))
+    return pl.pallas_call(
+        unpack_kernel,
+        grid_spec=pltpu.PrefetchScalarGridSpec(
+            num_scalar_prefetch=1,
+            grid=(1,),
+            in_specs=[fixed(16, 96, 128)] * 2,
+            out_specs=[fixed(256, 1024), fixed(256, 256), fixed(8, 128)],
+        ),
+        out_shape=[
+            jax.ShapeDtypeStruct((256, 1024), F32),
+            jax.ShapeDtypeStruct((256, 256), F32),
+            jax.ShapeDtypeStruct((8, 128), F32),
+        ],
+        compiler_params=params(),
+        cost_estimate=cost(1),
+        name="unpack",
+    )(place, mine, other)
 
 
 def local(x, gain, w, shift, wo, pair, pair_gain, wb, up):
@@ -349,22 +490,32 @@
     shift = shift.reshape(1, -1)
     pair_gain = pair_gain.reshape(1, -1)
     wt = wb.T
+    place = chip_order()
+    bias = swap(pair_bias(pair, pair_gain, wt), "res")
     packed, gate, dg = project(x, gain, w, shift, wo, up)
-    bias = pair_bias(pair, pair_gain, wt)
-    bias = gather_bias(swap(bias, "res"))
-    back, d_bias = attention(swap(packed, "res"), bias)
-    d_bias = swap(scatter_bias(d_bias), "res")
+    couple = jnp.stack([bias, send(bias, FAR)])
+    couple, packed = lax.optimization_barrier((couple, packed))
+    heads = swap(packed, "res")
+    own = jnp.concatenate([couple] + [send(couple, along(shift)) for shift in (1, 2, 3)])
+    own, heads = lax.optimization_barrier((own, heads))
+    other = send(own, OTHER)
+    back, d_own, d_other = attention(place, heads, own, other, None, 0, True)
     back = swap(back, "res")
+    both = d_own.astype(F32) + send(d_other, OTHER).astype(F32)
+    low = both.astype(BF16)
+    total = both[0:2]
+    for turn in (1, 2, 3):
+        total = total + send(low[2 * turn : 2 * turn + 2], along(-turn)).astype(F32)
+    keep, away = total[0], total[1].astype(BF16)
+    keep, away, back = lax.optimization_barrier((keep, away, back))
+    d_bias = (keep + send(away, FAR).astype(F32)).astype(BF16)
+    d_bias = swap(d_bias, "res")
     inc, dx, dw = finish(x, gain, w, wo, up, gate, dg, back)
+    part = halve(dw.reshape(2, 16, 80, 128))
+    d_bias, part = lax.optimization_barrier((d_bias, part))
     d_pair, dwb = pair_grad(pair, pair_gain, wt, d_bias)
-    rows = jnp.concatenate(
-        [dw.reshape(2560, 128), dwb.astype(BF16), jnp.zeros((120, 128), BF16)], axis=0
-    ).reshape(128, 21, 128)
-    part = jnp.sum(swap(rows, ("seq", "res")).astype(F32), axis=0).astype(BF16)
-    rows = swap(jnp.broadcast_to(part[None], (128, 21, 128)), ("seq", "res"))
-    rows = rows.reshape(2688, 128).astype(F32)
-    dw = jnp.swapaxes(rows[:2560].reshape(10, 256, 128), 0, 1).reshape(256, 1280)
-    return inc, dx, d_pair, dw[:, :1024], dw[:, 1024:], rows[2560:2568].T
+    dw, dwo, dwb = unpack(place, *sum_layers(part, dwb))
+    return inc, dx, d_pair, dw, dwo, dwb.T
 
 
 def solution(mesh):

time: 216 us -> 169 us (0.78)
  blocking collectives: 97.2 us -> 25.7 us
  starting transfers between devices: 16.3 us -> 38.6 us
  waiting for transfers between devices: 28.5 us -> 40.3 us
  local copies, waits for them, and re-layouts: 14.3 us -> 9.17 us
  other arithmetic: 7.32 us -> 4.74 us
    all_to_all x5 -> x2, blocking collectives: 97.2 us -> 25.7 us  [the longest x1 14.8 us: layer_swap(): lax.all_to_all(x, ALL, split_axis=0, concat_axis=0, tiled=True, axis_inde...]
    ppermute x2 -> x15, waiting for transfers between devices: 2.42 us -> 29.4 us  [the longest x12 27 us: send(): return lax.ppermute(x, 'seq', pairs)]
    ppermute x2 -> x15, starting transfers between devices: 4.82 us -> 21.7 us  [the longest x12 18.4 us: send(): return lax.ppermute(x, 'seq', pairs)]
    all_to_all x3 -> x4, waiting for transfers between devices: 26.1 us -> 11 us  [the longest x3 11 us: swap(): return lax.all_to_all(x, axis, split_axis=0, concat_axis=0, tiled=True)]
    all_to_all x3 -> x4, starting transfers between devices: 11.4 us -> 16.9 us  [the longest x3 12 us: swap(): return lax.all_to_all(x, axis, split_axis=0, concat_axis=0, tiled=True)]
    pallas_call x1, Pallas kernels: 14.4 us -> 10.2 us  [pair_grad(): pl.pallas_call(pair_grad_kernel, grid=(j // step,), in_specs=[pl.BlockSpe...]
    unnamed x44 -> x32, local copies, waits for them, and re-layouts: 11.6 us -> 8.21 us
    another operation x2 -> x1, other arithmetic: 2.88 us -> 0.03 us  [local(): couple = jnp.stack([bias, send(bias, FAR)])]
  transfers between devices with their start and end apart: 5 -> 19, of which waited for: 3 -> 12; matrix products, arithmetic and copies ran while one was open for 3% -> 2% of each run, Pallas kernels for 4% -> 11%
where the time goes in v2:
time: 169 us
  Pallas kernels  49.2 us (29%)
  waiting for transfers between devices  40.3 us (24%)
  starting transfers between devices  38.6 us (23%)
  blocking collectives  25.7 us (15%)
  local copies, waits for them, and re-layouts  9.17 us (5%)
  other arithmetic  4.74 us (3%)
    ppermute x12, waiting for transfers between devices, send(): return lax.ppermute(x, 'seq', pairs)  27 us
    pallas_call x1, Pallas kernels, attention(): pl.pallas_call(kernel, grid_spec=pltpu.PrefetchScalarGridSpec(num_scalar_...  25.4 us
    ppermute x12, starting transfers between devices, send(): return lax.ppermute(x, 'seq', pairs)  18.4 us
    all_to_all x1, blocking collectives, layer_swap(): lax.all_to_all(x, ALL, split_axis=0, concat_axis=0, tiled=True, axis_inde...  14.8 us
    all_to_all x3, starting transfers between devices, swap(): return lax.all_to_all(x, axis, split_axis=0, concat_axis=0, tiled=True)  12 us
    all_to_all x3, waiting for transfers between devices, swap(): return lax.all_to_all(x, axis, split_axis=0, concat_axis=0, tiled=True)  11 us
    all_to_all x1, blocking collectives, swap(): return lax.all_to_all(x, axis, split_axis=0, concat_axis=0, tiled=True)  10.9 us
    pallas_call x1, Pallas kernels, pair_grad(): pl.pallas_call(pair_grad_kernel, grid=(j // step,), in_specs=[pl.BlockSpe...  10.2 us
  transfers between devices with their start and end apart: 19, of which 12 were waited for; matrix products, arithmetic and copies ran while one was open for 2% of the time, Pallas kernels for 11%

profile of v2, /device:TPU:1, one launch (start us, length us, event | category | flops | bytes accessed | tf_op | source)
XLA Modules:
  0.0 168.5 jit_solution(14184174308248308598)
XLA Ops:
  3.6 3.7 %pair_bias.1 = bf16[8,64,128]{2,1,0:T(8,128)(2,1)S(1)} custom-call(bf16[64,128,128]{2,1,0:T(8,128)(2,1)S(1)} %copy-done, f32[1,128]{1,0:T(1,128)S(1)} %bitcast.33, bf16[8,128]{1,0:T(8,128)(2,1)S(1)} %bitcast.28), custom_call_target="tpu_custom_call" | custom-call | flops 4000000000 | bytes 12000000 | tf_op jit(solution)/shard_map/pair_bias/pallas_call | solution.py:104
  7.3 10.9 %all_to_all.30 = bf16[8,64,128]{2,1,0:T(8,128)(2,1)S(1)} all-to-all(bf16[8,64,128]{2,1,0:T(8,128)(2,1)S(1)} %pair_bias.1), channel_id=1, replica_groups=mesh['seq'=16,'res'=8] {'res'}, dimensions={0} | all-to-all | bytes 262144 | tf_op jit(solution)/shard_map/all_to_all | solution.py:363
  18.2 2.6 %collective-permute-start = (bf16[8,64,128]{2,1,0:T(8,128)(2,1)S(1)}, bf16[8,64,128]{2,1,0:T(8,128)(2,1)S(1)}, u32[]{:S(2)}, u32[]{:S(2)}) collective-permute-start(bf16[8,64,128]{2,1,0:T(8,128)(2,1)S(1)} %all_to_all.30), channel_id=1, source_target_pairs={{0,64},{8,72},{16,80},{24,88},{32,96},{40,104},{48,112},{56,120},{... | collective-permute-start | bytes 393224 | tf_op jit(solution)/shard_map/ppermute | solution.py:376
  20.9 3.2 %project.1 = (bf16[8,4,128,128]{3,2,1,0:T(8,128)(2,1)}, f32[4,128,256]{2,1,0:T(8,128)S(1)}, f32[4,128,256]{2,1,0:T(8,128)S(1)}) custom-call(bf16[4,128,256]{2,1,0:T(8,128)(2,1)S(1)} %copy-done.3, f32[1,256]{1,0:T(1,128)S(1)} %bitcast.31, bf16[256,1024]{1,0:T(8,128)(2,1)S(1)} %copy-done.2, f32[1,256]{1,0:T(1,128)S(1)} %bitcast.30, ...), custom_call_target="tpu_custom_call" | custom-call | flops 3000000000 | bytes 9000000 | tf_op jit(solution)/shard_map/project/pallas_call | solution.py:76
  25.7 3.6 %all-to-all-start.1 = ((bf16[8,4,128,128]{3,2,1,0:T(8,128)(2,1)}), bf16[8,4,128,128]{3,2,1,0:T(8,128)(2,1)S(1)}, u32[]{:S(2)}, u32[]{:S(2)}) async-start(bf16[8,4,128,128]{3,2,1,0:T(8,128)(2,1)} %get-tuple-element.33), calls=%async_computation.1 | async-start | bytes 2097152 | tf_op jit(solution)/shard_map/all_to_all | solution.py:363
  29.3 3.8 %collective-permute-start.3 = (bf16[2,8,64,128]{3,2,1,0:T(8,128)(2,1)S(1)}, bf16[2,8,64,128]{3,2,1,0:T(8,128)(2,1)S(1)}, u32[]{:S(2)}, u32[]{:S(2)}) collective-permute-start(bf16[2,8,64,128]{3,2,1,0:T(8,128)(2,1)S(1)} %pad_maximum_fusion.1), channel_id=1, source_target_pairs={{0,48},{8,56},{16,0},{24,8},{32,16},{40,24},{48,32},{56,40},{64,11... | collective-permute-start | bytes 786440 | tf_op jit(solution)/shard_map/ppermute | solution.py:376
  33.8 9.2 %collective-permute-done.3 = bf16[2,8,64,128]{3,2,1,0:T(8,128)(2,1)S(1)} collective-permute-done((bf16[2,8,64,128]{3,2,1,0:T(8,128)(2,1)S(1)}, bf16[2,8,64,128]{3,2,1,0:T(8,128)(2,1)S(1)}, u32[]{:S(2)}, u32[]{:S(2)}) %collective-permute-start.3) | collective-permute-done | bytes 262176 | tf_op jit(solution)/shard_map/ppermute | solution.py:376
  43.0 4.8 %collective-permute-done.1 = bf16[2,8,64,128]{3,2,1,0:T(8,128)(2,1)S(1)} collective-permute-done((bf16[2,8,64,128]{3,2,1,0:T(8,128)(2,1)S(1)}, bf16[2,8,64,128]{3,2,1,0:T(8,128)(2,1)S(1)}, u32[]{:S(2)}, u32[]{:S(2)}) %collective-permute-start.1) | collective-permute-done | bytes 262176 | tf_op jit(solution)/shard_map/ppermute | solution.py:376
  49.0 2.3 %collective-permute-done.4.b = bf16[8,8,64,128]{3,2,1,0:T(8,128)(2,1)} collective-permute-done((bf16[8,8,64,128]{3,2,1,0:T(8,128)(2,1)S(1)}, bf16[8,8,64,128]{3,2,1,0:T(8,128)(2,1)}, u32[]{:S(2)}, u32[]{:S(2)}) %collective-permute-start.4) | collective-permute-done | bytes 1048608 | tf_op jit(solution)/shard_map/ppermute | solution.py:376
  51.3 25.4 %attention.1 = (bf16[8,4,128,128]{3,2,1,0:T(8,128)(2,1)}, bf16[8,8,64,128]{3,2,1,0:T(8,128)(2,1)S(1)}, bf16[8,8,64,128]{3,2,1,0:T(8,128)(2,1)S(1)}) custom-call(s32[9]{0:T(128)S(1)} %stack.48.p.place_ref, bf16[8,4,128,128]{3,2,1,0:T(8,128)(2,1)S(1)} %all-to-all-done.1.x, bf16[8,8,64,128]{3,2,1,0:T(8,128)(2,1)S(1)} %pad_maximum_fusion.a, ...), custom_call_target="tpu_custom_call" | custom-call | flops 24999999488 | bytes 75000000 | tf_op jit(solution)/shard_map/attention/pallas_call | solution.py:218
  77.1 2.3 %collective-permute-done.5 = bf16[8,8,64,128]{3,2,1,0:T(8,128)(2,1)S(1)} collective-permute-done((bf16[8,8,64,128]{3,2,1,0:T(8,128)(2,1)S(1)}, bf16[8,8,64,128]{3,2,1,0:T(8,128)(2,1)S(1)}, u32[]{:S(2)}, u32[]{:S(2)}) %collective-permute-start.5) | collective-permute-done | bytes 1048608 | tf_op jit(solution)/shard_map/ppermute | solution.py:376
  79.4 1.8 %fusion.5 = (bf16[8,8,64,128]{3,2,1,0:T(8,128)(2,1)S(1)}, f32[8,8,64,128]{3,2,1,0:T(8,128)}) fusion(bf16[8,8,64,128]{3,2,1,0:T(8,128)(2,1)S(1)} %collective-permute-done.5, bf16[8,8,64,128]{3,2,1,0:T(8,128)(2,1)S(1)} %get-tuple-element.36), kind=kLoop, calls=%fused_computation.18 | loop fusion | flops 2097152 | bytes 5242880 | tf_op jit(solution)/shard_map/convert_element_type | solution.py:505
  84.7 5.0 %all-to-all-start.2 = ((bf16[8,4,128,128]{3,2,1,0:T(8,128)(2,1)}), bf16[8,4,128,128]{3,2,1,0:T(8,128)(2,1)S(1)}, u32[]{:S(2)}, u32[]{:S(2)}) async-start(bf16[8,4,128,128]{3,2,1,0:T(8,128)(2,1)} %get-tuple-element.38), calls=%async_computation.2 | async-start | bytes 2097152 | tf_op jit(solution)/shard_map/all_to_all | solution.py:363
  89.7 2.1 %collective-permute-done.8 = bf16[2,8,64,128]{3,2,1,0:T(8,128)(2,1)S(1)} collective-permute-done((bf16[2,8,64,128]{3,2,1,0:T(8,128)(2,1)}, bf16[2,8,64,128]{3,2,1,0:T(8,128)(2,1)S(1)}, u32[]{:S(2)}, u32[]{:S(2)}) %collective-permute-start.8) | collective-permute-done | bytes 262176 | tf_op jit(solution)/shard_map/ppermute | solution.py:376
  91.8 4.0 %collective-permute-done.7 = bf16[2,8,64,128]{3,2,1,0:T(8,128)(2,1)S(1)} collective-permute-done((bf16[2,8,64,128]{3,2,1,0:T(8,128)(2,1)S(1)}, bf16[2,8,64,128]{3,2,1,0:T(8,128)(2,1)S(1)}, u32[]{:S(2)}, u32[]{:S(2)}) %collective-permute-start.7) | collective-permute-done | bytes 262176 | tf_op jit(solution)/shard_map/ppermute | solution.py:376
  97.9 6.6 %all-to-all-done.2.back_ref = bf16[8,4,128,128]{3,2,1,0:T(8,128)(2,1)S(1)} async-done(((bf16[8,4,128,128]{3,2,1,0:T(8,128)(2,1)}), bf16[8,4,128,128]{3,2,1,0:T(8,128)(2,1)S(1)}, u32[]{:S(2)}, u32[]{:S(2)}) %all-to-all-start.2) | async-done | bytes 1048608 | tf_op jit(solution)/shard_map/all_to_all | solution.py:363
  107.1 4.9 %finish.1 = (bf16[4,128,256]{2,1,0:T(8,128)(2,1)}, bf16[4,128,256]{2,1,0:T(8,128)(2,1)}, bf16[10,256,128]{2,1,0:T(8,128)(2,1)S(1)}) custom-call(bf16[4,128,256]{2,1,0:T(8,128)(2,1)S(1)} %copy-done.3, f32[1,256]{1,0:T(1,128)S(1)} %bitcast.32, bf16[256,1024]{1,0:T(8,128)(2,1)S(1)} %copy-done.2, bf16[256,256]{1,0:T(8,128)(2,1)S(1)} %copy-done.5, ...), custom_call_target="tpu_custom_call" | custom-call | flops 5000000000 | bytes 15000000 | tf_op jit(solution)/shard_map/finish/pallas_call | solution.py:286
  112.0 2.1 %collective-permute-start.10 = (bf16[16,80,128]{2,1,0:T(8,128)(2,1)S(1)}, bf16[16,80,128]{2,1,0:T(8,128)(2,1)S(1)}, u32[]{:S(2)}, u32[]{:S(2)}) collective-permute-start(bf16[16,80,128]{2,1,0:T(8,128)(2,1)S(1)} %dynamic-slice_bitcast_fusion), channel_id=1, source_target_pairs={{0,8},{8,0},{16,24},{24,16},{32,40},{40,32},{48,56},{56,48},{64,72... | collective-permute-start | bytes 983048 | tf_op jit(solution)/shard_map/ppermute | solution.py:376
  114.8 3.4 %all-to-all-start.3 = ((bf16[8,64,128]{2,1,0:T(8,128)(2,1)}), bf16[8,64,128]{2,1,0:T(8,128)(2,1)S(1)}, u32[]{:S(2)}, u32[]{:S(2)}) async-start(bf16[8,64,128]{2,1,0:T(8,128)(2,1)} %add_convert_fusion), calls=%async_computation.3 | async-start | bytes 262144 | tf_op jit(solution)/shard_map/all_to_all | solution.py:363
  119.0 4.4 %all-to-all-done.3.db_ref = bf16[8,64,128]{2,1,0:T(8,128)(2,1)S(1)} async-done(((bf16[8,64,128]{2,1,0:T(8,128)(2,1)}), bf16[8,64,128]{2,1,0:T(8,128)(2,1)S(1)}, u32[]{:S(2)}, u32[]{:S(2)}) %all-to-all-start.3) | async-done | bytes 131104 | tf_op jit(solution)/shard_map/all_to_all | solution.py:363
  123.4 4.9 %all-to-all-start.4 = ((bf16[16,80,128]{2,1,0:T(8,128)(2,1)}), bf16[16,80,128]{2,1,0:T(8,128)(2,1)S(1)}, u32[]{:S(2)}, u32[]{:S(2)}) async-start(bf16[16,80,128]{2,1,0:T(8,128)(2,1)} %fusion), calls=%async_computation.4 | async-start | bytes 655360 | tf_op jit(solution)/shard_map/all_to_all | solution.py:400
  129.9 10.2 %pair_grad.1 = (bf16[64,128,128]{2,1,0:T(8,128)(2,1)}, f32[8,128]{1,0:T(8,128)S(1)}) custom-call(bf16[64,128,128]{2,1,0:T(8,128)(2,1)S(1)} %copy-done.1, f32[1,128]{1,0:T(1,128)S(1)} %bitcast.34, bf16[8,128]{1,0:T(8,128)(2,1)S(1)} %bitcast.29, bf16[8,64,128]{2,1,0:T(8,128)(2,1)S(1)} %all-to-all-done.3.db_ref), custom_call_target="tpu_custom_call" | custom-call | flops 5000000000 | bytes 15000000 | tf_op jit(solution)/shard_map/pair_grad/pallas_call | solution.py:335
  146.0 14.8 %all_to_all.31.mine_ref = bf16[16,96,128]{2,1,0:T(8,128)(2,1)S(1)} all-to-all(bf16[16,96,128]{2,1,0:T(8,128)(2,1)S(1)} %broadcast_in_dim.2), channel_id=1, replica_groups={{0,2,4,6,16,18,20,22,32,34,36,38,48,50,52,54},{8,10,12,14,24,26,28,30,4..., dimensions={0} | all-to-all | bytes 786432 | tf_op jit(solution)/shard_map/all_to_all | solution.py:400
  160.7 4.7 %collective-permute-start.14 = (bf16[16,96,128]{2,1,0:T(8,128)(2,1)S(1)}, bf16[16,96,128]{2,1,0:T(8,128)(2,1)S(1)}, u32[]{:S(2)}, u32[]{:S(2)}) collective-permute-start(bf16[16,96,128]{2,1,0:T(8,128)(2,1)S(1)} %all_to_all.31.mine_ref), channel_id=1, source_target_pairs={{0,8},{8,0},{16,24},{24,16},{32,40},{40,32},{48,56},{56,48},{64,72... | collective-permute-start | bytes 1179656 | tf_op jit(solution)/shard_map/ppermute | solution.py:376
  (69 shorter events, 27.1 us)
Async XLA Ops:
  3.6 17.3 %copy-start.3 = (bf16[4,128,256]{2,1,0:T(8,128)(2,1)S(1)}, bf16[4,128,256]{2,1,0:T(8,128)(2,1)}, u32[]{:S(2)}) copy-start(bf16[4,128,256]{2,1,0:T(8,128)(2,1)} %x_ref.6) | copy-start | bytes 786436
  3.6 17.3 %copy-start.4 = (bf16[4,128,256]{2,1,0:T(8,128)(2,1)S(1)}, bf16[4,128,256]{2,1,0:T(8,128)(2,1)}, u32[]{:S(2)}) copy-start(bf16[4,128,256]{2,1,0:T(8,128)(2,1)} %up_ref.3) | copy-start | bytes 786436
  3.6 17.3 %copy-start.5 = (bf16[256,256]{1,0:T(8,128)(2,1)S(1)}, bf16[256,256]{1,0:T(8,128)(2,1)}, u32[]{:S(2)}) copy-start(bf16[256,256]{1,0:T(8,128)(2,1)} %wo_ref.3) | copy-start | bytes 393220
  3.6 17.3 %copy-start.8 = (f32[256]{0:T(256)S(1)}, f32[256]{0:T(256)}, u32[]{:S(2)}) copy-start(f32[256]{0:T(256)} %param.12) | copy-start | bytes 3076
  3.6 17.3 %copy-start.9 = (f32[256]{0:T(256)S(1)}, f32[256]{0:T(256)}, u32[]{:S(2)}) copy-start(f32[256]{0:T(256)} %param.10) | copy-start | bytes 3076
  18.2 7.4 %collective-permute-start = (bf16[8,64,128]{2,1,0:T(8,128)(2,1)S(1)}, bf16[8,64,128]{2,1,0:T(8,128)(2,1)S(1)}, u32[]{:S(2)}, u32[]{:S(2)}) collective-permute-start(bf16[8,64,128]{2,1,0:T(8,128)(2,1)S(1)} %all_to_all.30), channel_id=1, source_target_pairs={{0,64},{8,72},{16,80},{24,88},{32,96},{40,104},{48,112},{56,120},{... | collective-permute-start | bytes 393224 | tf_op jit(solution)/shard_map/ppermute | solution.py:376
  25.7 22.2 %all-to-all-start.1 = ((bf16[8,4,128,128]{3,2,1,0:T(8,128)(2,1)}), bf16[8,4,128,128]{3,2,1,0:T(8,128)(2,1)S(1)}, u32[]{:S(2)}, u32[]{:S(2)}) async-start(bf16[8,4,128,128]{3,2,1,0:T(8,128)(2,1)} %get-tuple-element.33), calls=%async_computation.1 | async-start | bytes 2097152 | tf_op jit(solution)/shard_map/all_to_all | solution.py:363
  29.3 13.7 %collective-permute-start.3 = (bf16[2,8,64,128]{3,2,1,0:T(8,128)(2,1)S(1)}, bf16[2,8,64,128]{3,2,1,0:T(8,128)(2,1)S(1)}, u32[]{:S(2)}, u32[]{:S(2)}) collective-permute-start(bf16[2,8,64,128]{3,2,1,0:T(8,128)(2,1)S(1)} %pad_maximum_fusion.1), channel_id=1, source_target_pairs={{0,48},{8,56},{16,0},{24,8},{32,16},{40,24},{48,32},{56,40},{64,11... | collective-permute-start | bytes 786440 | tf_op jit(solution)/shard_map/ppermute | solution.py:376
  33.1 9.9 %collective-permute-start.2 = (bf16[2,8,64,128]{3,2,1,0:T(8,128)(2,1)S(1)}, bf16[2,8,64,128]{3,2,1,0:T(8,128)(2,1)S(1)}, u32[]{:S(2)}, u32[]{:S(2)}) collective-permute-start(bf16[2,8,64,128]{3,2,1,0:T(8,128)(2,1)S(1)} %pad_maximum_fusion.1), channel_id=1, source_target_pairs={{0,32},{8,40},{16,48},{24,56},{32,0},{40,8},{48,16},{56,24},{64,96... | collective-permute-start | bytes 786440 | tf_op jit(solution)/shard_map/ppermute | solution.py:376
  33.1 14.7 %collective-permute-start.1 = (bf16[2,8,64,128]{3,2,1,0:T(8,128)(2,1)S(1)}, bf16[2,8,64,128]{3,2,1,0:T(8,128)(2,1)S(1)}, u32[]{:S(2)}, u32[]{:S(2)}) collective-permute-start(bf16[2,8,64,128]{3,2,1,0:T(8,128)(2,1)S(1)} %pad_maximum_fusion.1), channel_id=1, source_target_pairs={{0,16},{8,24},{16,32},{24,40},{32,48},{40,56},{48,0},{56,8},{64,80... | collective-permute-start | bytes 786440 | tf_op jit(solution)/shard_map/ppermute | solution.py:376
  48.0 3.3 %collective-permute-start.4 = (bf16[8,8,64,128]{3,2,1,0:T(8,128)(2,1)S(1)}, bf16[8,8,64,128]{3,2,1,0:T(8,128)(2,1)}, u32[]{:S(2)}, u32[]{:S(2)}) collective-permute-start(bf16[8,8,64,128]{3,2,1,0:T(8,128)(2,1)S(1)} %pad_maximum_fusion.a), channel_id=1, source_target_pairs={{0,8},{8,0},{16,24},{24,16},{32,40},{40,32},{48,56},{56,48},{64,72... | collective-permute-start | bytes 3145736 | tf_op jit(solution)/shard_map/ppermute | solution.py:376
  76.8 2.7 %collective-permute-start.5 = (bf16[8,8,64,128]{3,2,1,0:T(8,128)(2,1)S(1)}, bf16[8,8,64,128]{3,2,1,0:T(8,128)(2,1)S(1)}, u32[]{:S(2)}, u32[]{:S(2)}) collective-permute-start(bf16[8,8,64,128]{3,2,1,0:T(8,128)(2,1)S(1)} %get-tuple-element.37), channel_id=1, source_target_pairs={{0,8},{8,0},{16,24},{24,16},{32,40},{40,32},{48,56},{56,48},{64,72... | collective-permute-start | bytes 3145736 | tf_op jit(solution)/shard_map/ppermute | solution.py:376
  82.0 9.8 %collective-permute-start.8 = (bf16[2,8,64,128]{3,2,1,0:T(8,128)(2,1)}, bf16[2,8,64,128]{3,2,1,0:T(8,128)(2,1)S(1)}, u32[]{:S(2)}, u32[]{:S(2)}) collective-permute-start(bf16[2,8,64,128]{3,2,1,0:T(8,128)(2,1)} %get-tuple-element.55), channel_id=1, source_target_pairs={{0,16},{8,24},{16,32},{24,40},{32,48},{40,56},{48,0},{56,8},{64,80... | collective-permute-start | bytes 786440 | tf_op jit(solution)/shard_map/ppermute | solution.py:376
  82.0 13.7 %collective-permute-start.7 = (bf16[2,8,64,128]{3,2,1,0:T(8,128)(2,1)S(1)}, bf16[2,8,64,128]{3,2,1,0:T(8,128)(2,1)S(1)}, u32[]{:S(2)}, u32[]{:S(2)}) collective-permute-start(bf16[2,8,64,128]{3,2,1,0:T(8,128)(2,1)S(1)} %get-tuple-element.56), channel_id=1, source_target_pairs={{0,32},{8,40},{16,48},{24,56},{32,0},{40,8},{48,16},{56,24},{64,96... | collective-permute-start | bytes 786440 | tf_op jit(solution)/shard_map/ppermute | solution.py:376
  83.8 12.9 %collective-permute-start.6 = (bf16[2,8,64,128]{3,2,1,0:T(8,128)(2,1)S(1)}, bf16[2,8,64,128]{3,2,1,0:T(8,128)(2,1)S(1)}, u32[]{:S(2)}, u32[]{:S(2)}) collective-permute-start(bf16[2,8,64,128]{3,2,1,0:T(8,128)(2,1)S(1)} %get-tuple-element.54), channel_id=1, source_target_pairs={{0,48},{8,56},{16,0},{24,8},{32,16},{40,24},{48,32},{56,40},{64,11... | collective-permute-start | bytes 786440 | tf_op jit(solution)/shard_map/ppermute | solution.py:376
  84.7 19.8 %all-to-all-start.2 = ((bf16[8,4,128,128]{3,2,1,0:T(8,128)(2,1)}), bf16[8,4,128,128]{3,2,1,0:T(8,128)(2,1)S(1)}, u32[]{:S(2)}, u32[]{:S(2)}) async-start(bf16[8,4,128,128]{3,2,1,0:T(8,128)(2,1)} %get-tuple-element.38), calls=%async_computation.2 | async-start | bytes 2097152 | tf_op jit(solution)/shard_map/all_to_all | solution.py:363
  104.5 9.6 %collective-permute-start.9 = (bf16[8,64,128]{2,1,0:T(8,128)(2,1)S(1)}, bf16[8,64,128]{2,1,0:T(8,128)(2,1)S(1)}, u32[]{:S(2)}, u32[]{:S(2)}) collective-permute-start(bf16[8,64,128]{2,1,0:T(8,128)(2,1)S(1)} %fusion.3), channel_id=1, source_target_pairs={{0,64},{8,72},{16,80},{24,88},{32,96},{40,104},{48,112},{56,120},{... | collective-permute-start | bytes 393224 | tf_op jit(solution)/shard_map/ppermute | solution.py:376
  112.0 6.2 %collective-permute-start.10 = (bf16[16,80,128]{2,1,0:T(8,128)(2,1)S(1)}, bf16[16,80,128]{2,1,0:T(8,128)(2,1)S(1)}, u32[]{:S(2)}, u32[]{:S(2)}) collective-permute-start(bf16[16,80,128]{2,1,0:T(8,128)(2,1)S(1)} %dynamic-slice_bitcast_fusion), channel_id=1, source_target_pairs={{0,8},{8,0},{16,24},{24,16},{32,40},{40,32},{48,56},{56,48},{64,72... | collective-permute-start | bytes 983048 | tf_op jit(solution)/shard_map/ppermute | solution.py:376
  114.8 8.6 %all-to-all-start.3 = ((bf16[8,64,128]{2,1,0:T(8,128)(2,1)}), bf16[8,64,128]{2,1,0:T(8,128)(2,1)S(1)}, u32[]{:S(2)}, u32[]{:S(2)}) async-start(bf16[8,64,128]{2,1,0:T(8,128)(2,1)} %add_convert_fusion), calls=%async_computation.3 | async-start | bytes 262144 | tf_op jit(solution)/shard_map/all_to_all | solution.py:363
  123.4 16.7 %all-to-all-start.4 = ((bf16[16,80,128]{2,1,0:T(8,128)(2,1)}), bf16[16,80,128]{2,1,0:T(8,128)(2,1)S(1)}, u32[]{:S(2)}, u32[]{:S(2)}) async-start(bf16[16,80,128]{2,1,0:T(8,128)(2,1)} %fusion), calls=%async_computation.4 | async-start | bytes 655360 | tf_op jit(solution)/shard_map/all_to_all | solution.py:400
  140.2 4.0 %collective-permute-start.13 = (bf16[96,128]{1,0:T(8,128)(2,1)S(1)}, bf16[96,128]{1,0:T(8,128)(2,1)S(1)}, u32[]{:S(2)}, u32[]{:S(2)}) collective-permute-start(bf16[96,128]{1,0:T(8,128)(2,1)S(1)} %fusion.4), channel_id=1, source_target_pairs={{0,65},{1,64},{2,67},{3,66},{4,69},{5,68},{6,71},{7,70},{8,73},{9,... | collective-permute-start | bytes 73736 | tf_op jit(solution)/shard_map/ppermute | solution.py:425
  141.7 4.2 %collective-permute-start.12 = (bf16[96,128]{1,0:T(8,128)(2,1)S(1)}, bf16[96,128]{1,0:T(8,128)(2,1)S(1)}, u32[]{:S(2)}, u32[]{:S(2)}) collective-permute-start(bf16[96,128]{1,0:T(8,128)(2,1)S(1)} %fusion.4), channel_id=1, source_target_pairs={{0,64},{1,65},{2,66},{3,67},{4,68},{5,69},{6,70},{7,71},{8,72},{9,... | collective-permute-start | bytes 73736 | tf_op jit(solution)/shard_map/ppermute | solution.py:425
  142.8 3.1 %collective-permute-start.11 = (bf16[96,128]{1,0:T(8,128)(2,1)S(1)}, bf16[96,128]{1,0:T(8,128)(2,1)S(1)}, u32[]{:S(2)}, u32[]{:S(2)}) collective-permute-start(bf16[96,128]{1,0:T(8,128)(2,1)S(1)} %fusion.4), channel_id=1, source_target_pairs={{0,1},{1,0},{2,3},{3,2},{4,5},{5,4},{6,7},{7,6},{8,9},{9,8},{10,11... | collective-permute-start | bytes 73736 | tf_op jit(solution)/shard_map/ppermute | solution.py:425
  160.7 6.0 %collective-permute-start.14 = (bf16[16,96,128]{2,1,0:T(8,128)(2,1)S(1)}, bf16[16,96,128]{2,1,0:T(8,128)(2,1)S(1)}, u32[]{:S(2)}, u32[]{:S(2)}) collective-permute-start(bf16[16,96,128]{2,1,0:T(8,128)(2,1)S(1)} %all_to_all.31.mine_ref), channel_id=1, source_target_pairs={{0,8},{8,0},{16,24},{24,16},{32,40},{40,32},{48,56},{56,48},{64,72... | collective-permute-start | bytes 1179656 | tf_op jit(solution)/shard_map/ppermute | solution.py:376
  (11 other events, 58.2 us)

commit v3 on v2

v3 whole, which is shorter than its diff:
```python
import functools

import jax
import jax.numpy as jnp
from jax import lax
from jax.experimental import pallas as pl
from jax.experimental.pallas import tpu as pltpu
from jax.sharding import PartitionSpec as P

EPS = 1e-05
F32 = jnp.float32
BF16 = jnp.bfloat16
HEADS = 8
DH = 32
SCALE = DH ** (-0.5)


def nn(a, b):
    return lax.dot_general(a, b, (((1,), (0,)), ((), ())), preferred_element_type=F32)


def nt(a, b):
    return lax.dot_general(a, b, (((1,), (1,)), ((), ())), preferred_element_type=F32)


def tn(a, b):
    return lax.dot_general(a, b, (((0,), (0,)), ((), ())), preferred_element_type=F32)


def normalize(x):
    x = x.astype(F32)
    centered = x - jnp.mean(x, axis=-1, keepdims=True)
    inv = lax.rsqrt(jnp.mean(centered * centered, axis=-1, keepdims=True) + EPS)
    return centered * inv, inv


def normalize_grad(hat, inv, gain, grad):
    g = grad * gain
    mean_g = jnp.mean(g, axis=-1, keepdims=True)
    mean_gx = jnp.mean(g * hat, axis=-1, keepdims=True)
    return inv * (g - mean_g - hat * mean_gx)


def split(x):
    high = x.astype(BF16)
    return jnp.concatenate([high, (x - high.astype(F32)).astype(BF16)], axis=1)


def row_mean(x, ones):
    return nn(split(x), ones)


def normalize_pairs(x, ones):
    centered = x.astype(F32) - nn(x, ones[:128])
    inv = lax.rsqrt(row_mean(centered * centered, ones) + EPS)
    return centered * inv, inv


def cost(us):
    return pl.CostEstimate(flops=int(us * 1e9), bytes_accessed=int(us * 3e6), transcendentals=0)


def params(megabytes=60):
    return pltpu.CompilerParams(
        dimension_semantics=("arbitrary",), vmem_limit_bytes=megabytes * 1024 * 1024
    )


def project_kernel(x_ref, gain_ref, w_ref, shift_ref, wo_ref, up_ref, pack_ref, gate_ref, dg_ref):
    seqs, rows, width = x_ref.shape
    flat = lambda ref: ref[...].reshape(seqs * rows, width)
    hat, _ = normalize(flat(x_ref))
    normed = (hat * gain_ref[...]).astype(BF16)
    proj = nn(normed, w_ref[...])
    q = (proj[:, :256] * SCALE).astype(BF16)
    k = proj[:, 256:512].astype(BF16)
    v = proj[:, 512:768].astype(BF16)
    gate = jax.nn.sigmoid(proj[:, 768:] + shift_ref[...])
    d_gated = nt(flat(up_ref), wo_ref[...])
    da = (d_gated * gate).astype(BF16)
    gate_ref[...] = gate.reshape(seqs, rows, width)
    dg_ref[...] = d_gated.reshape(seqs, rows, width)
    for h in range(HEADS):
        c = slice(h * DH, (h + 1) * DH)
        packed = jnp.concatenate([q[:, c], k[:, c], v[:, c], da[:, c]], axis=1)
        pack_ref[h] = packed.reshape(seqs, rows, 128)


def project(x, gain, w, shift, wo, up):
    s, n, c = x.shape
    whole = lambda *shape: pl.BlockSpec(shape, lambda i: (0,) * len(shape))
    row = pl.BlockSpec((2, n, c), lambda i: (i, 0, 0))
    return pl.pallas_call(
        project_kernel,
        grid=(s // 2,),
        in_specs=[row, whole(1, c), whole(c, 4 * c), whole(1, c), whole(c, c), row],
        out_specs=[pl.BlockSpec((HEADS, 2, n, 128), lambda i: (0, i, 0, 0)), row, row],
        out_shape=[
            jax.ShapeDtypeStruct((HEADS, s, n, 128), BF16),
            jax.ShapeDtypeStruct((s, n, c), F32),
            jax.ShapeDtypeStruct((s, n, c), F32),
        ],
        compiler_params=params(),
        cost_estimate=cost(3),
        name="project",
    )(x, gain, w, shift, wo, up)


def bias_kernel(x_ref, gain_ref, wt_ref, out_ref, normed_ref, tmp):
    ones = jnp.full((256, 128), 1 / 128, BF16)
    rows = x_ref.shape[0]
    hat, _ = normalize_pairs(x_ref[...].reshape(rows * 128, 128), ones)
    normed = (hat * gain_ref[...]).astype(BF16).reshape(rows, 128, 128)
    normed_ref[...] = normed
    flat = nt(wt_ref[...], normed.reshape(rows * 128, 128))
    for j in range(rows):
        tmp[:, j, :] = flat[:, j * 128 : (j + 1) * 128]
    low = tmp[...].astype(BF16)
    out_ref[0] = low
    out_ref[1] = low


def pair_bias(pair, gain, wt):
    j, i, c = pair.shape
    step = 32
    return pl.pallas_call(
        bias_kernel,
        grid=(j // step,),
        in_specs=[
            pl.BlockSpec((step, i, c), lambda g: (g, 0, 0)),
            pl.BlockSpec((1, c), lambda g: (0, 0)),
            pl.BlockSpec((HEADS, c), lambda g: (0, 0)),
        ],
        out_specs=[
            pl.BlockSpec((2, HEADS, step, i), lambda g: (0, 0, g, 0)),
            pl.BlockSpec((step, i, c), lambda g: (g, 0, 0)),
        ],
        out_shape=[
            jax.ShapeDtypeStruct((2, HEADS, j, i), BF16),
            jax.ShapeDtypeStruct((j, i, c), BF16),
        ],
        scratch_shapes=[pltpu.VMEM((HEADS, step, i), F32)],
        compiler_params=params(),
        cost_estimate=cost(4),
        name="pair_bias",
    )(pair, gain, wt)


def attention_kernel(
    place_ref, x_ref, own_ref, other_ref, o_ref, down_ref, dother_ref,
    xr, xt, acc, qd, scores, ed, total,
):
    step = pl.program_id(0)
    n_seq = x_ref.shape[1]
    iw = 256
    core = place_ref[8]
    mine = pl.ds(pl.multiple_of(core * 64, 64), 64)
    others = pl.ds(pl.multiple_of((1 - core) * 64, 64), 64)
    zeros = lambda rows: jnp.zeros((rows, iw), BF16)

    @pl.when(step == 0)
    def _():
        for s in range(n_seq):
            for c in range(8):
                chip = place_ref[c]
                xr[c, s, 0:64] = x_ref[chip, s, mine]
                xr[c, s, 64:128] = x_ref[chip, s, others]
                xt[s, :, c * 128 : (c + 1) * 128] = xr[c, s].T
        acc[...] = jnp.zeros_like(acc)

    ones = jnp.ones((16, 1024), BF16)
    block = 2 * step

    def score(s):
        xq = jnp.concatenate([x_ref[block, s].T, x_ref[block + 1, s].T], axis=1)
        rhs_q = jnp.concatenate([zeros(32), xq[0:32], zeros(64)], axis=0)
        top = jnp.full((8, iw), -jnp.inf, F32)
        k = 8
        for d in range(0, 8, k):
            big = nn(xr[d : d + k, s].reshape(k * 128, 128), rhs_q)
            for c in range(d, d + k):
                lo = jnp.concatenate([own_ref[c, 0], other_ref[c, 0]], axis=0)
                hi = jnp.concatenate([own_ref[c, 1], other_ref[c, 1]], axis=0)
                sc = big[(c - d) * 128 : (c - d + 1) * 128]
                sc = sc + jnp.concatenate([lo, hi], axis=1).astype(F32)
                scores[s % 2, c] = sc
                top = jnp.maximum(top, jnp.max(sc.reshape(16, 8, iw), axis=0))
                yield
        return xq, rhs_q, jnp.max(top, axis=0, keepdims=True)

    def weigh(s, xq, top):
        for c in range(8):
            ed[s % 2, c, :, :iw] = jnp.exp(scores[s % 2, c] - top).astype(BF16)
            yield
        left = jnp.concatenate([xt[s, 64:96, :], ones], axis=0)
        ot = nn(left, ed[s % 2, :, :, :iw].reshape(1024, iw))
        inv = 1.0 / ot[32:33]
        ot = ot[0:32] * inv
        da = (xq[96:128].astype(F32) * inv).astype(BF16)
        delta = jnp.sum(da.astype(F32) * ot, axis=0, keepdims=True)
        rhs_a = jnp.concatenate([zeros(64), da, zeros(32)], axis=0)
        return ot, rhs_a, delta

    def back(s, rhs_q, rhs_a, delta, ot):
        k = 8
        for c in range(8):
            if c % k == 0:
                big = nn(xr[c : c + k, s].reshape(k * 128, 128), rhs_a)
            e = ed[s % 2, c, :, :iw]
            ds = e.astype(F32) * (big[c % k * 128 : (c % k + 1) * 128] - delta)
            low = ds.astype(BF16)
            ed[s % 2, c, :, iw:] = low
            if s == 0:
                total[c] = ds
            elif s < n_seq - 1:
                total[c] += ds
            else:
                low = (total[c] + ds).astype(BF16)
                for t in range(2):
                    down_ref[c, t] = low[:64, t * 128 : (t + 1) * 128]
                    dother_ref[c, t] = low[64:, t * 128 : (t + 1) * 128]
            if (c + 1) % 8 == 0:
                w = slice(c + 1 - 8, c + 1)
                both = jnp.concatenate([rhs_a, rhs_q], axis=1)
                more = nt(ed[s % 2, w].reshape(8 * 128, 2 * iw), both)
                acc[s, w] += more.reshape(8, 128, 128)
            yield
        dq = nn(xt[s, 32:64, :], ed[s % 2, :, :, iw:].reshape(1024, iw)) * SCALE
        both = jnp.concatenate([ot, jnp.zeros((64, iw), F32), dq], axis=0)
        for t in range(2):
            qd[s, block + t] = both[:, t * 128 : (t + 1) * 128].T

    state = {}

    def drive(gens):
        live = list(gens)
        while live:
            for item in list(live):
                key, gen = item
                try:
                    next(gen)
                except StopIteration as stop:
                    state[key] = stop.value
                    live.remove(item)

    for t in range(n_seq + 2):
        gens = []
        if 0 <= t - 2 < n_seq:
            s = t - 2
            xq, rhs_q, top = state["s", s]
            ot, rhs_a, delta = state["w", s]
            late = (("b", s), back(s, rhs_q, rhs_a, delta, ot))
        if 0 <= t - 1 < n_seq:
            s = t - 1
            xq, rhs_q, top = state["s", s]
            gens.append((("w", s), weigh(s, xq, top)))
        if t < n_seq:
            gens.append((("s", t), score(t)))
        if t >= 2:
            gens.append(late)
        drive(gens)

    @pl.when(step == pl.num_programs(0) - 1)
    def _():
        for s in range(n_seq):
            for c in range(8):
                chip = place_ref[c]
                o_ref[chip, s, mine] = (acc[s, c, 0:64] + qd[s, chip, mine]).astype(BF16)
                o_ref[chip, s, others] = (acc[s, c, 64:128] + qd[s, chip, others]).astype(BF16)


def attention(place, x, own, other):
    r, s, n, _ = x.shape
    half = pl.BlockSpec((8, 2, 64, 128), lambda g, p: (0, g, 0, 0))
    whole = pl.BlockSpec((r, s, n, 128), lambda g, p: (0, 0, 0, 0))
    return pl.pallas_call(
        attention_kernel,
        grid_spec=pltpu.PrefetchScalarGridSpec(
            num_scalar_prefetch=1,
            grid=(4,),
            in_specs=[whole, half, half],
            out_specs=[whole, half, half],
            scratch_shapes=[
                pltpu.VMEM((r, s, n, 128), BF16),
                pltpu.VMEM((s, 128, 1024), BF16),
                pltpu.VMEM((s, 8, 128, 128), F32),
                pltpu.VMEM((s, 8, 128, 128), F32),
                pltpu.VMEM((2, 8, 128, 256), F32),
                pltpu.VMEM((2, 8, 128, 512), BF16),
                pltpu.VMEM((8, 128, 256), F32),
            ],
        ),
        out_shape=[
            jax.ShapeDtypeStruct((r, s, n, 128), BF16),
            jax.ShapeDtypeStruct((8, r, 64, 128), BF16),
            jax.ShapeDtypeStruct((8, r, 64, 128), BF16),
        ],
        compiler_params=params(),
        cost_estimate=cost(18),
        name="attention",
    )(place, x, own, other)


def finish_kernel(
    place_ref, x_ref, gain_ref, w_ref, wo_ref, up_ref, gate_ref, dg_ref, back_ref,
    inc_ref, dx_ref, keep_ref, away_ref, acc,
):
    step = pl.program_id(0)
    seqs, rows, width = x_ref.shape
    flat = lambda ref: ref[...].reshape(seqs * rows, width)
    hat, inv = normalize(flat(x_ref))
    gain = gain_ref[...]
    normed = (hat * gain).astype(BF16)
    gate = flat(gate_ref)
    d_gated = flat(dg_ref)
    up = flat(up_ref)
    back = [back_ref[h].reshape(seqs * rows, 128) for h in range(HEADS)]
    pick = lambda a: jnp.concatenate([b[:, a * DH : (a + 1) * DH] for b in back], axis=1)
    attended = pick(0).astype(F32)
    gated = (gate * attended).astype(BF16)
    inc_ref[...] = nn(gated, wo_ref[...]).astype(BF16).reshape(seqs, rows, width)
    d_pre = (d_gated * attended * gate * (1.0 - gate)).astype(BF16)
    d_proj = jnp.concatenate([pick(3), pick(1), pick(2), d_pre], axis=1)
    grad = nt(d_proj, w_ref[...])
    grad = normalize_grad(hat, inv, gain, grad).astype(BF16)
    dx_ref[...] = grad.reshape(seqs, rows, width)

    @pl.when(step == 0)
    def _():
        acc[...] = jnp.zeros_like(acc)

    acc[:, :1024] += tn(normed, d_proj)
    acc[:, 1024:] += tn(gated, up)

    last = step == pl.num_programs(0) - 1
    core = place_ref[8]

    def write(low_ref, high_ref):
        for b in range(5):
            low_ref[b] = acc[:, b * 128 : (b + 1) * 128].astype(BF16)
            high_ref[b] = acc[:, (b + 5) * 128 : (b + 6) * 128].astype(BF16)

    @pl.when(jnp.logical_and(last, core == 0))
    def _():
        write(keep_ref, away_ref)

    @pl.when(jnp.logical_and(last, core != 0))
    def _():
        write(away_ref, keep_ref)


def finish(place, x, gain, w, wo, up, gate, dg, back):
    s, n, c = x.shape
    whole = lambda *shape: pl.BlockSpec(shape, lambda i, p: (0,) * len(shape))
    row = pl.BlockSpec((2, n, c), lambda i, p: (i, 0, 0))
    return pl.pallas_call(
        finish_kernel,
        grid_spec=pltpu.PrefetchScalarGridSpec(
            num_scalar_prefetch=1,
            grid=(s // 2,),
            in_specs=[
                row, whole(1, c), whole(c, 4 * c), whole(c, c), row, row, row,
                pl.BlockSpec((HEADS, 2, n, 128), lambda i, p: (0, i, 0, 0)),
            ],
            out_specs=[row, row, whole(5, 256, 128), whole(5, 256, 128)],
            scratch_shapes=[pltpu.VMEM((c, 5 * c), F32)],
        ),
        out_shape=[
            jax.ShapeDtypeStruct((s, n, c), BF16),
            jax.ShapeDtypeStruct((s, n, c), BF16),
            jax.ShapeDtypeStruct((5, 256, 128), BF16),
            jax.ShapeDtypeStruct((5, 256, 128), BF16),
        ],
        compiler_params=params(),
        cost_estimate=cost(5),
        name="finish",
    )(place, x, gain, w, wo, up, gate, dg, back)


def pair_weight_kernel(n_ref, db_ref, dw_ref, tmp):
    tmp[...] = db_ref[0].astype(F32) + db_ref[1].astype(F32)
    total = jnp.zeros((HEADS, 128), F32)
    for j in range(n_ref.shape[0]):
        total = total + nn(tmp[:, j, :].astype(BF16), n_ref[j])

    @pl.when(pl.program_id(0) == 0)
    def _():
        dw_ref[...] = total

    @pl.when(pl.program_id(0) > 0)
    def _():
        dw_ref[...] += total


def pair_weight(normed, db):
    j, i, c = normed.shape
    step = 32
    return pl.pallas_call(
        pair_weight_kernel,
        grid=(j // step,),
        in_specs=[
            pl.BlockSpec((step, i, c), lambda g: (g, 0, 0)),
            pl.BlockSpec((2, HEADS, step, i), lambda g: (0, 0, g, 0)),
        ],
        out_specs=pl.BlockSpec((HEADS, c), lambda g: (0, 0)),
        out_shape=jax.ShapeDtypeStruct((HEADS, c), F32),
        scratch_shapes=[pltpu.VMEM((HEADS, step, i), F32)],
        compiler_params=params(),
        cost_estimate=cost(2),
        name="pair_weight",
    )(normed, db)


def pair_grad_kernel(x_ref, gain_ref, wt_ref, db_ref, dx_ref, spread):
    step = pl.program_id(0)
    gain = gain_ref[...]
    rows = x_ref.shape[0]
    ones = jnp.full((256, 128), 1 / 128, BF16)

    @pl.when(step == 0)
    def _():
        place = lax.broadcasted_iota(jnp.int32, (HEADS, rows, 128), 1)
        weight = wt_ref[...].astype(F32) * gain
        mean = jnp.broadcast_to(jnp.mean(weight, axis=1, keepdims=True), (HEADS, 128))
        parts = []
        for value in (weight, mean):
            high = value.astype(BF16).astype(F32)
            parts.append((high, value - high))
        for j in range(rows):
            for t in range(2):
                for k in range(2):
                    wide = jnp.broadcast_to(parts[t][k][:, None, :], (HEADS, rows, 128))
                    block = jnp.where(place == j, wide, 0.0).reshape(HEADS * rows, 128)
                    spread[j, k * 128 : (k + 1) * 128, t * 128 : (t + 1) * 128] = block.astype(
                        BF16
                    )

    db = db_ref[0].astype(F32) + db_ref[1].astype(F32)
    turned = db.reshape(HEADS * rows, 128).T.astype(BF16)
    turned = jnp.concatenate([turned, turned], axis=1)
    hat, inv = normalize_pairs(x_ref[...].reshape(rows * 128, 128), ones)
    both = [nn(turned, spread[j]) for j in range(rows)]
    grad = jnp.concatenate([b[:, :128] for b in both], axis=0)
    mean = jnp.concatenate([b[:, 128:] for b in both], axis=0)
    out = inv * (grad - mean - hat * row_mean(grad * hat, ones))
    dx_ref[...] = out.astype(BF16).reshape(rows, 128, 128)


def pair_grad(pair, gain, wt, db):
    j, i, c = pair.shape
    step = 16
    return pl.pallas_call(
        pair_grad_kernel,
        grid=(j // step,),
        in_specs=[
            pl.BlockSpec((step, i, c), lambda g: (g, 0, 0)),
            pl.BlockSpec((1, c), lambda g: (0, 0)),
            pl.BlockSpec((HEADS, c), lambda g: (0, 0)),
            pl.BlockSpec((2, HEADS, step, i), lambda g: (0, 0, g, 0)),
        ],
        out_specs=pl.BlockSpec((step, i, c), lambda g: (g, 0, 0)),
        out_shape=jax.ShapeDtypeStruct((j, i, c), BF16),
        scratch_shapes=[pltpu.VMEM((step, 2 * HEADS * step, 256), BF16)],
        compiler_params=params(),
        cost_estimate=cost(8),
        name="pair_grad",
    )(pair, gain, wt, db)


def swap(x, axis):
    return lax.all_to_all(x, axis, split_axis=0, concat_axis=0, tiled=True)


OTHER = [(i, i ^ 1) for i in range(16)]


def along(shift):
    move = lambda i: (i & 9) | (((((i >> 1) & 3) + shift) % 4) << 1)
    return [(i, move(i)) for i in range(16)]


def send(x, pairs):
    return lax.ppermute(x, "seq", pairs)


def chip_order():
    me = lax.axis_index("seq")
    z, core = (me >> 1) & 3, me & 1
    chips = [d * 4 + ((z - shift) & 3) for shift in range(4) for d in range(2)]
    return jnp.stack(chips + [core]).astype(jnp.int32)


def device(far, low, z, x, core):
    return (far * 8 + z * 2 + core) * 8 + x * 2 + low


LAYERS = [
    [device(far, low, z, x, core) for z in range(4) for x in range(4)]
    for far in range(2)
    for low in range(2)
    for core in range(2)
]
ALL = ("seq", "res")


COLUMNS = [
    [(far * 8 + line) * 8 + res for far in range(2) for res in range(8)] for line in range(8)
]


def group_swap(x, groups):
    return lax.all_to_all(
        x, ALL, split_axis=0, concat_axis=0, tiled=True, axis_index_groups=groups
    )


def across(k):
    pairs = []
    for i in range(128):
        seq, res = divmod(i, 8)
        pairs.append((i, (seq ^ ((k >> 1) * 8)) * 8 + (res ^ (k & 1))))
    return pairs


def sum_layers(part, extra):
    part = jnp.sum(group_swap(part, LAYERS).astype(F32), axis=0)
    part = jnp.concatenate([part, jnp.pad(extra, ((0, 8), (0, 0)))])
    low = part.astype(BF16)
    for k in (1, 2, 3):
        part = part + lax.ppermute(low, ALL, across(k)).astype(F32)
    part = part.astype(BF16)
    return group_swap(jnp.broadcast_to(part[None], (16,) + part.shape), LAYERS)


def unpack_kernel(place_ref, mine_ref, other_ref, dw_ref, dwo_ref, dwb_ref):
    dwb_ref[...] = sum(
        ref[i, 80:96].astype(F32) for ref in (mine_ref, other_ref) for i in range(16)
    )[0:8]

    def write(low, high):
        get = lambda ref, b: jnp.concatenate(
            [ref[i, lo:hi].astype(F32) for i, lo, hi in block_rows(b)], axis=0
        )
        for b in range(10):
            block = get(low, b) if b < 5 else get(high, b - 5)
            if b < 8:
                dw_ref[:, b * 128 : (b + 1) * 128] = block
            else:
                dwo_ref[:, (b - 8) * 128 : (b - 7) * 128] = block

    @pl.when(place_ref[8] == 0)
    def _():
        write(mine_ref, other_ref)

    @pl.when(place_ref[8] != 0)
    def _():
        write(other_ref, mine_ref)


def block_rows(b):
    pieces = []
    row = b * 256
    while row < (b + 1) * 256:
        i, lo = divmod(row, 80)
        hi = min(80, lo + (b + 1) * 256 - row)
        pieces.append((i, lo, hi))
        row += hi - lo
    return pieces


def unpack(place, mine, other):
    fixed = lambda *shape: pl.BlockSpec(shape, lambda g, p: (0,) * len(shape))
    return pl.pallas_call(
        unpack_kernel,
        grid_spec=pltpu.PrefetchScalarGridSpec(
            num_scalar_prefetch=1,
            grid=(1,),
            in_specs=[fixed(16, 96, 128)] * 2,
            out_specs=[fixed(256, 1024), fixed(256, 256), fixed(8, 128)],
        ),
        out_shape=[
            jax.ShapeDtypeStruct((256, 1024), F32),
            jax.ShapeDtypeStruct((256, 256), F32),
            jax.ShapeDtypeStruct((8, 128), F32),
        ],
        compiler_params=params(16),
        cost_estimate=cost(1),
        name="unpack",
    )(place, mine, other)


def local(x, gain, w, shift, wo, pair, pair_gain, wb, up):
    gain = gain.reshape(1, -1)
    shift = shift.reshape(1, -1)
    pair_gain = pair_gain.reshape(1, -1)
    wt = wb.T
    place = chip_order()
    bias, normed = pair_bias(pair, pair_gain, wt)
    couple = group_swap(bias.reshape(16, 64, 128), COLUMNS).reshape(2, 8, 64, 128)
    packed, gate, dg = project(x, gain, w, shift, wo, up)
    couple, packed = lax.optimization_barrier((couple, packed))
    heads = swap(packed, "res")
    own = jnp.concatenate([couple] + [send(couple, along(turn)) for turn in (1, 2, 3)])
    own, heads = lax.optimization_barrier((own, heads))
    other = send(own, OTHER)
    back, d_own, d_other = attention(place, heads, own, other)
    back = swap(back, "res")
    low = (d_own.astype(F32) + send(d_other, OTHER).astype(F32)).astype(BF16)
    total = low[0:2].astype(F32)
    for turn in (1, 2, 3):
        total = total + send(low[2 * turn : 2 * turn + 2], along(-turn)).astype(F32)
    d_bias = group_swap(total.astype(BF16).reshape(16, 64, 128), COLUMNS).reshape(2, 8, 64, 128)
    inc, dx, keep, away = finish(place, x, gain, w, wo, up, gate, dg, back)
    d_bias, away = lax.optimization_barrier((d_bias, away))
    part = (keep.astype(F32) + send(away, OTHER).astype(F32)).astype(BF16)
    part = part.reshape(16, 80, 128)
    dwb = pair_weight(normed, d_bias)
    mine = sum_layers(part, dwb)
    d_pair = pair_grad(pair, pair_gain, wt, d_bias)
    mine, d_pair = lax.optimization_barrier((mine, d_pair))
    dw, dwo, dwb = unpack(place, mine, send(mine, OTHER))
    return inc, dx, d_pair, dw, dwo, dwb.T


def solution(mesh):
    tok = P("seq", "res", None)
    return jax.shard_map(
        local,
        mesh=mesh,
        in_specs=(tok, P(), P(), P(), P(), tok, P(), P(), tok),
        out_specs=(tok, tok, tok, P(), P(), P()),
        check_vma=False,
    )
```

time: 169 us -> 148 us (0.88)
  blocking collectives: 25.7 us -> 0 us
  starting transfers between devices: 38.6 us -> 46.7 us
  local copies, waits for them, and re-layouts: 9.17 us -> 2.44 us
  waiting for transfers between devices: 40.3 us -> 46.1 us
  Pallas kernels: 49.2 us -> 45.9 us
    all_to_all x2 -> x0, blocking collectives: 25.7 us -> none  [the longest x1 14.8 us: layer_swap(): lax.all_to_all(x, ALL, split_axis=0, concat_axis=0, tiled=True, axis_inde...]
    all_to_all x1 -> x4, starting transfers between devices: 4.94 us -> 18.4 us  [group_swap(): lax.all_to_all(x, ALL, split_axis=0, concat_axis=0, tiled=True, axis_inde...]
    all_to_all x1 -> x4, waiting for transfers between devices: 0.01 us -> 12.3 us  [group_swap(): lax.all_to_all(x, ALL, split_axis=0, concat_axis=0, tiled=True, axis_inde...]
    all_to_all x3 -> x2, waiting for transfers between devices: 11 us -> 1.27 us  [swap(): return lax.all_to_all(x, axis, split_axis=0, concat_axis=0, tiled=True)]
    unnamed x32 -> x14, local copies, waits for them, and re-layouts: 8.21 us -> 0.99 us
    all_to_all x3 -> x2, starting transfers between devices: 12 us -> 8.56 us  [swap(): return lax.all_to_all(x, axis, split_axis=0, concat_axis=0, tiled=True)]
    pallas_call x1, Pallas kernels: 10.2 us -> 7.09 us  [pair_grad(): pl.pallas_call(pair_grad_kernel, grid=(j // step,), in_specs=[pl.BlockSpe...]
    ppermute x12 -> x10, waiting for transfers between devices: 27 us -> 29.8 us  [send(): return lax.ppermute(x, 'seq', pairs)]
  transfers between devices with their start and end apart: 19 -> 19, of which waited for: 12 -> 15; matrix products, arithmetic and copies ran while one was open for 2% -> 1% of each run, Pallas kernels for 11% -> 13%
where the time goes in v3:
time: 148 us; the launch traced here: 147 us
  starting transfers between devices  46.7 us (32%)
  waiting for transfers between devices  46.1 us (31%)
  Pallas kernels  45.9 us (31%)
  other arithmetic  4.64 us (3%)
  local copies, waits for them, and re-layouts  2.44 us (2%)
    ppermute x10, waiting for transfers between devices, send(): return lax.ppermute(x, 'seq', pairs)  29.8 us
    pallas_call x1, Pallas kernels, attention(): pl.pallas_call(attention_kernel, grid_spec=pltpu.PrefetchScalarGridSpec(n...  19.3 us
    all_to_all x4, starting transfers between devices, group_swap(): lax.all_to_all(x, ALL, split_axis=0, concat_axis=0, tiled=True, axis_inde...  18.4 us
    ppermute x10, starting transfers between devices, send(): return lax.ppermute(x, 'seq', pairs)  16.5 us
    all_to_all x4, waiting for transfers between devices, group_swap(): lax.all_to_all(x, ALL, split_axis=0, concat_axis=0, tiled=True, axis_inde...  12.3 us
    all_to_all x2, starting transfers between devices, swap(): return lax.all_to_all(x, axis, split_axis=0, concat_axis=0, tiled=True)  8.56 us
    pallas_call x1, Pallas kernels, pair_grad(): pl.pallas_call(pair_grad_kernel, grid=(j // step,), in_specs=[pl.BlockSpe...  7.09 us
    pallas_call x1, Pallas kernels, finish(): pl.pallas_call(finish_kernel, grid_spec=pltpu.PrefetchScalarGridSpec(num_...  5.96 us
  transfers between devices with their start and end apart: 19, of which 15 were waited for; matrix products, arithmetic and copies ran while one was open for 1% of the time, Pallas kernels for 13%

profile of v3, /device:TPU:1, one launch (start us, length us, event | category | flops | bytes accessed | tf_op | source)
XLA Modules:
  0.0 146.6 jit_solution(7002381733389159838)
XLA Ops:
  0.6 5.3 %pair_bias.1 = (bf16[2,8,64,128]{3,2,1,0:T(8,128)(2,1)}, bf16[64,128,128]{2,1,0:T(8,128)(2,1)}) custom-call(bf16[64,128,128]{2,1,0:T(8,128)(2,1)} %x_ref.7, f32[1,128]{1,0:T(1,128)} %bitcast.31, bf16[8,128]{1,0:T(8,128)(2,1)} %bitcast.26), custom_call_target="tpu_custom_call" | custom-call | flops 4000000000 | bytes 12000000 | tf_op jit(solution)/shard_map/pair_bias/pallas_call | solution.py:126
  5.9 7.6 %all-to-all-start = ((bf16[16,64,128]{2,1,0:T(8,128)(2,1)}), bf16[16,64,128]{2,1,0:T(8,128)(2,1)S(1)}, u32[]{:S(2)}, u32[]{:S(2)}) async-start(bf16[16,64,128]{2,1,0:T(8,128)(2,1)} %bitcast.25), calls=%async_computation | async-start | bytes 524288 | tf_op jit(solution)/shard_map/all_to_all | solution.py:512
  13.5 3.9 %project.1 = (bf16[8,4,128,128]{3,2,1,0:T(8,128)(2,1)}, f32[4,128,256]{2,1,0:T(8,128)}, f32[4,128,256]{2,1,0:T(8,128)}) custom-call(bf16[4,128,256]{2,1,0:T(8,128)(2,1)} %x_ref.6, f32[1,256]{1,0:T(1,128)} %bitcast.29, bf16[256,1024]{1,0:T(8,128)(2,1)} %w_ref.3, f32[1,256]{1,0:T(1,128)} %bitcast.28, bf16[256,256]{1,0:T(8,128)(2,1)} %wo_ref.3, ...), custom_call_target="tpu_custom_call" | custom-call | flops 3000000000 | bytes 9000000 | tf_op jit(solution)/shard_map/project/pallas_call | solution.py:93
  17.4 3.5 %all-to-all-done = bf16[16,64,128]{2,1,0:T(8,128)(2,1)S(1)} async-done(((bf16[16,64,128]{2,1,0:T(8,128)(2,1)}), bf16[16,64,128]{2,1,0:T(8,128)(2,1)S(1)}, u32[]{:S(2)}, u32[]{:S(2)}) %all-to-all-start) | async-done | bytes 262176 | tf_op jit(solution)/shard_map/all_to_all | solution.py:512
  20.9 3.6 %all-to-all-start.1 = ((bf16[8,4,128,128]{3,2,1,0:T(8,128)(2,1)}), bf16[8,4,128,128]{3,2,1,0:T(8,128)(2,1)S(1)}, u32[]{:S(2)}, u32[]{:S(2)}) async-start(bf16[8,4,128,128]{3,2,1,0:T(8,128)(2,1)} %get-tuple-element.34), calls=%async_computation.1 | async-start | bytes 2097152 | tf_op jit(solution)/shard_map/all_to_all | solution.py:471
  24.5 3.8 %collective-permute-start.2 = (bf16[2,8,64,128]{3,2,1,0:T(8,128)(2,1)S(1)}, bf16[2,8,64,128]{3,2,1,0:T(8,128)(2,1)S(1)}, u32[]{:S(2)}, u32[]{:S(2)}) collective-permute-start(bf16[2,8,64,128]{3,2,1,0:T(8,128)(2,1)S(1)} %bitcast.19), channel_id=1, source_target_pairs={{0,48},{8,56},{16,0},{24,8},{32,16},{40,24},{48,32},{56,40},{64,11... | collective-permute-start | bytes 786440 | tf_op jit(solution)/shard_map/ppermute | solution.py:483
  29.0 9.2 %collective-permute-done.2 = bf16[2,8,64,128]{3,2,1,0:T(8,128)(2,1)S(1)} collective-permute-done((bf16[2,8,64,128]{3,2,1,0:T(8,128)(2,1)S(1)}, bf16[2,8,64,128]{3,2,1,0:T(8,128)(2,1)S(1)}, u32[]{:S(2)}, u32[]{:S(2)}) %collective-permute-start.2) | collective-permute-done | bytes 262176 | tf_op jit(solution)/shard_map/ppermute | solution.py:483
  38.2 4.8 %collective-permute-done = bf16[2,8,64,128]{3,2,1,0:T(8,128)(2,1)S(1)} collective-permute-done((bf16[2,8,64,128]{3,2,1,0:T(8,128)(2,1)S(1)}, bf16[2,8,64,128]{3,2,1,0:T(8,128)(2,1)S(1)}, u32[]{:S(2)}, u32[]{:S(2)}) %collective-permute-start) | collective-permute-done | bytes 262176 | tf_op jit(solution)/shard_map/ppermute | solution.py:483
  47.4 19.3 %attention.1 = (bf16[8,4,128,128]{3,2,1,0:T(8,128)(2,1)}, bf16[8,8,64,128]{3,2,1,0:T(8,128)(2,1)}, bf16[8,8,64,128]{3,2,1,0:T(8,128)(2,1)}) custom-call(s32[9]{0:T(128)} %stack.39.place_ref, bf16[8,4,128,128]{3,2,1,0:T(8,128)(2,1)} %copy-done.2, bf16[8,8,64,128]{3,2,1,0:T(8,128)(2,1)} %copy-done.3, bf16[8,8,64,128]{3,2,1,0:T(8,128)(2,1)} %copy-done.6), custom_call_target="tpu_custom_call" | custom-call | flops 17999998976 | bytes 54000000 | tf_op jit(solution)/shard_map/attention/pallas_call | solution.py:276
  67.1 5.0 %all-to-all-start.2 = ((bf16[8,4,128,128]{3,2,1,0:T(8,128)(2,1)}), bf16[8,4,128,128]{3,2,1,0:T(8,128)(2,1)S(1)}, u32[]{:S(2)}, u32[]{:S(2)}) async-start(bf16[8,4,128,128]{3,2,1,0:T(8,128)(2,1)} %get-tuple-element.37), calls=%async_computation.2 | async-start | bytes 2097152 | tf_op jit(solution)/shard_map/all_to_all | solution.py:471
  74.5 5.4 %collective-permute-done.5 = bf16[2,8,64,128]{3,2,1,0:T(8,128)(2,1)S(1)} collective-permute-done((bf16[2,8,64,128]{3,2,1,0:T(8,128)(2,1)S(1)}, bf16[2,8,64,128]{3,2,1,0:T(8,128)(2,1)S(1)}, u32[]{:S(2)}, u32[]{:S(2)}) %collective-permute-start.5) | collective-permute-done | bytes 262176 | tf_op jit(solution)/shard_map/ppermute | solution.py:483
  80.0 2.7 %collective-permute-done.7 = bf16[2,8,64,128]{3,2,1,0:T(8,128)(2,1)S(1)} collective-permute-done((bf16[2,8,64,128]{3,2,1,0:T(8,128)(2,1)S(1)}, bf16[2,8,64,128]{3,2,1,0:T(8,128)(2,1)S(1)}, u32[]{:S(2)}, u32[]{:S(2)}) %collective-permute-start.7) | collective-permute-done | bytes 262176 | tf_op jit(solution)/shard_map/ppermute | solution.py:483
  82.7 3.2 %collective-permute-done.6 = bf16[2,8,64,128]{3,2,1,0:T(8,128)(2,1)S(1)} collective-permute-done((bf16[2,8,64,128]{3,2,1,0:T(8,128)(2,1)S(1)}, bf16[2,8,64,128]{3,2,1,0:T(8,128)(2,1)S(1)}, u32[]{:S(2)}, u32[]{:S(2)}) %collective-permute-start.6) | collective-permute-done | bytes 262176 | tf_op jit(solution)/shard_map/ppermute | solution.py:483
  88.0 3.8 %all-to-all-start.3 = ((bf16[16,64,128]{2,1,0:T(8,128)(2,1)}), bf16[16,64,128]{2,1,0:T(8,128)(2,1)S(1)}, u32[]{:S(2)}, u32[]{:S(2)}) async-start(bf16[16,64,128]{2,1,0:T(8,128)(2,1)} %bitcast.15), calls=%async_computation.3 | async-start | bytes 524288 | tf_op jit(solution)/shard_map/all_to_all | solution.py:512
  91.8 6.0 %finish.1 = (bf16[4,128,256]{2,1,0:T(8,128)(2,1)}, bf16[4,128,256]{2,1,0:T(8,128)(2,1)}, bf16[5,256,128]{2,1,0:T(8,128)(2,1)}, bf16[5,256,128]{2,1,0:T(8,128)(2,1)}) custom-call(s32[9]{0:T(128)} %stack.39.place_ref, bf16[4,128,256]{2,1,0:T(8,128)(2,1)} %x_ref.6, f32[1,256]{1,0:T(1,128)} %bitcast.30, bf16[256,1024]{1,0:T(8,128)(2,1)} %w_ref.3, ...), custom_call_target="tpu_custom_call" | custom-call | flops 5000000000 | bytes 15000000 | tf_op jit(solution)/shard_map/finish/pallas_call | solution.py:356
  99.1 4.7 %collective-permute-start.8 = (bf16[5,256,128]{2,1,0:T(8,128)(2,1)}, bf16[5,256,128]{2,1,0:T(8,128)(2,1)S(1)}, u32[]{:S(2)}, u32[]{:S(2)}) collective-permute-start(bf16[5,256,128]{2,1,0:T(8,128)(2,1)} %get-tuple-element.44), channel_id=1, source_target_pairs={{0,8},{8,0},{16,24},{24,16},{32,40},{40,32},{48,56},{56,48},{64,72... | collective-permute-start | bytes 983048 | tf_op jit(solution)/shard_map/ppermute | solution.py:483
  105.2 1.8 %add_convert_fusion.1 = bf16[5,256,128]{2,1,0:T(8,128)(2,1)} fusion(bf16[5,256,128]{2,1,0:T(8,128)(2,1)S(1)} %collective-permute-done.8, bf16[5,256,128]{2,1,0:T(8,128)(2,1)} %get-tuple-element.40), kind=kLoop, calls=%fused_computation.3 | loop fusion | flops 655360 | bytes 983040 | tf_op jit(solution)/shard_map/convert_element_type | solution.py:615
  107.0 3.5 %all-to-all-start.4 = ((bf16[16,80,128]{2,1,0:T(8,128)(2,1)}), bf16[16,80,128]{2,1,0:T(8,128)(2,1)S(1)}, u32[]{:S(2)}, u32[]{:S(2)}) async-start(bf16[16,80,128]{2,1,0:T(8,128)(2,1)} %bitcast.17), calls=%async_computation.4 | async-start | bytes 655360 | tf_op jit(solution)/shard_map/all_to_all | solution.py:512
  110.6 2.6 %pair_weight.1 = f32[8,128]{1,0:T(8,128)} custom-call(bf16[64,128,128]{2,1,0:T(8,128)(2,1)} %get-tuple-element.45.n_ref, bf16[2,8,64,128]{3,2,1,0:T(8,128)(2,1)} %bitcast.23), custom_call_target="tpu_custom_call" | custom-call | flops 2000000000 | bytes 6000000 | tf_op jit(solution)/shard_map/pair_weight/pallas_call | solution.py:398
  113.2 6.3 %all-to-all-done.4 = bf16[16,80,128]{2,1,0:T(8,128)(2,1)S(1)} async-done(((bf16[16,80,128]{2,1,0:T(8,128)(2,1)}), bf16[16,80,128]{2,1,0:T(8,128)(2,1)S(1)}, u32[]{:S(2)}, u32[]{:S(2)}) %all-to-all-start.4) | async-done | bytes 327712 | tf_op jit(solution)/shard_map/all_to_all | solution.py:512
  124.1 2.1 %collective-permute-done.10 = bf16[96,128]{1,0:T(8,128)(2,1)S(1)} collective-permute-done((bf16[96,128]{1,0:T(8,128)(2,1)S(1)}, bf16[96,128]{1,0:T(8,128)(2,1)S(1)}, u32[]{:S(2)}, u32[]{:S(2)}) %collective-permute-start.10) | collective-permute-done | bytes 24608 | tf_op jit(solution)/shard_map/ppermute | solution.py:530
  127.7 3.6 %all-to-all-start.5 = ((bf16[16,96,128]{2,1,0:T(8,128)(2,1)}), bf16[16,96,128]{2,1,0:T(8,128)(2,1)S(1)}, u32[]{:S(2)}, u32[]{:S(2)}) async-start(bf16[16,96,128]{2,1,0:T(8,128)(2,1)} %broadcast_in_dim.2), calls=%async_computation.5 | async-start | bytes 786432 | tf_op jit(solution)/shard_map/all_to_all | solution.py:512
  131.3 7.1 %pair_grad.1 = bf16[64,128,128]{2,1,0:T(8,128)(2,1)} custom-call(bf16[64,128,128]{2,1,0:T(8,128)(2,1)} %x_ref.7, f32[1,128]{1,0:T(1,128)} %bitcast.32, bf16[8,128]{1,0:T(8,128)(2,1)} %bitcast.27, bf16[2,8,64,128]{3,2,1,0:T(8,128)(2,1)} %bitcast.24), custom_call_target="tpu_custom_call" | custom-call | flops 8000000000 | bytes 24000000 | tf_op jit(solution)/shard_map/pair_grad/pallas_call | solution.py:452
  139.5 4.0 %collective-permute-start.12 = (bf16[16,96,128]{2,1,0:T(8,128)(2,1)S(1)}, bf16[16,96,128]{2,1,0:T(8,128)(2,1)S(1)}, u32[]{:S(2)}, u32[]{:S(2)}) collective-permute-start(bf16[16,96,128]{2,1,0:T(8,128)(2,1)S(1)} %all-to-all-done.5.mine_ref), channel_id=1, source_target_pairs={{0,8},{8,0},{16,24},{24,16},{32,40},{40,32},{48,56},{56,48},{64,72... | collective-permute-start | bytes 1179656 | tf_op jit(solution)/shard_map/ppermute | solution.py:483
  (45 shorter events, 23.2 us)
Async XLA Ops:
  5.9 15.0 %all-to-all-start = ((bf16[16,64,128]{2,1,0:T(8,128)(2,1)}), bf16[16,64,128]{2,1,0:T(8,128)(2,1)S(1)}, u32[]{:S(2)}, u32[]{:S(2)}) async-start(bf16[16,64,128]{2,1,0:T(8,128)(2,1)} %bitcast.25), calls=%async_computation | async-start | bytes 524288 | tf_op jit(solution)/shard_map/all_to_all | solution.py:512
  20.9 22.2 %all-to-all-start.1 = ((bf16[8,4,128,128]{3,2,1,0:T(8,128)(2,1)}), bf16[8,4,128,128]{3,2,1,0:T(8,128)(2,1)S(1)}, u32[]{:S(2)}, u32[]{:S(2)}) async-start(bf16[8,4,128,128]{3,2,1,0:T(8,128)(2,1)} %get-tuple-element.34), calls=%async_computation.1 | async-start | bytes 2097152 | tf_op jit(solution)/shard_map/all_to_all | solution.py:471
  24.5 13.7 %collective-permute-start.2 = (bf16[2,8,64,128]{3,2,1,0:T(8,128)(2,1)S(1)}, bf16[2,8,64,128]{3,2,1,0:T(8,128)(2,1)S(1)}, u32[]{:S(2)}, u32[]{:S(2)}) collective-permute-start(bf16[2,8,64,128]{3,2,1,0:T(8,128)(2,1)S(1)} %bitcast.19), channel_id=1, source_target_pairs={{0,48},{8,56},{16,0},{24,8},{32,16},{40,24},{48,32},{56,40},{64,11... | collective-permute-start | bytes 786440 | tf_op jit(solution)/shard_map/ppermute | solution.py:483
  28.3 9.9 %collective-permute-start.1 = (bf16[2,8,64,128]{3,2,1,0:T(8,128)(2,1)S(1)}, bf16[2,8,64,128]{3,2,1,0:T(8,128)(2,1)S(1)}, u32[]{:S(2)}, u32[]{:S(2)}) collective-permute-start(bf16[2,8,64,128]{3,2,1,0:T(8,128)(2,1)S(1)} %bitcast.20), channel_id=1, source_target_pairs={{0,32},{8,40},{16,48},{24,56},{32,0},{40,8},{48,16},{56,24},{64,96... | collective-permute-start | bytes 786440 | tf_op jit(solution)/shard_map/ppermute | solution.py:483
  28.3 14.7 %collective-permute-start = (bf16[2,8,64,128]{3,2,1,0:T(8,128)(2,1)S(1)}, bf16[2,8,64,128]{3,2,1,0:T(8,128)(2,1)S(1)}, u32[]{:S(2)}, u32[]{:S(2)}) collective-permute-start(bf16[2,8,64,128]{3,2,1,0:T(8,128)(2,1)S(1)} %bitcast.21), channel_id=1, source_target_pairs={{0,16},{8,24},{16,32},{24,40},{32,48},{40,56},{48,0},{56,8},{64,80... | collective-permute-start | bytes 786440 | tf_op jit(solution)/shard_map/ppermute | solution.py:483
  43.2 3.3 %copy-start.3 = (bf16[8,8,64,128]{3,2,1,0:T(8,128)(2,1)}, bf16[8,8,64,128]{3,2,1,0:T(8,128)(2,1)S(1)}, u32[]{:S(2)}) copy-start(bf16[8,8,64,128]{3,2,1,0:T(8,128)(2,1)S(1)} %pad_maximum_fusion.own_ref) | copy-start | bytes 3145732
  43.2 3.2 %collective-permute-start.3 = (bf16[8,8,64,128]{3,2,1,0:T(8,128)(2,1)S(1)}, bf16[8,8,64,128]{3,2,1,0:T(8,128)(2,1)S(1)}, u32[]{:S(2)}, u32[]{:S(2)}) collective-permute-start(bf16[8,8,64,128]{3,2,1,0:T(8,128)(2,1)S(1)} %pad_maximum_fusion.own_ref), channel_id=1, source_target_pairs={{0,8},{8,0},{16,24},{24,16},{32,40},{40,32},{48,56},{56,48},{64,72... | collective-permute-start | bytes 3145736 | tf_op jit(solution)/shard_map/ppermute | solution.py:483
  66.7 5.4 %copy-start.1 = (bf16[8,8,64,128]{3,2,1,0:T(8,128)(2,1)S(1)}, bf16[8,8,64,128]{3,2,1,0:T(8,128)(2,1)}, u32[]{:S(2)}) copy-start(bf16[8,8,64,128]{3,2,1,0:T(8,128)(2,1)} %get-tuple-element.41) | copy-start | bytes 3145732
  66.7 5.4 %collective-permute-start.4 = (bf16[8,8,64,128]{3,2,1,0:T(8,128)(2,1)}, bf16[8,8,64,128]{3,2,1,0:T(8,128)(2,1)S(1)}, u32[]{:S(2)}, u32[]{:S(2)}) collective-permute-start(bf16[8,8,64,128]{3,2,1,0:T(8,128)(2,1)} %get-tuple-element.42), channel_id=1, source_target_pairs={{0,8},{8,0},{16,24},{24,16},{32,40},{40,32},{48,56},{56,48},{64,72... | collective-permute-start | bytes 3145736 | tf_op jit(solution)/shard_map/ppermute | solution.py:483
  67.1 20.9 %all-to-all-start.2 = ((bf16[8,4,128,128]{3,2,1,0:T(8,128)(2,1)}), bf16[8,4,128,128]{3,2,1,0:T(8,128)(2,1)S(1)}, u32[]{:S(2)}, u32[]{:S(2)}) async-start(bf16[8,4,128,128]{3,2,1,0:T(8,128)(2,1)} %get-tuple-element.37), calls=%async_computation.2 | async-start | bytes 2097152 | tf_op jit(solution)/shard_map/all_to_all | solution.py:471
  72.6 7.4 %collective-permute-start.5 = (bf16[2,8,64,128]{3,2,1,0:T(8,128)(2,1)S(1)}, bf16[2,8,64,128]{3,2,1,0:T(8,128)(2,1)S(1)}, u32[]{:S(2)}, u32[]{:S(2)}) collective-permute-start(bf16[2,8,64,128]{3,2,1,0:T(8,128)(2,1)S(1)} %get-tuple-element.52), channel_id=1, source_target_pairs={{0,48},{8,56},{16,0},{24,8},{32,16},{40,24},{48,32},{56,40},{64,11... | collective-permute-start | bytes 786440 | tf_op jit(solution)/shard_map/ppermute | solution.py:483
  73.2 9.4 %collective-permute-start.7 = (bf16[2,8,64,128]{3,2,1,0:T(8,128)(2,1)S(1)}, bf16[2,8,64,128]{3,2,1,0:T(8,128)(2,1)S(1)}, u32[]{:S(2)}, u32[]{:S(2)}) collective-permute-start(bf16[2,8,64,128]{3,2,1,0:T(8,128)(2,1)S(1)} %get-tuple-element.53), channel_id=1, source_target_pairs={{0,16},{8,24},{16,32},{24,40},{32,48},{40,56},{48,0},{56,8},{64,80... | collective-permute-start | bytes 786440 | tf_op jit(solution)/shard_map/ppermute | solution.py:483
  74.1 11.7 %collective-permute-start.6 = (bf16[2,8,64,128]{3,2,1,0:T(8,128)(2,1)S(1)}, bf16[2,8,64,128]{3,2,1,0:T(8,128)(2,1)S(1)}, u32[]{:S(2)}, u32[]{:S(2)}) collective-permute-start(bf16[2,8,64,128]{3,2,1,0:T(8,128)(2,1)S(1)} %get-tuple-element.54), channel_id=1, source_target_pairs={{0,32},{8,40},{16,48},{24,56},{32,0},{40,8},{48,16},{56,24},{64,96... | collective-permute-start | bytes 786440 | tf_op jit(solution)/shard_map/ppermute | solution.py:483
  88.0 3.8 %copy-start.4 = (bf16[8,4,128,128]{3,2,1,0:T(8,128)(2,1)}, bf16[8,4,128,128]{3,2,1,0:T(8,128)(2,1)S(1)}, u32[]{:S(2)}) copy-start(bf16[8,4,128,128]{3,2,1,0:T(8,128)(2,1)S(1)} %all-to-all-done.2.back_ref) | copy-start | bytes 3145732
  88.0 11.1 %all-to-all-start.3 = ((bf16[16,64,128]{2,1,0:T(8,128)(2,1)}), bf16[16,64,128]{2,1,0:T(8,128)(2,1)S(1)}, u32[]{:S(2)}, u32[]{:S(2)}) async-start(bf16[16,64,128]{2,1,0:T(8,128)(2,1)} %bitcast.15), calls=%async_computation.3 | async-start | bytes 524288 | tf_op jit(solution)/shard_map/all_to_all | solution.py:512
  99.1 11.5 %copy-start.5 = (bf16[16,64,128]{2,1,0:T(8,128)(2,1)}, bf16[16,64,128]{2,1,0:T(8,128)(2,1)S(1)}, u32[]{:S(2)}) copy-start(bf16[16,64,128]{2,1,0:T(8,128)(2,1)S(1)} %all-to-all-done.3) | copy-start | bytes 786436
  99.1 6.2 %collective-permute-start.8 = (bf16[5,256,128]{2,1,0:T(8,128)(2,1)}, bf16[5,256,128]{2,1,0:T(8,128)(2,1)S(1)}, u32[]{:S(2)}, u32[]{:S(2)}) collective-permute-start(bf16[5,256,128]{2,1,0:T(8,128)(2,1)} %get-tuple-element.44), channel_id=1, source_target_pairs={{0,8},{8,0},{16,24},{24,16},{32,40},{40,32},{48,56},{56,48},{64,72... | collective-permute-start | bytes 983048 | tf_op jit(solution)/shard_map/ppermute | solution.py:483
  107.0 12.5 %all-to-all-start.4 = ((bf16[16,80,128]{2,1,0:T(8,128)(2,1)}), bf16[16,80,128]{2,1,0:T(8,128)(2,1)S(1)}, u32[]{:S(2)}, u32[]{:S(2)}) async-start(bf16[16,80,128]{2,1,0:T(8,128)(2,1)} %bitcast.17), calls=%async_computation.4 | async-start | bytes 655360 | tf_op jit(solution)/shard_map/all_to_all | solution.py:512
  120.3 3.9 %collective-permute-start.11 = (bf16[96,128]{1,0:T(8,128)(2,1)S(1)}, bf16[96,128]{1,0:T(8,128)(2,1)S(1)}, u32[]{:S(2)}, u32[]{:S(2)}) collective-permute-start(bf16[96,128]{1,0:T(8,128)(2,1)S(1)} %fusion), channel_id=1, source_target_pairs={{0,65},{1,64},{2,67},{3,66},{4,69},{5,68},{6,71},{7,70},{8,73},{9,... | collective-permute-start | bytes 73736 | tf_op jit(solution)/shard_map/ppermute | solution.py:530
  121.9 4.3 %collective-permute-start.10 = (bf16[96,128]{1,0:T(8,128)(2,1)S(1)}, bf16[96,128]{1,0:T(8,128)(2,1)S(1)}, u32[]{:S(2)}, u32[]{:S(2)}) collective-permute-start(bf16[96,128]{1,0:T(8,128)(2,1)S(1)} %fusion), channel_id=1, source_target_pairs={{0,64},{1,65},{2,66},{3,67},{4,68},{5,69},{6,70},{7,71},{8,72},{9,... | collective-permute-start | bytes 73736 | tf_op jit(solution)/shard_map/ppermute | solution.py:530
  122.5 3.7 %collective-permute-start.9 = (bf16[96,128]{1,0:T(8,128)(2,1)S(1)}, bf16[96,128]{1,0:T(8,128)(2,1)S(1)}, u32[]{:S(2)}, u32[]{:S(2)}) collective-permute-start(bf16[96,128]{1,0:T(8,128)(2,1)S(1)} %fusion), channel_id=1, source_target_pairs={{0,1},{1,0},{2,3},{3,2},{4,5},{5,4},{6,7},{7,6},{8,9},{9,8},{10,11... | collective-permute-start | bytes 73736 | tf_op jit(solution)/shard_map/ppermute | solution.py:530
  127.7 11.8 %all-to-all-start.5 = ((bf16[16,96,128]{2,1,0:T(8,128)(2,1)}), bf16[16,96,128]{2,1,0:T(8,128)(2,1)S(1)}, u32[]{:S(2)}, u32[]{:S(2)}) async-start(bf16[16,96,128]{2,1,0:T(8,128)(2,1)} %broadcast_in_dim.2), calls=%async_computation.5 | async-start | bytes 786432 | tf_op jit(solution)/shard_map/all_to_all | solution.py:512
  131.3 13.6 %copy-start = (s32[9]{0:T(128)S(1)}, s32[9]{0:T(128)}, u32[]{:S(2)}) copy-start(s32[9]{0:T(128)} %stack.39.place_ref) | copy-start | bytes 112
  139.5 5.3 %collective-permute-start.12 = (bf16[16,96,128]{2,1,0:T(8,128)(2,1)S(1)}, bf16[16,96,128]{2,1,0:T(8,128)(2,1)S(1)}, u32[]{:S(2)}, u32[]{:S(2)}) collective-permute-start(bf16[16,96,128]{2,1,0:T(8,128)(2,1)S(1)} %all-to-all-done.5.mine_ref), channel_id=1, source_target_pairs={{0,8},{8,0},{16,24},{24,16},{32,40},{40,32},{48,56},{56,48},{64,72... | collective-permute-start | bytes 1179656 | tf_op jit(solution)/shard_map/ppermute | solution.py:483
  (2 other events, 4.2 us)

commit v4 on v3

--- a/solution.py
+++ b/solution.py
@@ -41,17 +41,12 @@
     return inv * (g - mean_g - hat * mean_gx)
 
 
-def split(x):
-    high = x.astype(BF16)
-    return jnp.concatenate([high, (x - high.astype(F32)).astype(BF16)], axis=1)
-
-
 def row_mean(x, ones):
-    return nn(split(x), ones)
+    return nn(x.astype(BF16), ones)
 
 
 def normalize_pairs(x, ones):
-    centered = x.astype(F32) - nn(x, ones[:128])
+    centered = x.astype(F32) - nn(x, ones)
     inv = lax.rsqrt(row_mean(centered * centered, ones) + EPS)
     return centered * inv, inv
 
@@ -107,7 +102,7 @@
 
 
 def bias_kernel(x_ref, gain_ref, wt_ref, out_ref, normed_ref, tmp):
-    ones = jnp.full((256, 128), 1 / 128, BF16)
+    ones = jnp.full((128, 128), 1 / 128, BF16)
     rows = x_ref.shape[0]
     hat, _ = normalize_pairs(x_ref[...].reshape(rows * 128, 128), ones)
     normed = (hat * gain_ref[...]).astype(BF16).reshape(rows, 128, 128)
@@ -169,9 +164,13 @@
         acc[...] = jnp.zeros_like(acc)
 
     ones = jnp.ones((16, 1024), BF16)
-    block = 2 * step
-
-    def score(s):
+    turns = own_ref.shape[1] // 2
+    rounds = [(u, s) for u in range(turns) for s in range(n_seq)]
+    blocks = [2 * (step * turns + u) for u in range(turns)]
+
+    def score(n):
+        u, s = rounds[n]
+        block = blocks[u]
         xq = jnp.concatenate([x_ref[block, s].T, x_ref[block + 1, s].T], axis=1)
         rhs_q = jnp.concatenate([zeros(32), xq[0:32], zeros(64)], axis=0)
         top = jnp.full((8, iw), -jnp.inf, F32)
@@ -179,21 +178,22 @@
         for d in range(0, 8, k):
             big = nn(xr[d : d + k, s].reshape(k * 128, 128), rhs_q)
             for c in range(d, d + k):
-                lo = jnp.concatenate([own_ref[c, 0], other_ref[c, 0]], axis=0)
-                hi = jnp.concatenate([own_ref[c, 1], other_ref[c, 1]], axis=0)
+                lo = jnp.concatenate([own_ref[c, 2 * u], other_ref[c, 2 * u]], axis=0)
+                hi = jnp.concatenate([own_ref[c, 2 * u + 1], other_ref[c, 2 * u + 1]], axis=0)
                 sc = big[(c - d) * 128 : (c - d + 1) * 128]
                 sc = sc + jnp.concatenate([lo, hi], axis=1).astype(F32)
-                scores[s % 2, c] = sc
+                scores[n % 2, c] = sc
                 top = jnp.maximum(top, jnp.max(sc.reshape(16, 8, iw), axis=0))
                 yield
         return xq, rhs_q, jnp.max(top, axis=0, keepdims=True)
 
-    def weigh(s, xq, top):
+    def weigh(n, xq, top):
+        u, s = rounds[n]
         for c in range(8):
-            ed[s % 2, c, :, :iw] = jnp.exp(scores[s % 2, c] - top).astype(BF16)
+            ed[n % 2, c, :, :iw] = jnp.exp(scores[n % 2, c] - top).astype(BF16)
             yield
         left = jnp.concatenate([xt[s, 64:96, :], ones], axis=0)
-        ot = nn(left, ed[s % 2, :, :, :iw].reshape(1024, iw))
+        ot = nn(left, ed[n % 2, :, :, :iw].reshape(1024, iw))
         inv = 1.0 / ot[32:33]
         ot = ot[0:32] * inv
         da = (xq[96:128].astype(F32) * inv).astype(BF16)
@@ -201,15 +201,17 @@
         rhs_a = jnp.concatenate([zeros(64), da, zeros(32)], axis=0)
         return ot, rhs_a, delta
 
-    def back(s, rhs_q, rhs_a, delta, ot):
+    def back(n, rhs_q, rhs_a, delta, ot):
+        u, s = rounds[n]
+        block = blocks[u]
         k = 8
         for c in range(8):
             if c % k == 0:
                 big = nn(xr[c : c + k, s].reshape(k * 128, 128), rhs_a)
-            e = ed[s % 2, c, :, :iw]
+            e = ed[n % 2, c, :, :iw]
             ds = e.astype(F32) * (big[c % k * 128 : (c % k + 1) * 128] - delta)
             low = ds.astype(BF16)
-            ed[s % 2, c, :, iw:] = low
+            ed[n % 2, c, :, iw:] = low
             if s == 0:
                 total[c] = ds
             elif s < n_seq - 1:
@@ -217,15 +219,15 @@
             else:
                 low = (total[c] + ds).astype(BF16)
                 for t in range(2):
-                    down_ref[c, t] = low[:64, t * 128 : (t + 1) * 128]
-                    dother_ref[c, t] = low[64:, t * 128 : (t + 1) * 128]
+                    down_ref[c, 2 * u + t] = low[:64, t * 128 : (t + 1) * 128]
+                    dother_ref[c, 2 * u + t] = low[64:, t * 128 : (t + 1) * 128]
             if (c + 1) % 8 == 0:
                 w = slice(c + 1 - 8, c + 1)
                 both = jnp.concatenate([rhs_a, rhs_q], axis=1)
-                more = nt(ed[s % 2, w].reshape(8 * 128, 2 * iw), both)
+                more = nt(ed[n % 2, w].reshape(8 * 128, 2 * iw), both)
                 acc[s, w] += more.reshape(8, 128, 128)
             yield
-        dq = nn(xt[s, 32:64, :], ed[s % 2, :, :, iw:].reshape(1024, iw)) * SCALE
+        dq = nn(xt[s, 32:64, :], ed[n % 2, :, :, iw:].reshape(1024, iw)) * SCALE
         both = jnp.concatenate([ot, jnp.zeros((64, iw), F32), dq], axis=0)
         for t in range(2):
             qd[s, block + t] = both[:, t * 128 : (t + 1) * 128].T
@@ -243,21 +245,17 @@
                     state[key] = stop.value
                     live.remove(item)
 
-    for t in range(n_seq + 2):
+    for t in range(len(rounds) + 2):
         gens = []
-        if 0 <= t - 2 < n_seq:
-            s = t - 2
-            xq, rhs_q, top = state["s", s]
-            ot, rhs_a, delta = state["w", s]
-            late = (("b", s), back(s, rhs_q, rhs_a, delta, ot))
-        if 0 <= t - 1 < n_seq:
-            s = t - 1
-            xq, rhs_q, top = state["s", s]
-            gens.append((("w", s), weigh(s, xq, top)))
-        if t < n_seq:
+        if 0 <= t - 1 < len(rounds):
+            xq, rhs_q, top = state["s", t - 1]
+            gens.append((("w", t - 1), weigh(t - 1, xq, top)))
+        if t < len(rounds):
             gens.append((("s", t), score(t)))
         if t >= 2:
-            gens.append(late)
+            xq, rhs_q, top = state["s", t - 2]
+            ot, rhs_a, delta = state["w", t - 2]
+            gens.append((("b", t - 2), back(t - 2, rhs_q, rhs_a, delta, ot)))
         drive(gens)
 
     @pl.when(step == pl.num_programs(0) - 1)
@@ -271,13 +269,13 @@
 
 def attention(place, x, own, other):
     r, s, n, _ = x.shape
-    half = pl.BlockSpec((8, 2, 64, 128), lambda g, p: (0, g, 0, 0))
+    half = pl.BlockSpec((8, 4, 64, 128), lambda g, p: (0, g, 0, 0))
     whole = pl.BlockSpec((r, s, n, 128), lambda g, p: (0, 0, 0, 0))
     return pl.pallas_call(
         attention_kernel,
         grid_spec=pltpu.PrefetchScalarGridSpec(
             num_scalar_prefetch=1,
-            grid=(4,),
+            grid=(2,),
             in_specs=[whole, half, half],
             out_specs=[whole, half, half],
             scratch_shapes=[
@@ -415,7 +413,7 @@
     step = pl.program_id(0)
     gain = gain_ref[...]
     rows = x_ref.shape[0]
-    ones = jnp.full((256, 128), 1 / 128, BF16)
+    ones = jnp.full((128, 128), 1 / 128, BF16)
 
     @pl.when(step == 0)
     def _():
@@ -446,25 +444,31 @@
     dx_ref[...] = out.astype(BF16).reshape(rows, 128, 128)
 
 
-def pair_grad(pair, gain, wt, db):
+def pair_grad(pair, gain, wt, db, begun=None):
     j, i, c = pair.shape
     step = 16
+    half = j // step // 2
+    first = 0 if begun is None else half
+    more = () if begun is None else (begun,)
+    body = lambda x, g, w, b, *rest: pair_grad_kernel(x, g, w, b, *rest[-2:])
     return pl.pallas_call(
-        pair_grad_kernel,
-        grid=(j // step,),
+        body,
+        grid=(half,),
         in_specs=[
-            pl.BlockSpec((step, i, c), lambda g: (g, 0, 0)),
+            pl.BlockSpec((step, i, c), lambda g: (g + first, 0, 0)),
             pl.BlockSpec((1, c), lambda g: (0, 0)),
             pl.BlockSpec((HEADS, c), lambda g: (0, 0)),
-            pl.BlockSpec((2, HEADS, step, i), lambda g: (0, 0, g, 0)),
-        ],
-        out_specs=pl.BlockSpec((step, i, c), lambda g: (g, 0, 0)),
+            pl.BlockSpec((2, HEADS, step, i), lambda g: (0, 0, g + first, 0)),
+        ]
+        + [pl.BlockSpec(memory_space=pl.ANY)] * len(more),
+        out_specs=pl.BlockSpec((step, i, c), lambda g: (g + first, 0, 0)),
         out_shape=jax.ShapeDtypeStruct((j, i, c), BF16),
         scratch_shapes=[pltpu.VMEM((step, 2 * HEADS * step, 256), BF16)],
+        input_output_aliases={4: 0} if more else {},
         compiler_params=params(),
-        cost_estimate=cost(8),
+        cost_estimate=cost(4),
         name="pair_grad",
-    )(pair, gain, wt, db)
+    )(pair, gain, wt, db, *more)
 
 
 def swap(x, axis):
@@ -523,7 +527,7 @@
 
 
 def sum_layers(part, extra):
-    part = jnp.sum(group_swap(part, LAYERS).astype(F32), axis=0)
+    part = jnp.sum(part.astype(F32), axis=0)
     part = jnp.concatenate([part, jnp.pad(extra, ((0, 8), (0, 0)))])
     low = part.astype(BF16)
     for k in (1, 2, 3):
@@ -615,8 +619,11 @@
     part = (keep.astype(F32) + send(away, OTHER).astype(F32)).astype(BF16)
     part = part.reshape(16, 80, 128)
     dwb = pair_weight(normed, d_bias)
+    part = group_swap(part, LAYERS)
+    begun = pair_grad(pair, pair_gain, wt, d_bias)
+    part, begun = lax.optimization_barrier((part, begun))
     mine = sum_layers(part, dwb)
-    d_pair = pair_grad(pair, pair_gain, wt, d_bias)
+    d_pair = pair_grad(pair, pair_gain, wt, d_bias, begun)
     mine, d_pair = lax.optimization_barrier((mine, d_pair))
     dw, dwo, dwb = unpack(place, mine, send(mine, OTHER))
     return inc, dx, d_pair, dw, dwo, dwb.T

time: 148 us -> 144 us (0.973)
  other arithmetic: 4.64 us -> 2.29 us
    all_to_all x4, waiting for transfers between devices: 12.3 us -> 13.8 us  [group_swap(): lax.all_to_all(x, ALL, split_axis=0, concat_axis=0, tiled=True, axis_inde...]
    ppermute x10, waiting for transfers between devices: 29.8 us -> 28.3 us  [send(): return lax.ppermute(x, 'seq', pairs)]
    pallas_call x1 -> x2, Pallas kernels: 7.09 us -> 8.24 us  [pair_grad(): pl.pallas_call(body, grid=(half,), in_specs=[pl.BlockSpec((step, i, c), l...]
  transfers between devices with their start and end apart: 19 -> 19, of which waited for: 15 -> 14; matrix products, arithmetic and copies ran while one was open for 1% -> 1% of each run, Pallas kernels for 13% -> 14%
where the time goes in v4:
time: 144 us
  starting transfers between devices  47.3 us (33%)
  waiting for transfers between devices  45.7 us (32%)
  Pallas kernels  45 us (31%)
  local copies, waits for them, and re-layouts  2.52 us (2%)
  other arithmetic  2.29 us (2%)
    ppermute x10, waiting for transfers between devices, send(): return lax.ppermute(x, 'seq', pairs)  28.3 us
    all_to_all x4, starting transfers between devices, group_swap(): lax.all_to_all(x, ALL, split_axis=0, concat_axis=0, tiled=True, axis_inde...  18.6 us
    pallas_call x1, Pallas kernels, attention(): pl.pallas_call(attention_kernel, grid_spec=pltpu.PrefetchScalarGridSpec(n...  18.1 us
    ppermute x10, starting transfers between devices, send(): return lax.ppermute(x, 'seq', pairs)  16.8 us
    all_to_all x4, waiting for transfers between devices, group_swap(): lax.all_to_all(x, ALL, split_axis=0, concat_axis=0, tiled=True, axis_inde...  13.8 us
    all_to_all x2, starting transfers between devices, swap(): return lax.all_to_all(x, axis, split_axis=0, concat_axis=0, tiled=True)  8.56 us
    pallas_call x2, Pallas kernels, pair_grad(): pl.pallas_call(body, grid=(half,), in_specs=[pl.BlockSpec((step, i, c), l...  8.24 us
    pallas_call x1, Pallas kernels, finish(): pl.pallas_call(finish_kernel, grid_spec=pltpu.PrefetchScalarGridSpec(num_...  5.97 us
  transfers between devices with their start and end apart: 19, of which 14 were waited for; matrix products, arithmetic and copies ran while one was open for 1% of the time, Pallas kernels for 14%

profile of v4, /device:TPU:1, one launch (start us, length us, event | category | flops | bytes accessed | tf_op | source)
XLA Modules:
  0.0 143.6 jit_solution(1639023696882835607)
XLA Ops:
  0.6 4.4 %pair_bias.1 = (bf16[2,8,64,128]{3,2,1,0:T(8,128)(2,1)}, bf16[64,128,128]{2,1,0:T(8,128)(2,1)}) custom-call(bf16[64,128,128]{2,1,0:T(8,128)(2,1)} %x.5, f32[1,128]{1,0:T(1,128)} %bitcast.33, bf16[8,128]{1,0:T(8,128)(2,1)} %bitcast.27), custom_call_target="tpu_custom_call" | custom-call | flops 4000000000 | bytes 12000000 | tf_op jit(solution)/shard_map/pair_bias/pallas_call | solution.py:121
  5.1 7.6 %all-to-all-start = ((bf16[16,64,128]{2,1,0:T(8,128)(2,1)}), bf16[16,64,128]{2,1,0:T(8,128)(2,1)S(1)}, u32[]{:S(2)}, u32[]{:S(2)}) async-start(bf16[16,64,128]{2,1,0:T(8,128)(2,1)} %bitcast.26), calls=%async_computation | async-start | bytes 524288 | tf_op jit(solution)/shard_map/all_to_all | solution.py:516
  12.6 3.9 %project.1 = (bf16[8,4,128,128]{3,2,1,0:T(8,128)(2,1)}, f32[4,128,256]{2,1,0:T(8,128)}, f32[4,128,256]{2,1,0:T(8,128)}) custom-call(bf16[4,128,256]{2,1,0:T(8,128)(2,1)} %x_ref.5, f32[1,256]{1,0:T(1,128)} %bitcast.31, bf16[256,1024]{1,0:T(8,128)(2,1)} %w_ref.3, f32[1,256]{1,0:T(1,128)} %bitcast.30, bf16[256,256]{1,0:T(8,128)(2,1)} %wo_ref.3, ...), custom_call_target="tpu_custom_call" | custom-call | flops 3000000000 | bytes 9000000 | tf_op jit(solution)/shard_map/project/pallas_call | solution.py:88
  16.5 3.5 %all-to-all-done = bf16[16,64,128]{2,1,0:T(8,128)(2,1)S(1)} async-done(((bf16[16,64,128]{2,1,0:T(8,128)(2,1)}), bf16[16,64,128]{2,1,0:T(8,128)(2,1)S(1)}, u32[]{:S(2)}, u32[]{:S(2)}) %all-to-all-start) | async-done | bytes 262176 | tf_op jit(solution)/shard_map/all_to_all | solution.py:516
  20.1 3.6 %all-to-all-start.1 = ((bf16[8,4,128,128]{3,2,1,0:T(8,128)(2,1)}), bf16[8,4,128,128]{3,2,1,0:T(8,128)(2,1)S(1)}, u32[]{:S(2)}, u32[]{:S(2)}) async-start(bf16[8,4,128,128]{3,2,1,0:T(8,128)(2,1)} %get-tuple-element.36), calls=%async_computation.1 | async-start | bytes 2097152 | tf_op jit(solution)/shard_map/all_to_all | solution.py:475
  23.6 3.8 %collective-permute-start.2 = (bf16[2,8,64,128]{3,2,1,0:T(8,128)(2,1)S(1)}, bf16[2,8,64,128]{3,2,1,0:T(8,128)(2,1)S(1)}, u32[]{:S(2)}, u32[]{:S(2)}) collective-permute-start(bf16[2,8,64,128]{3,2,1,0:T(8,128)(2,1)S(1)} %bitcast.19), channel_id=1, source_target_pairs={{0,48},{8,56},{16,0},{24,8},{32,16},{40,24},{48,32},{56,40},{64,11... | collective-permute-start | bytes 786440 | tf_op jit(solution)/shard_map/ppermute | solution.py:487
  28.2 9.2 %collective-permute-done.2 = bf16[2,8,64,128]{3,2,1,0:T(8,128)(2,1)S(1)} collective-permute-done((bf16[2,8,64,128]{3,2,1,0:T(8,128)(2,1)S(1)}, bf16[2,8,64,128]{3,2,1,0:T(8,128)(2,1)S(1)}, u32[]{:S(2)}, u32[]{:S(2)}) %collective-permute-start.2) | collective-permute-done | bytes 262176 | tf_op jit(solution)/shard_map/ppermute | solution.py:487
  37.3 4.8 %collective-permute-done = bf16[2,8,64,128]{3,2,1,0:T(8,128)(2,1)S(1)} collective-permute-done((bf16[2,8,64,128]{3,2,1,0:T(8,128)(2,1)S(1)}, bf16[2,8,64,128]{3,2,1,0:T(8,128)(2,1)S(1)}, u32[]{:S(2)}, u32[]{:S(2)}) %collective-permute-start) | collective-permute-done | bytes 262176 | tf_op jit(solution)/shard_map/ppermute | solution.py:487
  46.5 18.1 %attention.1 = (bf16[8,4,128,128]{3,2,1,0:T(8,128)(2,1)}, bf16[8,8,64,128]{3,2,1,0:T(8,128)(2,1)}, bf16[8,8,64,128]{3,2,1,0:T(8,128)(2,1)}) custom-call(s32[9]{0:T(128)} %stack.39.place_ref, bf16[8,4,128,128]{3,2,1,0:T(8,128)(2,1)} %copy-done.2, bf16[8,8,64,128]{3,2,1,0:T(8,128)(2,1)} %copy-done.3, bf16[8,8,64,128]{3,2,1,0:T(8,128)(2,1)} %copy-done.8), custom_call_target="tpu_custom_call" | custom-call | flops 17999998976 | bytes 54000000 | tf_op jit(solution)/shard_map/attention/pallas_call | solution.py:274
  64.9 5.0 %all-to-all-start.2 = ((bf16[8,4,128,128]{3,2,1,0:T(8,128)(2,1)}), bf16[8,4,128,128]{3,2,1,0:T(8,128)(2,1)S(1)}, u32[]{:S(2)}, u32[]{:S(2)}) async-start(bf16[8,4,128,128]{3,2,1,0:T(8,128)(2,1)} %get-tuple-element.39), calls=%async_computation.2 | async-start | bytes 2097152 | tf_op jit(solution)/shard_map/all_to_all | solution.py:475
  72.6 5.4 %collective-permute-done.5 = bf16[2,8,64,128]{3,2,1,0:T(8,128)(2,1)S(1)} collective-permute-done((bf16[2,8,64,128]{3,2,1,0:T(8,128)(2,1)S(1)}, bf16[2,8,64,128]{3,2,1,0:T(8,128)(2,1)S(1)}, u32[]{:S(2)}, u32[]{:S(2)}) %collective-permute-start.5) | collective-permute-done | bytes 262176 | tf_op jit(solution)/shard_map/ppermute | solution.py:487
  78.0 2.7 %collective-permute-done.7 = bf16[2,8,64,128]{3,2,1,0:T(8,128)(2,1)S(1)} collective-permute-done((bf16[2,8,64,128]{3,2,1,0:T(8,128)(2,1)S(1)}, bf16[2,8,64,128]{3,2,1,0:T(8,128)(2,1)S(1)}, u32[]{:S(2)}, u32[]{:S(2)}) %collective-permute-start.7) | collective-permute-done | bytes 262176 | tf_op jit(solution)/shard_map/ppermute | solution.py:487
  80.7 3.2 %collective-permute-done.6 = bf16[2,8,64,128]{3,2,1,0:T(8,128)(2,1)S(1)} collective-permute-done((bf16[2,8,64,128]{3,2,1,0:T(8,128)(2,1)S(1)}, bf16[2,8,64,128]{3,2,1,0:T(8,128)(2,1)S(1)}, u32[]{:S(2)}, u32[]{:S(2)}) %collective-permute-start.6) | collective-permute-done | bytes 262176 | tf_op jit(solution)/shard_map/ppermute | solution.py:487
  85.8 3.9 %all-to-all-start.3 = ((bf16[16,64,128]{2,1,0:T(8,128)(2,1)}), bf16[16,64,128]{2,1,0:T(8,128)(2,1)S(1)}, u32[]{:S(2)}, u32[]{:S(2)}) async-start(bf16[16,64,128]{2,1,0:T(8,128)(2,1)} %bitcast.15), calls=%async_computation.3 | async-start | bytes 524288 | tf_op jit(solution)/shard_map/all_to_all | solution.py:516
  89.7 6.0 %finish.1 = (bf16[4,128,256]{2,1,0:T(8,128)(2,1)}, bf16[4,128,256]{2,1,0:T(8,128)(2,1)}, bf16[5,256,128]{2,1,0:T(8,128)(2,1)}, bf16[5,256,128]{2,1,0:T(8,128)(2,1)}) custom-call(s32[9]{0:T(128)} %stack.39.place_ref, bf16[4,128,256]{2,1,0:T(8,128)(2,1)} %x_ref.5, f32[1,256]{1,0:T(1,128)} %bitcast.32, bf16[256,1024]{1,0:T(8,128)(2,1)} %w_ref.3, ...), custom_call_target="tpu_custom_call" | custom-call | flops 5000000000 | bytes 15000000 | tf_op jit(solution)/shard_map/finish/pallas_call | solution.py:354
  97.1 4.7 %collective-permute-start.8 = (bf16[5,256,128]{2,1,0:T(8,128)(2,1)}, bf16[5,256,128]{2,1,0:T(8,128)(2,1)S(1)}, u32[]{:S(2)}, u32[]{:S(2)}) collective-permute-start(bf16[5,256,128]{2,1,0:T(8,128)(2,1)} %get-tuple-element.46), channel_id=1, source_target_pairs={{0,8},{8,0},{16,24},{24,16},{32,40},{40,32},{48,56},{56,48},{64,72... | collective-permute-start | bytes 983048 | tf_op jit(solution)/shard_map/ppermute | solution.py:487
  101.8 2.7 %pair_weight.1 = f32[8,128]{1,0:T(8,128)} custom-call(bf16[64,128,128]{2,1,0:T(8,128)(2,1)} %get-tuple-element.49.n_ref, bf16[2,8,64,128]{3,2,1,0:T(8,128)(2,1)} %bitcast.23), custom_call_target="tpu_custom_call" | custom-call | flops 2000000000 | bytes 6000000 | tf_op jit(solution)/shard_map/pair_weight/pallas_call | solution.py:396
  105.3 3.5 %all-to-all-start.4 = ((bf16[16,80,128]{2,1,0:T(8,128)(2,1)}), bf16[16,80,128]{2,1,0:T(8,128)(2,1)S(1)}, u32[]{:S(2)}, u32[]{:S(2)}) async-start(bf16[16,80,128]{2,1,0:T(8,128)(2,1)} %bitcast.17), calls=%async_computation.4 | async-start | bytes 655360 | tf_op jit(solution)/shard_map/all_to_all | solution.py:516
  108.9 4.1 %pair_grad.2.rest_0_ = bf16[64,128,128]{2,1,0:T(8,128)(2,1)} custom-call(bf16[64,128,128]{2,1,0:T(8,128)(2,1)} %x.5, f32[1,128]{1,0:T(1,128)} %bitcast.34, bf16[8,128]{1,0:T(8,128)(2,1)} %bitcast.28, bf16[2,8,64,128]{3,2,1,0:T(8,128)(2,1)} %bitcast.24), custom_call_target="tpu_custom_call" | custom-call | flops 4000000000 | bytes 12000000 | tf_op jit(solution)/shard_map/pair_grad/pallas_call | solution.py:454
  113.0 4.6 %all-to-all-done.4 = bf16[16,80,128]{2,1,0:T(8,128)(2,1)S(1)} async-done(((bf16[16,80,128]{2,1,0:T(8,128)(2,1)}), bf16[16,80,128]{2,1,0:T(8,128)(2,1)S(1)}, u32[]{:S(2)}, u32[]{:S(2)}) %all-to-all-start.4) | async-done | bytes 327712 | tf_op jit(solution)/shard_map/all_to_all | solution.py:516
  124.4 3.6 %all-to-all-start.5 = ((bf16[16,96,128]{2,1,0:T(8,128)(2,1)}), bf16[16,96,128]{2,1,0:T(8,128)(2,1)S(1)}, u32[]{:S(2)}, u32[]{:S(2)}) async-start(bf16[16,96,128]{2,1,0:T(8,128)(2,1)} %broadcast_in_dim.2), calls=%async_computation.5 | async-start | bytes 786432 | tf_op jit(solution)/shard_map/all_to_all | solution.py:516
  127.9 4.1 %pair_grad.3 = bf16[64,128,128]{2,1,0:T(8,128)(2,1)} custom-call(bf16[64,128,128]{2,1,0:T(8,128)(2,1)} %x.5, f32[1,128]{1,0:T(1,128)} %bitcast.35, bf16[8,128]{1,0:T(8,128)(2,1)} %bitcast.29, bf16[2,8,64,128]{3,2,1,0:T(8,128)(2,1)} %bitcast.25, bf16[64,128,128]{2,1,0:T(8,128)(2,1)} %pair_grad.2.rest_0_), custom_call_target="tpu_custom_call", output_to_operand_aliasing={{}: (4, {})} | custom-call | flops 4000000000 | bytes 12000000 | tf_op jit(solution)/shard_map/pair_grad/pallas_call | solution.py:454
  132.1 4.3 %all-to-all-done.5.mine_ref = bf16[16,96,128]{2,1,0:T(8,128)(2,1)S(1)} async-done(((bf16[16,96,128]{2,1,0:T(8,128)(2,1)}), bf16[16,96,128]{2,1,0:T(8,128)(2,1)S(1)}, u32[]{:S(2)}, u32[]{:S(2)}) %all-to-all-start.5) | async-done | bytes 393248 | tf_op jit(solution)/shard_map/all_to_all | solution.py:516
  136.3 4.2 %collective-permute-start.12 = (bf16[16,96,128]{2,1,0:T(8,128)(2,1)S(1)}, bf16[16,96,128]{2,1,0:T(8,128)(2,1)S(1)}, u32[]{:S(2)}, u32[]{:S(2)}) collective-permute-start(bf16[16,96,128]{2,1,0:T(8,128)(2,1)S(1)} %all-to-all-done.5.mine_ref), channel_id=1, source_target_pairs={{0,8},{8,0},{16,24},{24,16},{32,40},{40,32},{48,56},{56,48},{64,72... | collective-permute-start | bytes 1179656 | tf_op jit(solution)/shard_map/ppermute | solution.py:487
  (50 shorter events, 22.0 us)
Async XLA Ops:
  5.1 15.0 %all-to-all-start = ((bf16[16,64,128]{2,1,0:T(8,128)(2,1)}), bf16[16,64,128]{2,1,0:T(8,128)(2,1)S(1)}, u32[]{:S(2)}, u32[]{:S(2)}) async-start(bf16[16,64,128]{2,1,0:T(8,128)(2,1)} %bitcast.26), calls=%async_computation | async-start | bytes 524288 | tf_op jit(solution)/shard_map/all_to_all | solution.py:516
  20.1 22.2 %all-to-all-start.1 = ((bf16[8,4,128,128]{3,2,1,0:T(8,128)(2,1)}), bf16[8,4,128,128]{3,2,1,0:T(8,128)(2,1)S(1)}, u32[]{:S(2)}, u32[]{:S(2)}) async-start(bf16[8,4,128,128]{3,2,1,0:T(8,128)(2,1)} %get-tuple-element.36), calls=%async_computation.1 | async-start | bytes 2097152 | tf_op jit(solution)/shard_map/all_to_all | solution.py:475
  23.6 13.7 %collective-permute-start.2 = (bf16[2,8,64,128]{3,2,1,0:T(8,128)(2,1)S(1)}, bf16[2,8,64,128]{3,2,1,0:T(8,128)(2,1)S(1)}, u32[]{:S(2)}, u32[]{:S(2)}) collective-permute-start(bf16[2,8,64,128]{3,2,1,0:T(8,128)(2,1)S(1)} %bitcast.19), channel_id=1, source_target_pairs={{0,48},{8,56},{16,0},{24,8},{32,16},{40,24},{48,32},{56,40},{64,11... | collective-permute-start | bytes 786440 | tf_op jit(solution)/shard_map/ppermute | solution.py:487
  27.5 9.9 %collective-permute-start.1 = (bf16[2,8,64,128]{3,2,1,0:T(8,128)(2,1)S(1)}, bf16[2,8,64,128]{3,2,1,0:T(8,128)(2,1)S(1)}, u32[]{:S(2)}, u32[]{:S(2)}) collective-permute-start(bf16[2,8,64,128]{3,2,1,0:T(8,128)(2,1)S(1)} %bitcast.20), channel_id=1, source_target_pairs={{0,32},{8,40},{16,48},{24,56},{32,0},{40,8},{48,16},{56,24},{64,96... | collective-permute-start | bytes 786440 | tf_op jit(solution)/shard_map/ppermute | solution.py:487
  27.5 14.7 %collective-permute-start = (bf16[2,8,64,128]{3,2,1,0:T(8,128)(2,1)S(1)}, bf16[2,8,64,128]{3,2,1,0:T(8,128)(2,1)S(1)}, u32[]{:S(2)}, u32[]{:S(2)}) collective-permute-start(bf16[2,8,64,128]{3,2,1,0:T(8,128)(2,1)S(1)} %bitcast.21), channel_id=1, source_target_pairs={{0,16},{8,24},{16,32},{24,40},{32,48},{40,56},{48,0},{56,8},{64,80... | collective-permute-start | bytes 786440 | tf_op jit(solution)/shard_map/ppermute | solution.py:487
  42.3 3.2 %collective-permute-start.3 = (bf16[8,8,64,128]{3,2,1,0:T(8,128)(2,1)S(1)}, bf16[8,8,64,128]{3,2,1,0:T(8,128)(2,1)S(1)}, u32[]{:S(2)}, u32[]{:S(2)}) collective-permute-start(bf16[8,8,64,128]{3,2,1,0:T(8,128)(2,1)S(1)} %pad_maximum_fusion.own_ref), channel_id=1, source_target_pairs={{0,8},{8,0},{16,24},{24,16},{32,40},{40,32},{48,56},{56,48},{64,72... | collective-permute-start | bytes 3145736 | tf_op jit(solution)/shard_map/ppermute | solution.py:487
  64.6 5.4 %copy-start.1 = (bf16[8,8,64,128]{3,2,1,0:T(8,128)(2,1)S(1)}, bf16[8,8,64,128]{3,2,1,0:T(8,128)(2,1)}, u32[]{:S(2)}) copy-start(bf16[8,8,64,128]{3,2,1,0:T(8,128)(2,1)} %get-tuple-element.43) | copy-start | bytes 3145732
  64.6 5.4 %collective-permute-start.4 = (bf16[8,8,64,128]{3,2,1,0:T(8,128)(2,1)}, bf16[8,8,64,128]{3,2,1,0:T(8,128)(2,1)S(1)}, u32[]{:S(2)}, u32[]{:S(2)}) collective-permute-start(bf16[8,8,64,128]{3,2,1,0:T(8,128)(2,1)} %get-tuple-element.44), channel_id=1, source_target_pairs={{0,8},{8,0},{16,24},{24,16},{32,40},{40,32},{48,56},{56,48},{64,72... | collective-permute-start | bytes 3145736 | tf_op jit(solution)/shard_map/ppermute | solution.py:487
  64.9 20.9 %all-to-all-start.2 = ((bf16[8,4,128,128]{3,2,1,0:T(8,128)(2,1)}), bf16[8,4,128,128]{3,2,1,0:T(8,128)(2,1)S(1)}, u32[]{:S(2)}, u32[]{:S(2)}) async-start(bf16[8,4,128,128]{3,2,1,0:T(8,128)(2,1)} %get-tuple-element.39), calls=%async_computation.2 | async-start | bytes 2097152 | tf_op jit(solution)/shard_map/all_to_all | solution.py:475
  70.4 7.6 %collective-permute-start.5 = (bf16[2,8,64,128]{3,2,1,0:T(8,128)(2,1)S(1)}, bf16[2,8,64,128]{3,2,1,0:T(8,128)(2,1)S(1)}, u32[]{:S(2)}, u32[]{:S(2)}) collective-permute-start(bf16[2,8,64,128]{3,2,1,0:T(8,128)(2,1)S(1)} %get-tuple-element.56), channel_id=1, source_target_pairs={{0,48},{8,56},{16,0},{24,8},{32,16},{40,24},{48,32},{56,40},{64,11... | collective-permute-start | bytes 786440 | tf_op jit(solution)/shard_map/ppermute | solution.py:487
  71.3 9.4 %collective-permute-start.7 = (bf16[2,8,64,128]{3,2,1,0:T(8,128)(2,1)S(1)}, bf16[2,8,64,128]{3,2,1,0:T(8,128)(2,1)S(1)}, u32[]{:S(2)}, u32[]{:S(2)}) collective-permute-start(bf16[2,8,64,128]{3,2,1,0:T(8,128)(2,1)S(1)} %get-tuple-element.57), channel_id=1, source_target_pairs={{0,16},{8,24},{16,32},{24,40},{32,48},{40,56},{48,0},{56,8},{64,80... | collective-permute-start | bytes 786440 | tf_op jit(solution)/shard_map/ppermute | solution.py:487
  72.1 11.8 %collective-permute-start.6 = (bf16[2,8,64,128]{3,2,1,0:T(8,128)(2,1)S(1)}, bf16[2,8,64,128]{3,2,1,0:T(8,128)(2,1)S(1)}, u32[]{:S(2)}, u32[]{:S(2)}) collective-permute-start(bf16[2,8,64,128]{3,2,1,0:T(8,128)(2,1)S(1)} %get-tuple-element.58), channel_id=1, source_target_pairs={{0,32},{8,40},{16,48},{24,56},{32,0},{40,8},{48,16},{56,24},{64,96... | collective-permute-start | bytes 786440 | tf_op jit(solution)/shard_map/ppermute | solution.py:487
  85.8 3.9 %copy-start.4 = (bf16[8,4,128,128]{3,2,1,0:T(8,128)(2,1)}, bf16[8,4,128,128]{3,2,1,0:T(8,128)(2,1)S(1)}, u32[]{:S(2)}) copy-start(bf16[8,4,128,128]{3,2,1,0:T(8,128)(2,1)S(1)} %all-to-all-done.2.back_ref) | copy-start | bytes 3145732
  85.8 11.3 %all-to-all-start.3 = ((bf16[16,64,128]{2,1,0:T(8,128)(2,1)}), bf16[16,64,128]{2,1,0:T(8,128)(2,1)S(1)}, u32[]{:S(2)}, u32[]{:S(2)}) async-start(bf16[16,64,128]{2,1,0:T(8,128)(2,1)} %bitcast.15), calls=%async_computation.3 | async-start | bytes 524288 | tf_op jit(solution)/shard_map/all_to_all | solution.py:516
  97.1 4.7 %copy-start.6 = (bf16[16,64,128]{2,1,0:T(8,128)(2,1)}, bf16[16,64,128]{2,1,0:T(8,128)(2,1)S(1)}, u32[]{:S(2)}) copy-start(bf16[16,64,128]{2,1,0:T(8,128)(2,1)S(1)} %all-to-all-done.3) | copy-start | bytes 786436
  97.1 7.4 %collective-permute-start.8 = (bf16[5,256,128]{2,1,0:T(8,128)(2,1)}, bf16[5,256,128]{2,1,0:T(8,128)(2,1)S(1)}, u32[]{:S(2)}, u32[]{:S(2)}) collective-permute-start(bf16[5,256,128]{2,1,0:T(8,128)(2,1)} %get-tuple-element.46), channel_id=1, source_target_pairs={{0,8},{8,0},{16,24},{24,16},{32,40},{40,32},{48,56},{56,48},{64,72... | collective-permute-start | bytes 983048 | tf_op jit(solution)/shard_map/ppermute | solution.py:487
  105.3 12.3 %all-to-all-start.4 = ((bf16[16,80,128]{2,1,0:T(8,128)(2,1)}), bf16[16,80,128]{2,1,0:T(8,128)(2,1)S(1)}, u32[]{:S(2)}, u32[]{:S(2)}) async-start(bf16[16,80,128]{2,1,0:T(8,128)(2,1)} %bitcast.17), calls=%async_computation.4 | async-start | bytes 655360 | tf_op jit(solution)/shard_map/all_to_all | solution.py:516
  108.9 8.8 %copy-start.7 = (f32[8,128]{1,0:T(8,128)S(1)}, f32[8,128]{1,0:T(8,128)}, u32[]{:S(2)}) copy-start(f32[8,128]{1,0:T(8,128)} %pair_weight.1) | copy-start | bytes 12292
  117.7 4.0 %collective-permute-start.11 = (bf16[96,128]{1,0:T(8,128)(2,1)S(1)}, bf16[96,128]{1,0:T(8,128)(2,1)S(1)}, u32[]{:S(2)}, u32[]{:S(2)}) collective-permute-start(bf16[96,128]{1,0:T(8,128)(2,1)S(1)} %fusion), channel_id=1, source_target_pairs={{0,65},{1,64},{2,67},{3,66},{4,69},{5,68},{6,71},{7,70},{8,73},{9,... | collective-permute-start | bytes 73736 | tf_op jit(solution)/shard_map/ppermute | solution.py:534
  119.3 4.2 %collective-permute-start.10 = (bf16[96,128]{1,0:T(8,128)(2,1)S(1)}, bf16[96,128]{1,0:T(8,128)(2,1)S(1)}, u32[]{:S(2)}, u32[]{:S(2)}) collective-permute-start(bf16[96,128]{1,0:T(8,128)(2,1)S(1)} %fusion), channel_id=1, source_target_pairs={{0,64},{1,65},{2,66},{3,67},{4,68},{5,69},{6,70},{7,71},{8,72},{9,... | collective-permute-start | bytes 73736 | tf_op jit(solution)/shard_map/ppermute | solution.py:534
  119.9 3.6 %collective-permute-start.9 = (bf16[96,128]{1,0:T(8,128)(2,1)S(1)}, bf16[96,128]{1,0:T(8,128)(2,1)S(1)}, u32[]{:S(2)}, u32[]{:S(2)}) collective-permute-start(bf16[96,128]{1,0:T(8,128)(2,1)S(1)} %fusion), channel_id=1, source_target_pairs={{0,1},{1,0},{2,3},{3,2},{4,5},{5,4},{6,7},{7,6},{8,9},{9,8},{10,11... | collective-permute-start | bytes 73736 | tf_op jit(solution)/shard_map/ppermute | solution.py:534
  124.4 12.0 %all-to-all-start.5 = ((bf16[16,96,128]{2,1,0:T(8,128)(2,1)}), bf16[16,96,128]{2,1,0:T(8,128)(2,1)S(1)}, u32[]{:S(2)}, u32[]{:S(2)}) async-start(bf16[16,96,128]{2,1,0:T(8,128)(2,1)} %broadcast_in_dim.2), calls=%async_computation.5 | async-start | bytes 786432 | tf_op jit(solution)/shard_map/all_to_all | solution.py:516
  127.9 13.9 %copy-start = (s32[9]{0:T(128)S(1)}, s32[9]{0:T(128)}, u32[]{:S(2)}) copy-start(s32[9]{0:T(128)} %stack.39.place_ref) | copy-start | bytes 112
  136.3 5.5 %collective-permute-start.12 = (bf16[16,96,128]{2,1,0:T(8,128)(2,1)S(1)}, bf16[16,96,128]{2,1,0:T(8,128)(2,1)S(1)}, u32[]{:S(2)}, u32[]{:S(2)}) collective-permute-start(bf16[16,96,128]{2,1,0:T(8,128)(2,1)S(1)} %all-to-all-done.5.mine_ref), channel_id=1, source_target_pairs={{0,8},{8,0},{16,24},{24,16},{32,40},{40,32},{48,56},{56,48},{64,72... | collective-permute-start | bytes 1179656 | tf_op jit(solution)/shard_map/ppermute | solution.py:487
  (4 other events, 10.1 us)

commit v5 on v4

--- a/solution.py
+++ b/solution.py
@@ -300,15 +300,14 @@
 
 
 def finish_kernel(
-    place_ref, x_ref, gain_ref, w_ref, wo_ref, up_ref, gate_ref, dg_ref, back_ref,
-    inc_ref, dx_ref, keep_ref, away_ref, acc,
+    place_ref, x_ref, gain_ref, up_ref, gate_ref, dg_ref, back_ref,
+    proj_ref, gated_ref, keep_ref, away_ref, acc,
 ):
     step = pl.program_id(0)
     seqs, rows, width = x_ref.shape
     flat = lambda ref: ref[...].reshape(seqs * rows, width)
-    hat, inv = normalize(flat(x_ref))
-    gain = gain_ref[...]
-    normed = (hat * gain).astype(BF16)
+    hat, _ = normalize(flat(x_ref))
+    normed = (hat * gain_ref[...]).astype(BF16)
     gate = flat(gate_ref)
     d_gated = flat(dg_ref)
     up = flat(up_ref)
@@ -316,12 +315,10 @@
     pick = lambda a: jnp.concatenate([b[:, a * DH : (a + 1) * DH] for b in back], axis=1)
     attended = pick(0).astype(F32)
     gated = (gate * attended).astype(BF16)
-    inc_ref[...] = nn(gated, wo_ref[...]).astype(BF16).reshape(seqs, rows, width)
+    gated_ref[...] = gated.reshape(seqs, rows, width)
     d_pre = (d_gated * attended * gate * (1.0 - gate)).astype(BF16)
     d_proj = jnp.concatenate([pick(3), pick(1), pick(2), d_pre], axis=1)
-    grad = nt(d_proj, w_ref[...])
-    grad = normalize_grad(hat, inv, gain, grad).astype(BF16)
-    dx_ref[...] = grad.reshape(seqs, rows, width)
+    proj_ref[...] = d_proj.reshape(seqs, rows, 4 * width)
 
     @pl.when(step == 0)
     def _():
@@ -347,7 +344,7 @@
         write(away_ref, keep_ref)
 
 
-def finish(place, x, gain, w, wo, up, gate, dg, back):
+def finish(place, x, gain, up, gate, dg, back):
     s, n, c = x.shape
     whole = lambda *shape: pl.BlockSpec(shape, lambda i, p: (0,) * len(shape))
     row = pl.BlockSpec((2, n, c), lambda i, p: (i, 0, 0))
@@ -357,14 +354,17 @@
             num_scalar_prefetch=1,
             grid=(s // 2,),
             in_specs=[
-                row, whole(1, c), whole(c, 4 * c), whole(c, c), row, row, row,
+                row, whole(1, c), row, row, row,
                 pl.BlockSpec((HEADS, 2, n, 128), lambda i, p: (0, i, 0, 0)),
             ],
-            out_specs=[row, row, whole(5, 256, 128), whole(5, 256, 128)],
+            out_specs=[
+                pl.BlockSpec((2, n, 4 * c), lambda i, p: (i, 0, 0)),
+                row, whole(5, 256, 128), whole(5, 256, 128),
+            ],
             scratch_shapes=[pltpu.VMEM((c, 5 * c), F32)],
         ),
         out_shape=[
-            jax.ShapeDtypeStruct((s, n, c), BF16),
+            jax.ShapeDtypeStruct((s, n, 4 * c), BF16),
             jax.ShapeDtypeStruct((s, n, c), BF16),
             jax.ShapeDtypeStruct((5, 256, 128), BF16),
             jax.ShapeDtypeStruct((5, 256, 128), BF16),
@@ -372,14 +372,43 @@
         compiler_params=params(),
         cost_estimate=cost(5),
         name="finish",
-    )(place, x, gain, w, wo, up, gate, dg, back)
+    )(place, x, gain, up, gate, dg, back)
+
+
+def input_kernel(x_ref, gain_ref, w_ref, wo_ref, proj_ref, gated_ref, inc_ref, dx_ref):
+    seqs, rows, width = x_ref.shape
+    flat = lambda ref: ref[...].reshape(seqs * rows, ref.shape[-1])
+    inc_ref[...] = nn(flat(gated_ref), wo_ref[...]).astype(BF16).reshape(x_ref.shape)
+    hat, inv = normalize(flat(x_ref))
+    grad = nt(flat(proj_ref), w_ref[...])
+    grad = normalize_grad(hat, inv, gain_ref[...], grad).astype(BF16)
+    dx_ref[...] = grad.reshape(x_ref.shape)
+
+
+def input_grad(x, gain, w, wo, d_proj, gated):
+    s, n, c = x.shape
+    whole = lambda *shape: pl.BlockSpec(shape, lambda i: (0,) * len(shape))
+    row = pl.BlockSpec((2, n, c), lambda i: (i, 0, 0))
+    return pl.pallas_call(
+        input_kernel,
+        grid=(s // 2,),
+        in_specs=[
+            row, whole(1, c), whole(c, 4 * c), whole(c, c),
+            pl.BlockSpec((2, n, 4 * c), lambda i: (i, 0, 0)), row,
+        ],
+        out_specs=[row, row],
+        out_shape=[jax.ShapeDtypeStruct((s, n, c), BF16)] * 2,
+        compiler_params=params(),
+        cost_estimate=cost(3),
+        name="input_grad",
+    )(x, gain, w, wo, d_proj, gated)
 
 
 def pair_weight_kernel(n_ref, db_ref, dw_ref, tmp):
     tmp[...] = db_ref[0].astype(F32) + db_ref[1].astype(F32)
-    total = jnp.zeros((HEADS, 128), F32)
-    for j in range(n_ref.shape[0]):
-        total = total + nn(tmp[:, j, :].astype(BF16), n_ref[j])
+    rows = n_ref.shape[0]
+    left = jnp.concatenate([tmp[:, j, :].astype(BF16) for j in range(rows)], axis=1)
+    total = nn(left, n_ref[...].reshape(rows * 128, 128))
 
     @pl.when(pl.program_id(0) == 0)
     def _():
@@ -526,20 +555,49 @@
     return pairs
 
 
+def add_kernel(a_ref, b_ref, out_ref):
+    out_ref[...] = (a_ref[...].astype(F32) + b_ref[...].astype(F32)).astype(BF16)
+
+
+def add_halves(a, b):
+    return pl.pallas_call(
+        add_kernel,
+        out_shape=jax.ShapeDtypeStruct(a.shape, BF16),
+        compiler_params=pltpu.CompilerParams(vmem_limit_bytes=8 * 1024 * 1024),
+        cost_estimate=cost(1),
+        name="add_halves",
+    )(a, b)
+
+
+def spread_kernel(a_ref, b_ref, c_ref, d_ref, out_ref):
+    near = a_ref[...].astype(F32) + b_ref[...].astype(F32)
+    far = c_ref[...].astype(F32) + d_ref[...].astype(F32)
+    total = (near + far).astype(BF16)
+    for i in range(out_ref.shape[0]):
+        out_ref[i] = total
+
+
+def spread_sum(*parts):
+    return pl.pallas_call(
+        spread_kernel,
+        out_shape=jax.ShapeDtypeStruct((16,) + parts[0].shape, BF16),
+        compiler_params=pltpu.CompilerParams(vmem_limit_bytes=8 * 1024 * 1024),
+        cost_estimate=cost(1),
+        name="spread_sum",
+    )(*parts)
+
+
 def sum_layers(part, extra):
     part = jnp.sum(part.astype(F32), axis=0)
     part = jnp.concatenate([part, jnp.pad(extra, ((0, 8), (0, 0)))])
     low = part.astype(BF16)
-    for k in (1, 2, 3):
-        part = part + lax.ppermute(low, ALL, across(k)).astype(F32)
-    part = part.astype(BF16)
-    return group_swap(jnp.broadcast_to(part[None], (16,) + part.shape), LAYERS)
+    parts = [low] + [lax.ppermute(low, ALL, across(k)) for k in (1, 2, 3)]
+    return group_swap(spread_sum(*parts), LAYERS)
 
 
 def unpack_kernel(place_ref, mine_ref, other_ref, dw_ref, dwo_ref, dwb_ref):
-    dwb_ref[...] = sum(
-        ref[i, 80:96].astype(F32) for ref in (mine_ref, other_ref) for i in range(16)
-    )[0:8]
+    column = lambda ref: sum(ref[i, 80:96].astype(F32) for i in range(16))
+    dwb_ref[...] = (column(mine_ref) + column(other_ref))[0:8]
 
     def write(low, high):
         get = lambda ref, b: jnp.concatenate(
@@ -614,17 +672,17 @@
     for turn in (1, 2, 3):
         total = total + send(low[2 * turn : 2 * turn + 2], along(-turn)).astype(F32)
     d_bias = group_swap(total.astype(BF16).reshape(16, 64, 128), COLUMNS).reshape(2, 8, 64, 128)
-    inc, dx, keep, away = finish(place, x, gain, w, wo, up, gate, dg, back)
+    d_proj, gated, keep, away = finish(place, x, gain, up, gate, dg, back)
     d_bias, away = lax.optimization_barrier((d_bias, away))
-    part = (keep.astype(F32) + send(away, OTHER).astype(F32)).astype(BF16)
-    part = part.reshape(16, 80, 128)
+    part = add_halves(keep, send(away, OTHER)).reshape(16, 80, 128)
     dwb = pair_weight(normed, d_bias)
     part = group_swap(part, LAYERS)
     begun = pair_grad(pair, pair_gain, wt, d_bias)
     part, begun = lax.optimization_barrier((part, begun))
     mine = sum_layers(part, dwb)
     d_pair = pair_grad(pair, pair_gain, wt, d_bias, begun)
-    mine, d_pair = lax.optimization_barrier((mine, d_pair))
+    inc, dx = input_grad(x, gain, w, wo, d_proj, gated)
+    mine, d_pair, inc, dx = lax.optimization_barrier((mine, d_pair, inc, dx))
     dw, dwo, dwb = unpack(place, mine, send(mine, OTHER))
     return inc, dx, d_pair, dw, dwo, dwb.T
 

time: 144 us -> 145 us (level)
  Pallas kernels: 45 us -> 48.9 us
  waiting for transfers between devices: 45.7 us -> 43.6 us
    pallas_call x0 -> x3, Pallas kernels: none -> 4.65 us  [the longest x1 3.07 us: input_grad(): pl.pallas_call(input_kernel, grid=(s // 2,), in_specs=[row, whole(1, c),...]
    ppermute x3, waiting for transfers between devices: 2.54 us -> 0.01 us  [sum_layers(): parts = [low] + [lax.ppermute(low, ALL, across(k)) for k in (1, 2, 3)]]
  transfers between devices with their start and end apart: 19 -> 19, of which waited for: 14 -> 12; matrix products, arithmetic and copies ran while one was open for 1% -> 2% of each run, Pallas kernels for 14% -> 16%
where the time goes in v5:
time: 145 us; the launch traced here: 144 us
  Pallas kernels  48.9 us (34%)
  starting transfers between devices  46.7 us (32%)
  waiting for transfers between devices  43.6 us (30%)
  other arithmetic  2.15 us (1%)
  local copies, waits for them, and re-layouts  1.72 us (1%)
    ppermute x10, waiting for transfers between devices, send(): return lax.ppermute(x, 'seq', pairs)  28.3 us
    all_to_all x4, starting transfers between devices, group_swap(): lax.all_to_all(x, ALL, split_axis=0, concat_axis=0, tiled=True, axis_inde...  18.6 us
    pallas_call x1, Pallas kernels, attention(): pl.pallas_call(attention_kernel, grid_spec=pltpu.PrefetchScalarGridSpec(n...  18.1 us
    ppermute x10, starting transfers between devices, send(): return lax.ppermute(x, 'seq', pairs)  16.2 us
    all_to_all x4, waiting for transfers between devices, group_swap(): lax.all_to_all(x, ALL, split_axis=0, concat_axis=0, tiled=True, axis_inde...  14.3 us
    all_to_all x2, starting transfers between devices, swap(): return lax.all_to_all(x, axis, split_axis=0, concat_axis=0, tiled=True)  8.56 us
    pallas_call x2, Pallas kernels, pair_grad(): pl.pallas_call(body, grid=(half,), in_specs=[pl.BlockSpec((step, i, c), l...  8.24 us
    pallas_call x1, Pallas kernels, finish(): pl.pallas_call(finish_kernel, grid_spec=pltpu.PrefetchScalarGridSpec(num_...  5.31 us
  transfers between devices with their start and end apart: 19, of which 12 were waited for; matrix products, arithmetic and copies ran while one was open for 2% of the time, Pallas kernels for 16%

profile of v5, /device:TPU:1, one launch (start us, length us, event | category | flops | bytes accessed | tf_op | source)
XLA Modules:
  0.0 143.8 jit_solution(12283624880933443353)
XLA Ops:
  0.6 4.4 %pair_bias.1 = (bf16[2,8,64,128]{3,2,1,0:T(8,128)(2,1)}, bf16[64,128,128]{2,1,0:T(8,128)(2,1)}) custom-call(bf16[64,128,128]{2,1,0:T(8,128)(2,1)} %x.5, f32[1,128]{1,0:T(1,128)} %bitcast.34, bf16[8,128]{1,0:T(8,128)(2,1)} %bitcast.27), custom_call_target="tpu_custom_call" | custom-call | flops 4000000000 | bytes 12000000 | tf_op jit(solution)/shard_map/pair_bias/pallas_call | solution.py:121
  5.1 7.6 %all-to-all-start = ((bf16[16,64,128]{2,1,0:T(8,128)(2,1)}), bf16[16,64,128]{2,1,0:T(8,128)(2,1)S(1)}, u32[]{:S(2)}, u32[]{:S(2)}) async-start(bf16[16,64,128]{2,1,0:T(8,128)(2,1)} %bitcast.26), calls=%async_computation | async-start | bytes 524288 | tf_op jit(solution)/shard_map/all_to_all | solution.py:545
  12.7 3.9 %project.1 = (bf16[8,4,128,128]{3,2,1,0:T(8,128)(2,1)}, f32[4,128,256]{2,1,0:T(8,128)}, f32[4,128,256]{2,1,0:T(8,128)}) custom-call(bf16[4,128,256]{2,1,0:T(8,128)(2,1)} %x_ref.7, f32[1,256]{1,0:T(1,128)} %bitcast.31, bf16[256,1024]{1,0:T(8,128)(2,1)} %w_ref.3, f32[1,256]{1,0:T(1,128)} %bitcast.30, bf16[256,256]{1,0:T(8,128)(2,1)} %wo_ref.3, ...), custom_call_target="tpu_custom_call" | custom-call | flops 3000000000 | bytes 9000000 | tf_op jit(solution)/shard_map/project/pallas_call | solution.py:88
  16.5 3.5 %all-to-all-done = bf16[16,64,128]{2,1,0:T(8,128)(2,1)S(1)} async-done(((bf16[16,64,128]{2,1,0:T(8,128)(2,1)}), bf16[16,64,128]{2,1,0:T(8,128)(2,1)S(1)}, u32[]{:S(2)}, u32[]{:S(2)}) %all-to-all-start) | async-done | bytes 262176 | tf_op jit(solution)/shard_map/all_to_all | solution.py:545
  20.1 3.6 %all-to-all-start.1 = ((bf16[8,4,128,128]{3,2,1,0:T(8,128)(2,1)}), bf16[8,4,128,128]{3,2,1,0:T(8,128)(2,1)S(1)}, u32[]{:S(2)}, u32[]{:S(2)}) async-start(bf16[8,4,128,128]{3,2,1,0:T(8,128)(2,1)} %get-tuple-element.40), calls=%async_computation.1 | async-start | bytes 2097152 | tf_op jit(solution)/shard_map/all_to_all | solution.py:504
  23.6 3.8 %collective-permute-start.2 = (bf16[2,8,64,128]{3,2,1,0:T(8,128)(2,1)S(1)}, bf16[2,8,64,128]{3,2,1,0:T(8,128)(2,1)S(1)}, u32[]{:S(2)}, u32[]{:S(2)}) collective-permute-start(bf16[2,8,64,128]{3,2,1,0:T(8,128)(2,1)S(1)} %bitcast.19), channel_id=1, source_target_pairs={{0,48},{8,56},{16,0},{24,8},{32,16},{40,24},{48,32},{56,40},{64,11... | collective-permute-start | bytes 786440 | tf_op jit(solution)/shard_map/ppermute | solution.py:516
  28.2 9.2 %collective-permute-done.2 = bf16[2,8,64,128]{3,2,1,0:T(8,128)(2,1)S(1)} collective-permute-done((bf16[2,8,64,128]{3,2,1,0:T(8,128)(2,1)S(1)}, bf16[2,8,64,128]{3,2,1,0:T(8,128)(2,1)S(1)}, u32[]{:S(2)}, u32[]{:S(2)}) %collective-permute-start.2) | collective-permute-done | bytes 262176 | tf_op jit(solution)/shard_map/ppermute | solution.py:516
  37.3 4.8 %collective-permute-done = bf16[2,8,64,128]{3,2,1,0:T(8,128)(2,1)S(1)} collective-permute-done((bf16[2,8,64,128]{3,2,1,0:T(8,128)(2,1)S(1)}, bf16[2,8,64,128]{3,2,1,0:T(8,128)(2,1)S(1)}, u32[]{:S(2)}, u32[]{:S(2)}) %collective-permute-start) | collective-permute-done | bytes 262176 | tf_op jit(solution)/shard_map/ppermute | solution.py:516
  46.5 18.1 %attention.1 = (bf16[8,4,128,128]{3,2,1,0:T(8,128)(2,1)}, bf16[8,8,64,128]{3,2,1,0:T(8,128)(2,1)}, bf16[8,8,64,128]{3,2,1,0:T(8,128)(2,1)}) custom-call(s32[9]{0:T(128)} %stack.39.place_ref, bf16[8,4,128,128]{3,2,1,0:T(8,128)(2,1)} %copy-done.3, bf16[8,8,64,128]{3,2,1,0:T(8,128)(2,1)} %copy-done.4, bf16[8,8,64,128]{3,2,1,0:T(8,128)(2,1)} %copy-done.7), custom_call_target="tpu_custom_call" | custom-call | flops 17999998976 | bytes 54000000 | tf_op jit(solution)/shard_map/attention/pallas_call | solution.py:274
  64.9 5.0 %all-to-all-start.2 = ((bf16[8,4,128,128]{3,2,1,0:T(8,128)(2,1)}), bf16[8,4,128,128]{3,2,1,0:T(8,128)(2,1)S(1)}, u32[]{:S(2)}, u32[]{:S(2)}) async-start(bf16[8,4,128,128]{3,2,1,0:T(8,128)(2,1)} %get-tuple-element.43), calls=%async_computation.2 | async-start | bytes 2097152 | tf_op jit(solution)/shard_map/all_to_all | solution.py:504
  72.6 5.4 %collective-permute-done.5 = bf16[2,8,64,128]{3,2,1,0:T(8,128)(2,1)S(1)} collective-permute-done((bf16[2,8,64,128]{3,2,1,0:T(8,128)(2,1)S(1)}, bf16[2,8,64,128]{3,2,1,0:T(8,128)(2,1)S(1)}, u32[]{:S(2)}, u32[]{:S(2)}) %collective-permute-start.5) | collective-permute-done | bytes 262176 | tf_op jit(solution)/shard_map/ppermute | solution.py:516
  78.0 2.7 %collective-permute-done.7 = bf16[2,8,64,128]{3,2,1,0:T(8,128)(2,1)S(1)} collective-permute-done((bf16[2,8,64,128]{3,2,1,0:T(8,128)(2,1)S(1)}, bf16[2,8,64,128]{3,2,1,0:T(8,128)(2,1)S(1)}, u32[]{:S(2)}, u32[]{:S(2)}) %collective-permute-start.7) | collective-permute-done | bytes 262176 | tf_op jit(solution)/shard_map/ppermute | solution.py:516
  80.7 3.2 %collective-permute-done.6 = bf16[2,8,64,128]{3,2,1,0:T(8,128)(2,1)S(1)} collective-permute-done((bf16[2,8,64,128]{3,2,1,0:T(8,128)(2,1)S(1)}, bf16[2,8,64,128]{3,2,1,0:T(8,128)(2,1)S(1)}, u32[]{:S(2)}, u32[]{:S(2)}) %collective-permute-start.6) | collective-permute-done | bytes 262176 | tf_op jit(solution)/shard_map/ppermute | solution.py:516
  85.8 3.9 %all-to-all-start.3 = ((bf16[16,64,128]{2,1,0:T(8,128)(2,1)}), bf16[16,64,128]{2,1,0:T(8,128)(2,1)S(1)}, u32[]{:S(2)}, u32[]{:S(2)}) async-start(bf16[16,64,128]{2,1,0:T(8,128)(2,1)} %bitcast.15), calls=%async_computation.3 | async-start | bytes 524288 | tf_op jit(solution)/shard_map/all_to_all | solution.py:545
  89.7 5.3 %finish.1 = (bf16[4,128,1024]{2,1,0:T(8,128)(2,1)}, bf16[4,128,256]{2,1,0:T(8,128)(2,1)}, bf16[5,256,128]{2,1,0:T(8,128)(2,1)}, bf16[5,256,128]{2,1,0:T(8,128)(2,1)}) custom-call(s32[9]{0:T(128)} %stack.39.place_ref, bf16[4,128,256]{2,1,0:T(8,128)(2,1)} %x_ref.7, f32[1,256]{1,0:T(1,128)} %bitcast.32, bf16[4,128,256]{2,1,0:T(8,128)(2,1)} %up_ref.3, ...), custom_call_target="tpu_custom_call" | custom-call | flops 5000000000 | bytes 15000000 | tf_op jit(solution)/shard_map/finish/pallas_call | solution.py:351
  97.1 4.7 %collective-permute-start.8 = (bf16[5,256,128]{2,1,0:T(8,128)(2,1)}, bf16[5,256,128]{2,1,0:T(8,128)(2,1)S(1)}, u32[]{:S(2)}, u32[]{:S(2)}) collective-permute-start(bf16[5,256,128]{2,1,0:T(8,128)(2,1)} %get-tuple-element.48), channel_id=1, source_target_pairs={{0,8},{8,0},{16,24},{24,16},{32,40},{40,32},{48,56},{56,48},{64,72... | collective-permute-start | bytes 983048 | tf_op jit(solution)/shard_map/ppermute | solution.py:516
  105.8 3.5 %all-to-all-start.4 = ((bf16[16,80,128]{2,1,0:T(8,128)(2,1)}), bf16[16,80,128]{2,1,0:T(8,128)(2,1)S(1)}, u32[]{:S(2)}, u32[]{:S(2)}) async-start(bf16[16,80,128]{2,1,0:T(8,128)(2,1)} %bitcast.17), calls=%async_computation.4 | async-start | bytes 655360 | tf_op jit(solution)/shard_map/all_to_all | solution.py:545
  109.4 4.1 %pair_grad.2.rest_0_ = bf16[64,128,128]{2,1,0:T(8,128)(2,1)} custom-call(bf16[64,128,128]{2,1,0:T(8,128)(2,1)} %x.5, f32[1,128]{1,0:T(1,128)} %bitcast.35, bf16[8,128]{1,0:T(8,128)(2,1)} %bitcast.28, bf16[2,8,64,128]{3,2,1,0:T(8,128)(2,1)} %bitcast.24), custom_call_target="tpu_custom_call" | custom-call | flops 4000000000 | bytes 12000000 | tf_op jit(solution)/shard_map/pair_grad/pallas_call | solution.py:483
  113.5 4.6 %all-to-all-done.4 = bf16[16,80,128]{2,1,0:T(8,128)(2,1)S(1)} async-done(((bf16[16,80,128]{2,1,0:T(8,128)(2,1)}), bf16[16,80,128]{2,1,0:T(8,128)(2,1)S(1)}, u32[]{:S(2)}, u32[]{:S(2)}) %all-to-all-start.4) | async-done | bytes 327712 | tf_op jit(solution)/shard_map/all_to_all | solution.py:545
  121.5 3.1 %input_grad.1 = (bf16[4,128,256]{2,1,0:T(8,128)(2,1)}, bf16[4,128,256]{2,1,0:T(8,128)(2,1)}) custom-call(bf16[4,128,256]{2,1,0:T(8,128)(2,1)} %x_ref.7, f32[1,256]{1,0:T(1,128)} %bitcast.33, bf16[256,1024]{1,0:T(8,128)(2,1)} %w_ref.3, bf16[256,256]{1,0:T(8,128)(2,1)} %wo_ref.3, bf16[4,128,1024]{2,1,0:T(8,128)(2,1)} %get-tuple-element.53.proj_ref, ...), custom_call_target="tpu_custom_call" | custom-call | flops 3000000000 | bytes 9000000 | tf_op jit(solution)/shard_map/input_grad/pallas_call | solution.py:392
  125.4 3.6 %all-to-all-start.5 = ((bf16[16,96,128]{2,1,0:T(8,128)(2,1)}), bf16[16,96,128]{2,1,0:T(8,128)(2,1)S(1)}, u32[]{:S(2)}, u32[]{:S(2)}) async-start(bf16[16,96,128]{2,1,0:T(8,128)(2,1)} %spread_sum.1), calls=%async_computation.5 | async-start | bytes 786432 | tf_op jit(solution)/shard_map/all_to_all | solution.py:545
  129.0 4.1 %pair_grad.3 = bf16[64,128,128]{2,1,0:T(8,128)(2,1)} custom-call(bf16[64,128,128]{2,1,0:T(8,128)(2,1)} %x.5, f32[1,128]{1,0:T(1,128)} %bitcast.36, bf16[8,128]{1,0:T(8,128)(2,1)} %bitcast.29, bf16[2,8,64,128]{3,2,1,0:T(8,128)(2,1)} %bitcast.25, bf16[64,128,128]{2,1,0:T(8,128)(2,1)} %pair_grad.2.rest_0_), custom_call_target="tpu_custom_call", output_to_operand_aliasing={{}: (4, {})} | custom-call | flops 4000000000 | bytes 12000000 | tf_op jit(solution)/shard_map/pair_grad/pallas_call | solution.py:483
  133.1 4.1 %all-to-all-done.5.mine_ref = bf16[16,96,128]{2,1,0:T(8,128)(2,1)S(1)} async-done(((bf16[16,96,128]{2,1,0:T(8,128)(2,1)}), bf16[16,96,128]{2,1,0:T(8,128)(2,1)S(1)}, u32[]{:S(2)}, u32[]{:S(2)}) %all-to-all-start.5) | async-done | bytes 393248 | tf_op jit(solution)/shard_map/all_to_all | solution.py:545
  137.2 3.6 %collective-permute-start.12 = (bf16[16,96,128]{2,1,0:T(8,128)(2,1)S(1)}, bf16[16,96,128]{2,1,0:T(8,128)(2,1)S(1)}, u32[]{:S(2)}, u32[]{:S(2)}) collective-permute-start(bf16[16,96,128]{2,1,0:T(8,128)(2,1)S(1)} %all-to-all-done.5.mine_ref), channel_id=1, source_target_pairs={{0,8},{8,0},{16,24},{24,16},{32,40},{40,32},{48,56},{56,48},{64,72... | collective-permute-start | bytes 1179656 | tf_op jit(solution)/shard_map/ppermute | solution.py:516
  (49 shorter events, 23.3 us)
Async XLA Ops:
  5.1 15.0 %all-to-all-start = ((bf16[16,64,128]{2,1,0:T(8,128)(2,1)}), bf16[16,64,128]{2,1,0:T(8,128)(2,1)S(1)}, u32[]{:S(2)}, u32[]{:S(2)}) async-start(bf16[16,64,128]{2,1,0:T(8,128)(2,1)} %bitcast.26), calls=%async_computation | async-start | bytes 524288 | tf_op jit(solution)/shard_map/all_to_all | solution.py:545
  20.1 22.2 %all-to-all-start.1 = ((bf16[8,4,128,128]{3,2,1,0:T(8,128)(2,1)}), bf16[8,4,128,128]{3,2,1,0:T(8,128)(2,1)S(1)}, u32[]{:S(2)}, u32[]{:S(2)}) async-start(bf16[8,4,128,128]{3,2,1,0:T(8,128)(2,1)} %get-tuple-element.40), calls=%async_computation.1 | async-start | bytes 2097152 | tf_op jit(solution)/shard_map/all_to_all | solution.py:504
  23.6 13.7 %collective-permute-start.2 = (bf16[2,8,64,128]{3,2,1,0:T(8,128)(2,1)S(1)}, bf16[2,8,64,128]{3,2,1,0:T(8,128)(2,1)S(1)}, u32[]{:S(2)}, u32[]{:S(2)}) collective-permute-start(bf16[2,8,64,128]{3,2,1,0:T(8,128)(2,1)S(1)} %bitcast.19), channel_id=1, source_target_pairs={{0,48},{8,56},{16,0},{24,8},{32,16},{40,24},{48,32},{56,40},{64,11... | collective-permute-start | bytes 786440 | tf_op jit(solution)/shard_map/ppermute | solution.py:516
  27.5 9.9 %collective-permute-start.1 = (bf16[2,8,64,128]{3,2,1,0:T(8,128)(2,1)S(1)}, bf16[2,8,64,128]{3,2,1,0:T(8,128)(2,1)S(1)}, u32[]{:S(2)}, u32[]{:S(2)}) collective-permute-start(bf16[2,8,64,128]{3,2,1,0:T(8,128)(2,1)S(1)} %bitcast.20), channel_id=1, source_target_pairs={{0,32},{8,40},{16,48},{24,56},{32,0},{40,8},{48,16},{56,24},{64,96... | collective-permute-start | bytes 786440 | tf_op jit(solution)/shard_map/ppermute | solution.py:516
  27.5 14.7 %collective-permute-start = (bf16[2,8,64,128]{3,2,1,0:T(8,128)(2,1)S(1)}, bf16[2,8,64,128]{3,2,1,0:T(8,128)(2,1)S(1)}, u32[]{:S(2)}, u32[]{:S(2)}) collective-permute-start(bf16[2,8,64,128]{3,2,1,0:T(8,128)(2,1)S(1)} %bitcast.21), channel_id=1, source_target_pairs={{0,16},{8,24},{16,32},{24,40},{32,48},{40,56},{48,0},{56,8},{64,80... | collective-permute-start | bytes 786440 | tf_op jit(solution)/shard_map/ppermute | solution.py:516
  42.3 3.3 %copy-start.4 = (bf16[8,8,64,128]{3,2,1,0:T(8,128)(2,1)}, bf16[8,8,64,128]{3,2,1,0:T(8,128)(2,1)S(1)}, u32[]{:S(2)}) copy-start(bf16[8,8,64,128]{3,2,1,0:T(8,128)(2,1)S(1)} %pad_maximum_fusion.own_ref) | copy-start | bytes 3145732
  42.3 3.2 %collective-permute-start.3 = (bf16[8,8,64,128]{3,2,1,0:T(8,128)(2,1)S(1)}, bf16[8,8,64,128]{3,2,1,0:T(8,128)(2,1)S(1)}, u32[]{:S(2)}, u32[]{:S(2)}) collective-permute-start(bf16[8,8,64,128]{3,2,1,0:T(8,128)(2,1)S(1)} %pad_maximum_fusion.own_ref), channel_id=1, source_target_pairs={{0,8},{8,0},{16,24},{24,16},{32,40},{40,32},{48,56},{56,48},{64,72... | collective-permute-start | bytes 3145736 | tf_op jit(solution)/shard_map/ppermute | solution.py:516
  64.6 5.4 %copy-start.2 = (bf16[8,8,64,128]{3,2,1,0:T(8,128)(2,1)S(1)}, bf16[8,8,64,128]{3,2,1,0:T(8,128)(2,1)}, u32[]{:S(2)}) copy-start(bf16[8,8,64,128]{3,2,1,0:T(8,128)(2,1)} %get-tuple-element.45) | copy-start | bytes 3145732
  64.6 5.4 %collective-permute-start.4 = (bf16[8,8,64,128]{3,2,1,0:T(8,128)(2,1)}, bf16[8,8,64,128]{3,2,1,0:T(8,128)(2,1)S(1)}, u32[]{:S(2)}, u32[]{:S(2)}) collective-permute-start(bf16[8,8,64,128]{3,2,1,0:T(8,128)(2,1)} %get-tuple-element.46), channel_id=1, source_target_pairs={{0,8},{8,0},{16,24},{24,16},{32,40},{40,32},{48,56},{56,48},{64,72... | collective-permute-start | bytes 3145736 | tf_op jit(solution)/shard_map/ppermute | solution.py:516
  64.9 20.9 %all-to-all-start.2 = ((bf16[8,4,128,128]{3,2,1,0:T(8,128)(2,1)}), bf16[8,4,128,128]{3,2,1,0:T(8,128)(2,1)S(1)}, u32[]{:S(2)}, u32[]{:S(2)}) async-start(bf16[8,4,128,128]{3,2,1,0:T(8,128)(2,1)} %get-tuple-element.43), calls=%async_computation.2 | async-start | bytes 2097152 | tf_op jit(solution)/shard_map/all_to_all | solution.py:504
  70.4 7.6 %collective-permute-start.5 = (bf16[2,8,64,128]{3,2,1,0:T(8,128)(2,1)S(1)}, bf16[2,8,64,128]{3,2,1,0:T(8,128)(2,1)S(1)}, u32[]{:S(2)}, u32[]{:S(2)}) collective-permute-start(bf16[2,8,64,128]{3,2,1,0:T(8,128)(2,1)S(1)} %get-tuple-element.64), channel_id=1, source_target_pairs={{0,48},{8,56},{16,0},{24,8},{32,16},{40,24},{48,32},{56,40},{64,11... | collective-permute-start | bytes 786440 | tf_op jit(solution)/shard_map/ppermute | solution.py:516
  71.3 9.4 %collective-permute-start.7 = (bf16[2,8,64,128]{3,2,1,0:T(8,128)(2,1)S(1)}, bf16[2,8,64,128]{3,2,1,0:T(8,128)(2,1)S(1)}, u32[]{:S(2)}, u32[]{:S(2)}) collective-permute-start(bf16[2,8,64,128]{3,2,1,0:T(8,128)(2,1)S(1)} %get-tuple-element.65), channel_id=1, source_target_pairs={{0,16},{8,24},{16,32},{24,40},{32,48},{40,56},{48,0},{56,8},{64,80... | collective-permute-start | bytes 786440 | tf_op jit(solution)/shard_map/ppermute | solution.py:516
  72.1 11.8 %collective-permute-start.6 = (bf16[2,8,64,128]{3,2,1,0:T(8,128)(2,1)S(1)}, bf16[2,8,64,128]{3,2,1,0:T(8,128)(2,1)S(1)}, u32[]{:S(2)}, u32[]{:S(2)}) collective-permute-start(bf16[2,8,64,128]{3,2,1,0:T(8,128)(2,1)S(1)} %get-tuple-element.66), channel_id=1, source_target_pairs={{0,32},{8,40},{16,48},{24,56},{32,0},{40,8},{48,16},{56,24},{64,96... | collective-permute-start | bytes 786440 | tf_op jit(solution)/shard_map/ppermute | solution.py:516
  85.8 3.9 %copy-start.5 = (bf16[8,4,128,128]{3,2,1,0:T(8,128)(2,1)}, bf16[8,4,128,128]{3,2,1,0:T(8,128)(2,1)S(1)}, u32[]{:S(2)}) copy-start(bf16[8,4,128,128]{3,2,1,0:T(8,128)(2,1)S(1)} %all-to-all-done.2.back_ref) | copy-start | bytes 3145732
  85.8 11.3 %all-to-all-start.3 = ((bf16[16,64,128]{2,1,0:T(8,128)(2,1)}), bf16[16,64,128]{2,1,0:T(8,128)(2,1)S(1)}, u32[]{:S(2)}, u32[]{:S(2)}) async-start(bf16[16,64,128]{2,1,0:T(8,128)(2,1)} %bitcast.15), calls=%async_computation.3 | async-start | bytes 524288 | tf_op jit(solution)/shard_map/all_to_all | solution.py:545
  97.1 4.7 %copy-start.6 = (bf16[16,64,128]{2,1,0:T(8,128)(2,1)}, bf16[16,64,128]{2,1,0:T(8,128)(2,1)S(1)}, u32[]{:S(2)}) copy-start(bf16[16,64,128]{2,1,0:T(8,128)(2,1)S(1)} %all-to-all-done.3) | copy-start | bytes 786436
  97.1 7.9 %collective-permute-start.8 = (bf16[5,256,128]{2,1,0:T(8,128)(2,1)}, bf16[5,256,128]{2,1,0:T(8,128)(2,1)S(1)}, u32[]{:S(2)}, u32[]{:S(2)}) collective-permute-start(bf16[5,256,128]{2,1,0:T(8,128)(2,1)} %get-tuple-element.48), channel_id=1, source_target_pairs={{0,8},{8,0},{16,24},{24,16},{32,40},{40,32},{48,56},{56,48},{64,72... | collective-permute-start | bytes 983048 | tf_op jit(solution)/shard_map/ppermute | solution.py:516
  105.8 12.3 %all-to-all-start.4 = ((bf16[16,80,128]{2,1,0:T(8,128)(2,1)}), bf16[16,80,128]{2,1,0:T(8,128)(2,1)S(1)}, u32[]{:S(2)}, u32[]{:S(2)}) async-start(bf16[16,80,128]{2,1,0:T(8,128)(2,1)} %bitcast.17), calls=%async_computation.4 | async-start | bytes 655360 | tf_op jit(solution)/shard_map/all_to_all | solution.py:545
  118.2 6.4 %collective-permute-start.11 = (bf16[96,128]{1,0:T(8,128)(2,1)S(1)}, bf16[96,128]{1,0:T(8,128)(2,1)S(1)}, u32[]{:S(2)}, u32[]{:S(2)}) collective-permute-start(bf16[96,128]{1,0:T(8,128)(2,1)S(1)} %fusion.1.a_ref), channel_id=1, source_target_pairs={{0,65},{1,64},{2,67},{3,66},{4,69},{5,68},{6,71},{7,70},{8,73},{9,... | collective-permute-start | bytes 73736 | tf_op jit(solution)/shard_map/ppermute | solution.py:594
  119.2 5.4 %collective-permute-start.10 = (bf16[96,128]{1,0:T(8,128)(2,1)S(1)}, bf16[96,128]{1,0:T(8,128)(2,1)S(1)}, u32[]{:S(2)}, u32[]{:S(2)}) collective-permute-start(bf16[96,128]{1,0:T(8,128)(2,1)S(1)} %fusion.1.a_ref), channel_id=1, source_target_pairs={{0,64},{1,65},{2,66},{3,67},{4,68},{5,69},{6,70},{7,71},{8,72},{9,... | collective-permute-start | bytes 73736 | tf_op jit(solution)/shard_map/ppermute | solution.py:594
  120.3 4.3 %collective-permute-start.9 = (bf16[96,128]{1,0:T(8,128)(2,1)S(1)}, bf16[96,128]{1,0:T(8,128)(2,1)S(1)}, u32[]{:S(2)}, u32[]{:S(2)}) collective-permute-start(bf16[96,128]{1,0:T(8,128)(2,1)S(1)} %fusion.1.a_ref), channel_id=1, source_target_pairs={{0,1},{1,0},{2,3},{3,2},{4,5},{5,4},{6,7},{7,6},{8,9},{9,8},{10,11... | collective-permute-start | bytes 73736 | tf_op jit(solution)/shard_map/ppermute | solution.py:594
  125.4 11.8 %all-to-all-start.5 = ((bf16[16,96,128]{2,1,0:T(8,128)(2,1)}), bf16[16,96,128]{2,1,0:T(8,128)(2,1)S(1)}, u32[]{:S(2)}, u32[]{:S(2)}) async-start(bf16[16,96,128]{2,1,0:T(8,128)(2,1)} %spread_sum.1), calls=%async_computation.5 | async-start | bytes 786432 | tf_op jit(solution)/shard_map/all_to_all | solution.py:545
  129.0 13.1 %copy-start = (s32[9]{0:T(128)S(1)}, s32[9]{0:T(128)}, u32[]{:S(2)}) copy-start(s32[9]{0:T(128)} %stack.39.place_ref) | copy-start | bytes 112
  137.2 4.9 %collective-permute-start.12 = (bf16[16,96,128]{2,1,0:T(8,128)(2,1)S(1)}, bf16[16,96,128]{2,1,0:T(8,128)(2,1)S(1)}, u32[]{:S(2)}, u32[]{:S(2)}) collective-permute-start(bf16[16,96,128]{2,1,0:T(8,128)(2,1)S(1)} %all-to-all-done.5.mine_ref), channel_id=1, source_target_pairs={{0,8},{8,0},{16,24},{24,16},{32,40},{40,32},{48,56},{56,48},{64,72... | collective-permute-start | bytes 1179656 | tf_op jit(solution)/shard_map/ppermute | solution.py:516
  (3 other events, 7.4 us)

commit v6 on v4

--- a/solution.py
+++ b/solution.py
@@ -269,13 +269,13 @@
 
 def attention(place, x, own, other):
     r, s, n, _ = x.shape
-    half = pl.BlockSpec((8, 4, 64, 128), lambda g, p: (0, g, 0, 0))
+    half = pl.BlockSpec((8, 8, 64, 128), lambda g, p: (0, g, 0, 0))
     whole = pl.BlockSpec((r, s, n, 128), lambda g, p: (0, 0, 0, 0))
     return pl.pallas_call(
         attention_kernel,
         grid_spec=pltpu.PrefetchScalarGridSpec(
             num_scalar_prefetch=1,
-            grid=(2,),
+            grid=(1,),
             in_specs=[whole, half, half],
             out_specs=[whole, half, half],
             scratch_shapes=[
@@ -530,16 +530,14 @@
     part = jnp.sum(part.astype(F32), axis=0)
     part = jnp.concatenate([part, jnp.pad(extra, ((0, 8), (0, 0)))])
     low = part.astype(BF16)
-    for k in (1, 2, 3):
-        part = part + lax.ppermute(low, ALL, across(k)).astype(F32)
-    part = part.astype(BF16)
+    near, far, last = [lax.ppermute(low, ALL, across(k)).astype(F32) for k in (1, 2, 3)]
+    part = ((low.astype(F32) + near) + (far + last)).astype(BF16)
     return group_swap(jnp.broadcast_to(part[None], (16,) + part.shape), LAYERS)
 
 
 def unpack_kernel(place_ref, mine_ref, other_ref, dw_ref, dwo_ref, dwb_ref):
-    dwb_ref[...] = sum(
-        ref[i, 80:96].astype(F32) for ref in (mine_ref, other_ref) for i in range(16)
-    )[0:8]
+    column = lambda ref: sum(ref[i, 80:96].astype(F32) for i in range(16))
+    dwb_ref[...] = (column(mine_ref) + column(other_ref))[0:8]
 
     def write(low, high):
         get = lambda ref, b: jnp.concatenate(

time: 144 us -> 146 us (1.014)
  transfers between devices with their start and end apart: 19 -> 19, of which waited for: 14 -> 15; matrix products, arithmetic and copies ran while one was open for 1% -> 2% of each run, Pallas kernels for 14% -> 14%
where the time goes in v6:
time: 146 us; the launch traced here: 145 us
  starting transfers between devices  47.1 us (32%)
  waiting for transfers between devices  46.5 us (32%)
  Pallas kernels  44.9 us (31%)
  other arithmetic  2.99 us (2%)
  local copies, waits for them, and re-layouts  2.44 us (2%)
    ppermute x10, waiting for transfers between devices, send(): return lax.ppermute(x, 'seq', pairs)  28.4 us
    all_to_all x4, starting transfers between devices, group_swap(): lax.all_to_all(x, ALL, split_axis=0, concat_axis=0, tiled=True, axis_inde...  18.4 us
    pallas_call x1, Pallas kernels, attention(): pl.pallas_call(attention_kernel, grid_spec=pltpu.PrefetchScalarGridSpec(n...  18 us
    ppermute x10, starting transfers between devices, send(): return lax.ppermute(x, 'seq', pairs)  16.8 us
    all_to_all x4, waiting for transfers between devices, group_swap(): lax.all_to_all(x, ALL, split_axis=0, concat_axis=0, tiled=True, axis_inde...  13.6 us
    all_to_all x2, starting transfers between devices, swap(): return lax.all_to_all(x, axis, split_axis=0, concat_axis=0, tiled=True)  8.56 us
    pallas_call x2, Pallas kernels, pair_grad(): pl.pallas_call(body, grid=(half,), in_specs=[pl.BlockSpec((step, i, c), l...  8.24 us
    pallas_call x1, Pallas kernels, finish(): pl.pallas_call(finish_kernel, grid_spec=pltpu.PrefetchScalarGridSpec(num_...  5.98 us
  transfers between devices with their start and end apart: 19, of which 15 were waited for; matrix products, arithmetic and copies ran while one was open for 2% of the time, Pallas kernels for 14%

profile of v6, /device:TPU:1, one launch (start us, length us, event | category | flops | bytes accessed | tf_op | source)
XLA Modules:
  0.0 144.8 jit_solution(4027244970374884992)
XLA Ops:
  0.6 4.4 %pair_bias.1 = (bf16[2,8,64,128]{3,2,1,0:T(8,128)(2,1)}, bf16[64,128,128]{2,1,0:T(8,128)(2,1)}) custom-call(bf16[64,128,128]{2,1,0:T(8,128)(2,1)} %x.5, f32[1,128]{1,0:T(1,128)} %bitcast.33, bf16[8,128]{1,0:T(8,128)(2,1)} %bitcast.27), custom_call_target="tpu_custom_call" | custom-call | flops 4000000000 | bytes 12000000 | tf_op jit(solution)/shard_map/pair_bias/pallas_call | solution.py:121
  5.1 7.6 %all-to-all-start = ((bf16[16,64,128]{2,1,0:T(8,128)(2,1)}), bf16[16,64,128]{2,1,0:T(8,128)(2,1)S(1)}, u32[]{:S(2)}, u32[]{:S(2)}) async-start(bf16[16,64,128]{2,1,0:T(8,128)(2,1)} %bitcast.26), calls=%async_computation | async-start | bytes 524288 | tf_op jit(solution)/shard_map/all_to_all | solution.py:516
  12.6 3.9 %project.1 = (bf16[8,4,128,128]{3,2,1,0:T(8,128)(2,1)}, f32[4,128,256]{2,1,0:T(8,128)}, f32[4,128,256]{2,1,0:T(8,128)}) custom-call(bf16[4,128,256]{2,1,0:T(8,128)(2,1)} %x_ref.5, f32[1,256]{1,0:T(1,128)} %bitcast.31, bf16[256,1024]{1,0:T(8,128)(2,1)} %w_ref.3, f32[1,256]{1,0:T(1,128)} %bitcast.30, bf16[256,256]{1,0:T(8,128)(2,1)} %wo_ref.3, ...), custom_call_target="tpu_custom_call" | custom-call | flops 3000000000 | bytes 9000000 | tf_op jit(solution)/shard_map/project/pallas_call | solution.py:88
  16.6 3.5 %all-to-all-done = bf16[16,64,128]{2,1,0:T(8,128)(2,1)S(1)} async-done(((bf16[16,64,128]{2,1,0:T(8,128)(2,1)}), bf16[16,64,128]{2,1,0:T(8,128)(2,1)S(1)}, u32[]{:S(2)}, u32[]{:S(2)}) %all-to-all-start) | async-done | bytes 262176 | tf_op jit(solution)/shard_map/all_to_all | solution.py:516
  20.1 3.6 %all-to-all-start.1 = ((bf16[8,4,128,128]{3,2,1,0:T(8,128)(2,1)}), bf16[8,4,128,128]{3,2,1,0:T(8,128)(2,1)S(1)}, u32[]{:S(2)}, u32[]{:S(2)}) async-start(bf16[8,4,128,128]{3,2,1,0:T(8,128)(2,1)} %get-tuple-element.36), calls=%async_computation.1 | async-start | bytes 2097152 | tf_op jit(solution)/shard_map/all_to_all | solution.py:475
  23.6 3.8 %collective-permute-start.2 = (bf16[2,8,64,128]{3,2,1,0:T(8,128)(2,1)S(1)}, bf16[2,8,64,128]{3,2,1,0:T(8,128)(2,1)S(1)}, u32[]{:S(2)}, u32[]{:S(2)}) collective-permute-start(bf16[2,8,64,128]{3,2,1,0:T(8,128)(2,1)S(1)} %bitcast.19), channel_id=1, source_target_pairs={{0,48},{8,56},{16,0},{24,8},{32,16},{40,24},{48,32},{56,40},{64,11... | collective-permute-start | bytes 786440 | tf_op jit(solution)/shard_map/ppermute | solution.py:487
  28.2 9.2 %collective-permute-done.2 = bf16[2,8,64,128]{3,2,1,0:T(8,128)(2,1)S(1)} collective-permute-done((bf16[2,8,64,128]{3,2,1,0:T(8,128)(2,1)S(1)}, bf16[2,8,64,128]{3,2,1,0:T(8,128)(2,1)S(1)}, u32[]{:S(2)}, u32[]{:S(2)}) %collective-permute-start.2) | collective-permute-done | bytes 262176 | tf_op jit(solution)/shard_map/ppermute | solution.py:487
  37.3 4.8 %collective-permute-done = bf16[2,8,64,128]{3,2,1,0:T(8,128)(2,1)S(1)} collective-permute-done((bf16[2,8,64,128]{3,2,1,0:T(8,128)(2,1)S(1)}, bf16[2,8,64,128]{3,2,1,0:T(8,128)(2,1)S(1)}, u32[]{:S(2)}, u32[]{:S(2)}) %collective-permute-start) | collective-permute-done | bytes 262176 | tf_op jit(solution)/shard_map/ppermute | solution.py:487
  46.7 18.0 %attention.1 = (bf16[8,4,128,128]{3,2,1,0:T(8,128)(2,1)}, bf16[8,8,64,128]{3,2,1,0:T(8,128)(2,1)}, bf16[8,8,64,128]{3,2,1,0:T(8,128)(2,1)}) custom-call(s32[9]{0:T(128)} %stack.39.place_ref, bf16[8,4,128,128]{3,2,1,0:T(8,128)(2,1)} %copy-done.2, bf16[8,8,64,128]{3,2,1,0:T(8,128)(2,1)} %copy-done.3, bf16[8,8,64,128]{3,2,1,0:T(8,128)(2,1)} %copy-done.7), custom_call_target="tpu_custom_call" | custom-call | flops 17999998976 | bytes 54000000 | tf_op jit(solution)/shard_map/attention/pallas_call | solution.py:274
  65.0 5.0 %all-to-all-start.2 = ((bf16[8,4,128,128]{3,2,1,0:T(8,128)(2,1)}), bf16[8,4,128,128]{3,2,1,0:T(8,128)(2,1)S(1)}, u32[]{:S(2)}, u32[]{:S(2)}) async-start(bf16[8,4,128,128]{3,2,1,0:T(8,128)(2,1)} %get-tuple-element.39), calls=%async_computation.2 | async-start | bytes 2097152 | tf_op jit(solution)/shard_map/all_to_all | solution.py:475
  72.4 5.4 %collective-permute-done.5 = bf16[2,8,64,128]{3,2,1,0:T(8,128)(2,1)S(1)} collective-permute-done((bf16[2,8,64,128]{3,2,1,0:T(8,128)(2,1)S(1)}, bf16[2,8,64,128]{3,2,1,0:T(8,128)(2,1)S(1)}, u32[]{:S(2)}, u32[]{:S(2)}) %collective-permute-start.5) | collective-permute-done | bytes 262176 | tf_op jit(solution)/shard_map/ppermute | solution.py:487
  77.9 2.7 %collective-permute-done.7 = bf16[2,8,64,128]{3,2,1,0:T(8,128)(2,1)S(1)} collective-permute-done((bf16[2,8,64,128]{3,2,1,0:T(8,128)(2,1)S(1)}, bf16[2,8,64,128]{3,2,1,0:T(8,128)(2,1)S(1)}, u32[]{:S(2)}, u32[]{:S(2)}) %collective-permute-start.7) | collective-permute-done | bytes 262176 | tf_op jit(solution)/shard_map/ppermute | solution.py:487
  80.6 3.2 %collective-permute-done.6 = bf16[2,8,64,128]{3,2,1,0:T(8,128)(2,1)S(1)} collective-permute-done((bf16[2,8,64,128]{3,2,1,0:T(8,128)(2,1)S(1)}, bf16[2,8,64,128]{3,2,1,0:T(8,128)(2,1)S(1)}, u32[]{:S(2)}, u32[]{:S(2)}) %collective-permute-start.6) | collective-permute-done | bytes 262176 | tf_op jit(solution)/shard_map/ppermute | solution.py:487
  85.9 3.7 %all-to-all-start.3 = ((bf16[16,64,128]{2,1,0:T(8,128)(2,1)}), bf16[16,64,128]{2,1,0:T(8,128)(2,1)S(1)}, u32[]{:S(2)}, u32[]{:S(2)}) async-start(bf16[16,64,128]{2,1,0:T(8,128)(2,1)} %bitcast.15), calls=%async_computation.3 | async-start | bytes 524288 | tf_op jit(solution)/shard_map/all_to_all | solution.py:516
  89.7 6.0 %finish.1 = (bf16[4,128,256]{2,1,0:T(8,128)(2,1)}, bf16[4,128,256]{2,1,0:T(8,128)(2,1)}, bf16[5,256,128]{2,1,0:T(8,128)(2,1)}, bf16[5,256,128]{2,1,0:T(8,128)(2,1)}) custom-call(s32[9]{0:T(128)} %stack.39.place_ref, bf16[4,128,256]{2,1,0:T(8,128)(2,1)} %x_ref.5, f32[1,256]{1,0:T(1,128)} %bitcast.32, bf16[256,1024]{1,0:T(8,128)(2,1)} %w_ref.3, ...), custom_call_target="tpu_custom_call" | custom-call | flops 5000000000 | bytes 15000000 | tf_op jit(solution)/shard_map/finish/pallas_call | solution.py:354
  97.0 4.7 %collective-permute-start.8 = (bf16[5,256,128]{2,1,0:T(8,128)(2,1)}, bf16[5,256,128]{2,1,0:T(8,128)(2,1)S(1)}, u32[]{:S(2)}, u32[]{:S(2)}) collective-permute-start(bf16[5,256,128]{2,1,0:T(8,128)(2,1)} %get-tuple-element.46), channel_id=1, source_target_pairs={{0,8},{8,0},{16,24},{24,16},{32,40},{40,32},{48,56},{56,48},{64,72... | collective-permute-start | bytes 983048 | tf_op jit(solution)/shard_map/ppermute | solution.py:487
  101.7 2.7 %pair_weight.1 = f32[8,128]{1,0:T(8,128)} custom-call(bf16[64,128,128]{2,1,0:T(8,128)(2,1)} %get-tuple-element.49.n_ref, bf16[2,8,64,128]{3,2,1,0:T(8,128)(2,1)} %bitcast.23), custom_call_target="tpu_custom_call" | custom-call | flops 2000000000 | bytes 6000000 | tf_op jit(solution)/shard_map/pair_weight/pallas_call | solution.py:396
  105.9 3.5 %all-to-all-start.4 = ((bf16[16,80,128]{2,1,0:T(8,128)(2,1)}), bf16[16,80,128]{2,1,0:T(8,128)(2,1)S(1)}, u32[]{:S(2)}, u32[]{:S(2)}) async-start(bf16[16,80,128]{2,1,0:T(8,128)(2,1)} %bitcast.17), calls=%async_computation.4 | async-start | bytes 655360 | tf_op jit(solution)/shard_map/all_to_all | solution.py:516
  109.5 4.1 %pair_grad.2.rest_0_ = bf16[64,128,128]{2,1,0:T(8,128)(2,1)} custom-call(bf16[64,128,128]{2,1,0:T(8,128)(2,1)} %x.5, f32[1,128]{1,0:T(1,128)} %bitcast.34, bf16[8,128]{1,0:T(8,128)(2,1)} %bitcast.28, bf16[2,8,64,128]{3,2,1,0:T(8,128)(2,1)} %bitcast.24), custom_call_target="tpu_custom_call" | custom-call | flops 4000000000 | bytes 12000000 | tf_op jit(solution)/shard_map/pair_grad/pallas_call | solution.py:454
  113.6 4.6 %all-to-all-done.4 = bf16[16,80,128]{2,1,0:T(8,128)(2,1)S(1)} async-done(((bf16[16,80,128]{2,1,0:T(8,128)(2,1)}), bf16[16,80,128]{2,1,0:T(8,128)(2,1)S(1)}, u32[]{:S(2)}, u32[]{:S(2)}) %all-to-all-start.4) | async-done | bytes 327712 | tf_op jit(solution)/shard_map/all_to_all | solution.py:516
  125.7 3.6 %all-to-all-start.5 = ((bf16[16,96,128]{2,1,0:T(8,128)(2,1)}), bf16[16,96,128]{2,1,0:T(8,128)(2,1)S(1)}, u32[]{:S(2)}, u32[]{:S(2)}) async-start(bf16[16,96,128]{2,1,0:T(8,128)(2,1)} %broadcast_in_dim.2), calls=%async_computation.5 | async-start | bytes 786432 | tf_op jit(solution)/shard_map/all_to_all | solution.py:516
  129.2 4.1 %pair_grad.3 = bf16[64,128,128]{2,1,0:T(8,128)(2,1)} custom-call(bf16[64,128,128]{2,1,0:T(8,128)(2,1)} %x.5, f32[1,128]{1,0:T(1,128)} %bitcast.35, bf16[8,128]{1,0:T(8,128)(2,1)} %bitcast.29, bf16[2,8,64,128]{3,2,1,0:T(8,128)(2,1)} %bitcast.25, bf16[64,128,128]{2,1,0:T(8,128)(2,1)} %pair_grad.2.rest_0_), custom_call_target="tpu_custom_call", output_to_operand_aliasing={{}: (4, {})} | custom-call | flops 4000000000 | bytes 12000000 | tf_op jit(solution)/shard_map/pair_grad/pallas_call | solution.py:454
  133.3 4.1 %all-to-all-done.5.mine_ref = bf16[16,96,128]{2,1,0:T(8,128)(2,1)S(1)} async-done(((bf16[16,96,128]{2,1,0:T(8,128)(2,1)}), bf16[16,96,128]{2,1,0:T(8,128)(2,1)S(1)}, u32[]{:S(2)}, u32[]{:S(2)}) %all-to-all-start.5) | async-done | bytes 393248 | tf_op jit(solution)/shard_map/all_to_all | solution.py:516
  137.5 4.2 %collective-permute-start.12 = (bf16[16,96,128]{2,1,0:T(8,128)(2,1)S(1)}, bf16[16,96,128]{2,1,0:T(8,128)(2,1)S(1)}, u32[]{:S(2)}, u32[]{:S(2)}) collective-permute-start(bf16[16,96,128]{2,1,0:T(8,128)(2,1)S(1)} %all-to-all-done.5.mine_ref), channel_id=1, source_target_pairs={{0,8},{8,0},{16,24},{24,16},{32,40},{40,32},{48,56},{56,48},{64,72... | collective-permute-start | bytes 1179656 | tf_op jit(solution)/shard_map/ppermute | solution.py:487
  (49 shorter events, 23.6 us)
Async XLA Ops:
  5.1 15.0 %all-to-all-start = ((bf16[16,64,128]{2,1,0:T(8,128)(2,1)}), bf16[16,64,128]{2,1,0:T(8,128)(2,1)S(1)}, u32[]{:S(2)}, u32[]{:S(2)}) async-start(bf16[16,64,128]{2,1,0:T(8,128)(2,1)} %bitcast.26), calls=%async_computation | async-start | bytes 524288 | tf_op jit(solution)/shard_map/all_to_all | solution.py:516
  20.1 22.2 %all-to-all-start.1 = ((bf16[8,4,128,128]{3,2,1,0:T(8,128)(2,1)}), bf16[8,4,128,128]{3,2,1,0:T(8,128)(2,1)S(1)}, u32[]{:S(2)}, u32[]{:S(2)}) async-start(bf16[8,4,128,128]{3,2,1,0:T(8,128)(2,1)} %get-tuple-element.36), calls=%async_computation.1 | async-start | bytes 2097152 | tf_op jit(solution)/shard_map/all_to_all | solution.py:475
  23.6 13.7 %collective-permute-start.2 = (bf16[2,8,64,128]{3,2,1,0:T(8,128)(2,1)S(1)}, bf16[2,8,64,128]{3,2,1,0:T(8,128)(2,1)S(1)}, u32[]{:S(2)}, u32[]{:S(2)}) collective-permute-start(bf16[2,8,64,128]{3,2,1,0:T(8,128)(2,1)S(1)} %bitcast.19), channel_id=1, source_target_pairs={{0,48},{8,56},{16,0},{24,8},{32,16},{40,24},{48,32},{56,40},{64,11... | collective-permute-start | bytes 786440 | tf_op jit(solution)/shard_map/ppermute | solution.py:487
  27.5 9.9 %collective-permute-start.1 = (bf16[2,8,64,128]{3,2,1,0:T(8,128)(2,1)S(1)}, bf16[2,8,64,128]{3,2,1,0:T(8,128)(2,1)S(1)}, u32[]{:S(2)}, u32[]{:S(2)}) collective-permute-start(bf16[2,8,64,128]{3,2,1,0:T(8,128)(2,1)S(1)} %bitcast.20), channel_id=1, source_target_pairs={{0,32},{8,40},{16,48},{24,56},{32,0},{40,8},{48,16},{56,24},{64,96... | collective-permute-start | bytes 786440 | tf_op jit(solution)/shard_map/ppermute | solution.py:487
  27.5 14.7 %collective-permute-start = (bf16[2,8,64,128]{3,2,1,0:T(8,128)(2,1)S(1)}, bf16[2,8,64,128]{3,2,1,0:T(8,128)(2,1)S(1)}, u32[]{:S(2)}, u32[]{:S(2)}) collective-permute-start(bf16[2,8,64,128]{3,2,1,0:T(8,128)(2,1)S(1)} %bitcast.21), channel_id=1, source_target_pairs={{0,16},{8,24},{16,32},{24,40},{32,48},{40,56},{48,0},{56,8},{64,80... | collective-permute-start | bytes 786440 | tf_op jit(solution)/shard_map/ppermute | solution.py:487
  42.3 3.4 %copy-start.3 = (bf16[8,8,64,128]{3,2,1,0:T(8,128)(2,1)}, bf16[8,8,64,128]{3,2,1,0:T(8,128)(2,1)S(1)}, u32[]{:S(2)}) copy-start(bf16[8,8,64,128]{3,2,1,0:T(8,128)(2,1)S(1)} %pad_maximum_fusion.own_ref) | copy-start | bytes 3145732
  42.3 3.4 %collective-permute-start.3 = (bf16[8,8,64,128]{3,2,1,0:T(8,128)(2,1)S(1)}, bf16[8,8,64,128]{3,2,1,0:T(8,128)(2,1)S(1)}, u32[]{:S(2)}, u32[]{:S(2)}) collective-permute-start(bf16[8,8,64,128]{3,2,1,0:T(8,128)(2,1)S(1)} %pad_maximum_fusion.own_ref), channel_id=1, source_target_pairs={{0,8},{8,0},{16,24},{24,16},{32,40},{40,32},{48,56},{56,48},{64,72... | collective-permute-start | bytes 3145736 | tf_op jit(solution)/shard_map/ppermute | solution.py:487
  64.6 5.4 %copy-start.1 = (bf16[8,8,64,128]{3,2,1,0:T(8,128)(2,1)S(1)}, bf16[8,8,64,128]{3,2,1,0:T(8,128)(2,1)}, u32[]{:S(2)}) copy-start(bf16[8,8,64,128]{3,2,1,0:T(8,128)(2,1)} %get-tuple-element.43) | copy-start | bytes 3145732
  64.6 5.4 %collective-permute-start.4 = (bf16[8,8,64,128]{3,2,1,0:T(8,128)(2,1)}, bf16[8,8,64,128]{3,2,1,0:T(8,128)(2,1)S(1)}, u32[]{:S(2)}, u32[]{:S(2)}) collective-permute-start(bf16[8,8,64,128]{3,2,1,0:T(8,128)(2,1)} %get-tuple-element.44), channel_id=1, source_target_pairs={{0,8},{8,0},{16,24},{24,16},{32,40},{40,32},{48,56},{56,48},{64,72... | collective-permute-start | bytes 3145736 | tf_op jit(solution)/shard_map/ppermute | solution.py:487
  65.0 20.9 %all-to-all-start.2 = ((bf16[8,4,128,128]{3,2,1,0:T(8,128)(2,1)}), bf16[8,4,128,128]{3,2,1,0:T(8,128)(2,1)S(1)}, u32[]{:S(2)}, u32[]{:S(2)}) async-start(bf16[8,4,128,128]{3,2,1,0:T(8,128)(2,1)} %get-tuple-element.39), calls=%async_computation.2 | async-start | bytes 2097152 | tf_op jit(solution)/shard_map/all_to_all | solution.py:475
  70.5 7.4 %collective-permute-start.5 = (bf16[2,8,64,128]{3,2,1,0:T(8,128)(2,1)S(1)}, bf16[2,8,64,128]{3,2,1,0:T(8,128)(2,1)S(1)}, u32[]{:S(2)}, u32[]{:S(2)}) collective-permute-start(bf16[2,8,64,128]{3,2,1,0:T(8,128)(2,1)S(1)} %get-tuple-element.56), channel_id=1, source_target_pairs={{0,48},{8,56},{16,0},{24,8},{32,16},{40,24},{48,32},{56,40},{64,11... | collective-permute-start | bytes 786440 | tf_op jit(solution)/shard_map/ppermute | solution.py:487
  71.2 9.4 %collective-permute-start.7 = (bf16[2,8,64,128]{3,2,1,0:T(8,128)(2,1)S(1)}, bf16[2,8,64,128]{3,2,1,0:T(8,128)(2,1)S(1)}, u32[]{:S(2)}, u32[]{:S(2)}) collective-permute-start(bf16[2,8,64,128]{3,2,1,0:T(8,128)(2,1)S(1)} %get-tuple-element.57), channel_id=1, source_target_pairs={{0,16},{8,24},{16,32},{24,40},{32,48},{40,56},{48,0},{56,8},{64,80... | collective-permute-start | bytes 786440 | tf_op jit(solution)/shard_map/ppermute | solution.py:487
  72.0 11.7 %collective-permute-start.6 = (bf16[2,8,64,128]{3,2,1,0:T(8,128)(2,1)S(1)}, bf16[2,8,64,128]{3,2,1,0:T(8,128)(2,1)S(1)}, u32[]{:S(2)}, u32[]{:S(2)}) collective-permute-start(bf16[2,8,64,128]{3,2,1,0:T(8,128)(2,1)S(1)} %get-tuple-element.58), channel_id=1, source_target_pairs={{0,32},{8,40},{16,48},{24,56},{32,0},{40,8},{48,16},{56,24},{64,96... | collective-permute-start | bytes 786440 | tf_op jit(solution)/shard_map/ppermute | solution.py:487
  85.9 3.7 %copy-start.4 = (bf16[8,4,128,128]{3,2,1,0:T(8,128)(2,1)}, bf16[8,4,128,128]{3,2,1,0:T(8,128)(2,1)S(1)}, u32[]{:S(2)}) copy-start(bf16[8,4,128,128]{3,2,1,0:T(8,128)(2,1)S(1)} %all-to-all-done.2.back_ref) | copy-start | bytes 3145732
  85.9 11.1 %all-to-all-start.3 = ((bf16[16,64,128]{2,1,0:T(8,128)(2,1)}), bf16[16,64,128]{2,1,0:T(8,128)(2,1)S(1)}, u32[]{:S(2)}, u32[]{:S(2)}) async-start(bf16[16,64,128]{2,1,0:T(8,128)(2,1)} %bitcast.15), calls=%async_computation.3 | async-start | bytes 524288 | tf_op jit(solution)/shard_map/all_to_all | solution.py:516
  97.0 4.7 %copy-start.6 = (bf16[16,64,128]{2,1,0:T(8,128)(2,1)}, bf16[16,64,128]{2,1,0:T(8,128)(2,1)S(1)}, u32[]{:S(2)}) copy-start(bf16[16,64,128]{2,1,0:T(8,128)(2,1)S(1)} %all-to-all-done.3) | copy-start | bytes 786436
  97.0 8.1 %collective-permute-start.8 = (bf16[5,256,128]{2,1,0:T(8,128)(2,1)}, bf16[5,256,128]{2,1,0:T(8,128)(2,1)S(1)}, u32[]{:S(2)}, u32[]{:S(2)}) collective-permute-start(bf16[5,256,128]{2,1,0:T(8,128)(2,1)} %get-tuple-element.46), channel_id=1, source_target_pairs={{0,8},{8,0},{16,24},{24,16},{32,40},{40,32},{48,56},{56,48},{64,72... | collective-permute-start | bytes 983048 | tf_op jit(solution)/shard_map/ppermute | solution.py:487
  105.9 12.3 %all-to-all-start.4 = ((bf16[16,80,128]{2,1,0:T(8,128)(2,1)}), bf16[16,80,128]{2,1,0:T(8,128)(2,1)S(1)}, u32[]{:S(2)}, u32[]{:S(2)}) async-start(bf16[16,80,128]{2,1,0:T(8,128)(2,1)} %bitcast.17), calls=%async_computation.4 | async-start | bytes 655360 | tf_op jit(solution)/shard_map/all_to_all | solution.py:516
  118.2 4.3 %collective-permute-start.10 = (bf16[96,128]{1,0:T(8,128)(2,1)S(1)}, bf16[96,128]{1,0:T(8,128)(2,1)S(1)}, u32[]{:S(2)}, u32[]{:S(2)}) collective-permute-start(bf16[96,128]{1,0:T(8,128)(2,1)S(1)} %fusion.1), channel_id=1, source_target_pairs={{0,64},{1,65},{2,66},{3,67},{4,68},{5,69},{6,70},{7,71},{8,72},{9,... | collective-permute-start | bytes 73736 | tf_op jit(solution)/shard_map/ppermute | solution.py:533
  120.2 2.7 %collective-permute-start.9 = (bf16[96,128]{1,0:T(8,128)(2,1)S(1)}, bf16[96,128]{1,0:T(8,128)(2,1)S(1)}, u32[]{:S(2)}, u32[]{:S(2)}) collective-permute-start(bf16[96,128]{1,0:T(8,128)(2,1)S(1)} %fusion.1), channel_id=1, source_target_pairs={{0,1},{1,0},{2,3},{3,2},{4,5},{5,4},{6,7},{7,6},{8,9},{9,8},{10,11... | collective-permute-start | bytes 73736 | tf_op jit(solution)/shard_map/ppermute | solution.py:533
  120.5 4.3 %collective-permute-start.11 = (bf16[96,128]{1,0:T(8,128)(2,1)S(1)}, bf16[96,128]{1,0:T(8,128)(2,1)S(1)}, u32[]{:S(2)}, u32[]{:S(2)}) collective-permute-start(bf16[96,128]{1,0:T(8,128)(2,1)S(1)} %fusion.1), channel_id=1, source_target_pairs={{0,65},{1,64},{2,67},{3,66},{4,69},{5,68},{6,71},{7,70},{8,73},{9,... | collective-permute-start | bytes 73736 | tf_op jit(solution)/shard_map/ppermute | solution.py:533
  125.7 11.8 %all-to-all-start.5 = ((bf16[16,96,128]{2,1,0:T(8,128)(2,1)}), bf16[16,96,128]{2,1,0:T(8,128)(2,1)S(1)}, u32[]{:S(2)}, u32[]{:S(2)}) async-start(bf16[16,96,128]{2,1,0:T(8,128)(2,1)} %broadcast_in_dim.2), calls=%async_computation.5 | async-start | bytes 786432 | tf_op jit(solution)/shard_map/all_to_all | solution.py:516
  129.2 13.8 %copy-start = (s32[9]{0:T(128)S(1)}, s32[9]{0:T(128)}, u32[]{:S(2)}) copy-start(s32[9]{0:T(128)} %stack.39.place_ref) | copy-start | bytes 112
  137.5 5.5 %collective-permute-start.12 = (bf16[16,96,128]{2,1,0:T(8,128)(2,1)S(1)}, bf16[16,96,128]{2,1,0:T(8,128)(2,1)S(1)}, u32[]{:S(2)}, u32[]{:S(2)}) collective-permute-start(bf16[16,96,128]{2,1,0:T(8,128)(2,1)S(1)} %all-to-all-done.5.mine_ref), channel_id=1, source_target_pairs={{0,8},{8,0},{16,24},{24,16},{32,40},{40,32},{48,56},{56,48},{64,72... | collective-permute-start | bytes 1179656 | tf_op jit(solution)/shard_map/ppermute | solution.py:487
  (3 other events, 7.7 us)
